TPU v7x, 32 devices: a whole 2x2x4 slice. The times are simulated.
32 devices in a mesh: comp: 2 (over x), dom: 16 (over z, y, core).
Axes of the slice: x: 2, y: 2, z: 4, core: 2. Of those that a mesh axis runs over, the one named last changes fastest.
Arguments:
- state: float32 [2, 16, 262144], P('comp', None, 'dom'), may hold values from -6 to 6
- export_fields: float32 [2, 8, 262144], P('comp', None, 'dom'), may hold values from -6 to 6
- remap_weights: float32 [2, 2048, 128, 128], P('comp', 'dom'), may hold values from -0.5 to 0.5
- routes: int32 [2, 2048, 1], P('comp', 'dom'), may hold values from 0 to 15; in each aligned block of 128 rows (0 to 127, 128 to 255, ..., all dimensions but the last counted through in order) at most 16 rows name the same one
- target_block: int32 [2, 2048], P('comp', 'dom'), may hold values from 0 to 127
- source_block: int32 [2, 2048], P('comp', 'dom'), may hold values from 0 to 127
- wet_mask: int32 [2, 262144], P('comp', 'dom'), may hold values 0 or 1
- edge_coeff: float32 [2, 6, 262144], P('comp', None, 'dom'), may hold values from 0.02 to 0.15
- edge_offset: int32 [2, 6, 262144], P('comp', None, 'dom'), may hold values from -256 to 256
- vert_coeff: float32 [2, 15, 262144], P('comp', None, 'dom'), may hold values from 0.1 to 10
Outputs:
- new_state: float32 [2, 16, 262144], P('comp', None, 'dom')
- imported: float32 [2, 8, 262144], P('comp', None, 'dom')
Inputs may be any that keep to these rules, and one draw needn't show every extreme that they name: `routes`: in each device's 128 remap blocks no owner is named by more than 16 blocks, a bound that some block reaches.
All inputs are finite; a program needn't handle non-finite values. No bound on the sum of `wet_mask` on one device may be relied on, other than what follows from the above.
Results may differ from a plain program's by a relative error of at most 0.0001.
Values sent between devices are 32-bit elements; how exact they have to be, the bound alone decides.
No kernel may reach another device: no remote copies, remote signals or barrier semaphores. Data moves between devices by JAX's collectives and lax.ppermute only.
A program may use at most 192 MiB of HBM per device.

v0:
```python
import jax
import jax.numpy as jnp
from jax import lax
from jax.sharding import PartitionSpec as P

NB = 6
RIM = 256
STEPS = 4


force_scale = 0.5


def shifted(value, axis, steps):
    count = lax.axis_size(axis)
    pairs = [(source, (source + steps) % count) for source in range(count)]
    return lax.ppermute(value, axis, pairs)


def extended(block, sides, width):
    for axis, dim in sides:
        count = lax.axis_size(axis)
        forward = [(i, i + 1) for i in range(count - 1)]
        forward.append((count - 1, 0))
        backward = [(target, source) for source, target in forward]
        low = lax.ppermute(
            lax.slice_in_dim(block, block.shape[dim] - width, None, axis=dim), axis, forward
        )
        high = lax.ppermute(lax.slice_in_dim(block, 0, width, axis=dim), axis, backward)
        block = jnp.concatenate([low, block, high], axis=dim)
    return block


def factor_column(vert):
    level_count = vert.shape[0] + 1
    zero_row = jnp.zeros_like(vert[0])
    upper_rows = [zero_row] + [vert[index] for index in range(level_count - 1)]
    lower_rows = [vert[index] for index in range(level_count - 1)] + [zero_row]
    previous = zero_row
    ratios = []
    pivots = []
    for index in range(level_count):
        diag_row = 1.0 + upper_rows[index] + lower_rows[index]
        pivot_row = diag_row + upper_rows[index] * previous
        ratio_row = -lower_rows[index] / pivot_row
        ratios.append(ratio_row)
        pivots.append(pivot_row)
        previous = ratio_row
    return (upper_rows, ratios, pivots)


def solve_column(right_hand, forcing, factors):
    upper_rows, ratios, pivots = factors
    level_count = len(pivots)
    width = forcing.shape[0]
    previous = jnp.zeros_like(right_hand[0])
    partial_value = []
    for index in range(level_count):
        rhs_row = right_hand[index]
        if index < width:
            rhs_row = rhs_row + forcing[index]
        value = (rhs_row + upper_rows[index] * previous) / pivots[index]
        partial_value.append(value)
        previous = value
    following = jnp.zeros_like(right_hand[0])
    solved = [None] * level_count
    for index in range(level_count - 1, -1, -1):
        value = partial_value[index] - ratios[index] * following
        solved[index] = value
        following = value
    return jnp.stack(solved)


def local(
    state,
    export_fields,
    remap_weights,
    routes,
    target_block,
    source_block,
    wet_mask,
    edge_coeff,
    edge_offset,
    vert_coeff,
):
    highest = lax.Precision.HIGHEST
    owners = lax.axis_size("dom")
    cells = state.shape[2]
    block_cells = remap_weights.shape[2]
    block_count = remap_weights.shape[1]
    capacity = max(2, 2 * block_count // owners)
    exports = export_fields[0]
    width = exports.shape[0]
    blocks = exports.reshape(width, cells // block_cells, block_cells)
    source_hot = (
        source_block[0][:, None] == jnp.arange(cells // block_cells, dtype=jnp.int32)[None, :]
    ).astype(jnp.float32)
    picked = jnp.einsum("bn,fnt->bft", source_hot, blocks, precision=highest)
    mapped = jnp.einsum("bft,bts->bfs", picked, remap_weights[0], precision=highest)
    owner_list = routes[0, :, 0]
    positions = jnp.arange(block_count, dtype=jnp.int32)
    earlier = (owner_list[:, None] == owner_list[None, :]) & (
        positions[None, :] < positions[:, None]
    )
    ranks = jnp.sum(earlier.astype(jnp.int32), axis=1)
    slot_ids = owner_list * capacity + ranks
    slot_hot = (
        slot_ids[:, None] == jnp.arange(owners * capacity, dtype=jnp.int32)[None, :]
    ).astype(jnp.float32)
    send_values = jnp.einsum(
        "bk,bx->kx", slot_hot, mapped.reshape(block_count, width * block_cells), precision=highest
    )
    send_values = send_values.reshape(owners, capacity, width * block_cells)
    send_labels = jnp.einsum(
        "bk,b->k", slot_hot, (target_block[0] + 1).astype(jnp.float32), precision=highest
    )
    send_labels = send_labels.reshape(owners, capacity)
    grouped = (
        lax.all_to_all(send_values, "dom", split_axis=0, concat_axis=0, tiled=True),
        lax.all_to_all(send_labels, "dom", split_axis=0, concat_axis=0, tiled=True),
    )
    arrived = shifted((grouped[0], grouped[1]), "comp", 1)
    recv_values, recv_labels = arrived
    target_hot = (
        recv_labels.reshape(-1)[:, None] - 1.0
        == jnp.arange(cells // block_cells, dtype=jnp.float32)[None, :]
    ).astype(jnp.float32)
    assembled = jnp.einsum(
        "kn,kx->nx",
        target_hot,
        recv_values.reshape(owners * capacity, width * block_cells),
        precision=highest,
    )
    incoming = jnp.transpose(
        assembled.reshape(cells // block_cells, width, block_cells), (1, 0, 2)
    ).reshape(width, cells)
    forcing = incoming * wet_mask[0][None, :].astype(jnp.float32) * force_scale
    neighbours = jnp.arange(cells, dtype=jnp.int32)[None, :] + RIM + edge_offset[0]
    edge_row = edge_coeff[0]
    factors = factor_column(vert_coeff[0])
    column_state = state[0]
    for substep in range(STEPS):
        widened = extended(column_state, (("dom", 1),), RIM)
        spread = jnp.zeros_like(column_state)
        for which in range(NB):
            spread = spread + edge_row[which][None, :] * (
                widened[:, neighbours[which]] - column_state
            )
        right_hand = column_state + spread
        column_state = solve_column(right_hand, forcing, factors)
    return (column_state[None], incoming[None])


def solution(mesh):
    placed = (
        P("comp", None, "dom"),
        P("comp", None, "dom"),
        P("comp", "dom", None, None),
        P("comp", "dom", None),
        P("comp", "dom"),
        P("comp", "dom"),
        P("comp", "dom"),
        P("comp", None, "dom"),
        P("comp", None, "dom"),
        P("comp", None, "dom"),
    )
    return jax.shard_map(
        local,
        mesh=mesh,
        in_specs=placed,
        out_specs=(P("comp", None, "dom"), P("comp", None, "dom")),
        check_vma=False,
    )
```

profile of v0, /device:TPU:0, one launch (start us, length us, event | category | flops | bytes accessed | tf_op | source)
XLA Modules:
  0.0 1755.8 jit_solution(15982554337357326918)
XLA Ops:
  4.7 7.4 all-to-all-start
  21.9 9.5 fusion
  43.7 6.1 copy.694
  49.8 57.9 %gather_fusion.5 = f32[16384,16]{1,0:T(8,128)} fusion(f32[16,16896]{0,1:T(8,128)} %copy.694, s32[16384]{0:T(1024)S(1)} %broadcast_clamp_fusion), kind=kCustom, calls=%fused_computation.5 | custom fusion | bytes 2162688 | tf_op jit(solution)/shard_map/gather | solution.py:147
  107.7 6.0 copy.705
  113.7 57.9 %gather_fusion.4 = f32[16384,16]{1,0:T(8,128)} fusion(f32[16,16896]{0,1:T(8,128)} %copy.694, s32[16384]{0:T(1024)S(1)} %broadcast_clamp_fusion.1), kind=kCustom, calls=%fused_computation.4 | custom fusion | bytes 2162688 | tf_op jit(solution)/shard_map/gather | solution.py:147
  177.5 57.9 %gather_fusion.3 = f32[16384,16]{1,0:T(8,128)} fusion(f32[16,16896]{0,1:T(8,128)} %copy.694, s32[16384]{0:T(1024)S(1)} %broadcast_clamp_fusion.2), kind=kCustom, calls=%fused_computation.3 | custom fusion | bytes 2162688 | tf_op jit(solution)/shard_map/gather | solution.py:147
  235.4 6.0 copy.701
  241.4 57.9 %gather_fusion.2 = f32[16384,16]{1,0:T(8,128)} fusion(f32[16,16896]{0,1:T(8,128)} %copy.694, s32[16384]{0:T(1024)S(1)} %broadcast_clamp_fusion.3), kind=kCustom, calls=%fused_computation.2 | custom fusion | bytes 2162688 | tf_op jit(solution)/shard_map/gather | solution.py:147
  305.3 57.9 %gather_fusion.1 = f32[16384,16]{1,0:T(8,128)} fusion(f32[16,16896]{0,1:T(8,128)} %copy.694, s32[16384]{0:T(1024)S(1)} %broadcast_clamp_fusion.4), kind=kCustom, calls=%fused_computation.1 | custom fusion | bytes 2162688 | tf_op jit(solution)/shard_map/gather | solution.py:147
  363.2 6.0 copy.697
  369.2 57.9 %gather_fusion = f32[16384,16]{1,0:T(8,128)} fusion(f32[16,16896]{0,1:T(8,128)} %copy.694, s32[16384]{0:T(1024)S(1)} %broadcast_clamp_fusion.5), kind=kCustom, calls=%fused_computation | custom fusion | bytes 2162688 | tf_op jit(solution)/shard_map/gather | solution.py:147
  427.1 6.0 copy.695
  438.9 18.6 %collective-permute-done.3 = f32[16,16,1024]{2,1,0:T(8,128)S(1)} collective-permute-done((f32[16,16,1024]{2,1,0:T(8,128)}, f32[16,16,1024]{2,1,0:T(8,128)S(1)}, u32[]{:S(2)}, u32[]{:S(2)}) %collective-permute-start.3) | collective-permute-done | bytes 1048608 | tf_op jit(solution)/shard_map/ppermute | solution.py:17
  461.2 9.6 fusion.130
  484.9 6.1 copy.709
  491.0 63.1 %gather_fusion.11 = f32[16384,16]{1,0:T(8,128)} fusion(f32[16,16896]{0,1:T(8,128)} %copy.709, s32[16384]{0:T(1024)} %copy-done.4), kind=kCustom, calls=%fused_computation.11 | custom fusion | bytes 2162688 | tf_op jit(solution)/shard_map/gather | solution.py:147
  554.0 63.1 %gather_fusion.10 = f32[16384,16]{1,0:T(8,128)} fusion(f32[16,16896]{0,1:T(8,128)} %copy.709, s32[16384]{0:T(1024)} %copy-done.6), kind=kCustom, calls=%fused_computation.10 | custom fusion | bytes 2162688 | tf_op jit(solution)/shard_map/gather | solution.py:147
  617.2 63.1 %gather_fusion.9 = f32[16384,16]{1,0:T(8,128)} fusion(f32[16,16896]{0,1:T(8,128)} %copy.709, s32[16384]{0:T(1024)} %copy-done.8), kind=kCustom, calls=%fused_computation.9 | custom fusion | bytes 2162688 | tf_op jit(solution)/shard_map/gather | solution.py:147
  680.2 63.1 %gather_fusion.8 = f32[16384,16]{1,0:T(8,128)} fusion(f32[16,16896]{0,1:T(8,128)} %copy.709, s32[16384]{0:T(1024)} %copy-done.10), kind=kCustom, calls=%fused_computation.8 | custom fusion | bytes 2162688 | tf_op jit(solution)/shard_map/gather | solution.py:147
  743.4 63.1 %gather_fusion.7 = f32[16384,16]{1,0:T(8,128)} fusion(f32[16,16896]{0,1:T(8,128)} %copy.709, s32[16384]{0:T(1024)} %copy-done.12), kind=kCustom, calls=%fused_computation.7 | custom fusion | bytes 2162688 | tf_op jit(solution)/shard_map/gather | solution.py:147
  806.5 57.9 %gather_fusion.6 = f32[16384,16]{1,0:T(8,128)} fusion(f32[16,16896]{0,1:T(8,128)} %copy.709, s32[16384]{0:T(1024)S(1)} %broadcast_clamp_fusion.5), kind=kCustom, calls=%fused_computation.6 | custom fusion | bytes 2162688 | tf_op jit(solution)/shard_map/gather | solution.py:147
  864.4 6.0 copy.720
  870.3 6.0 copy.718
  882.3 6.0 copy.714
  894.3 6.0 copy.710
  919.4 6.1 copy.721
  925.5 63.1 %gather_fusion.17 = f32[16384,16]{1,0:T(8,128)} fusion(f32[16,16896]{0,1:T(8,128)} %copy.721, s32[16384]{0:T(1024)} %copy-done.4), kind=kCustom, calls=%fused_computation.17 | custom fusion | bytes 2162688 | tf_op jit(solution)/shard_map/gather | solution.py:147
  988.6 63.1 %gather_fusion.16 = f32[16384,16]{1,0:T(8,128)} fusion(f32[16,16896]{0,1:T(8,128)} %copy.721, s32[16384]{0:T(1024)} %copy-done.6), kind=kCustom, calls=%fused_computation.16 | custom fusion | bytes 2162688 | tf_op jit(solution)/shard_map/gather | solution.py:147
  1051.7 63.1 %gather_fusion.15 = f32[16384,16]{1,0:T(8,128)} fusion(f32[16,16896]{0,1:T(8,128)} %copy.721, s32[16384]{0:T(1024)} %copy-done.8), kind=kCustom, calls=%fused_computation.15 | custom fusion | bytes 2162688 | tf_op jit(solution)/shard_map/gather | solution.py:147
  1114.8 63.1 %gather_fusion.14 = f32[16384,16]{1,0:T(8,128)} fusion(f32[16,16896]{0,1:T(8,128)} %copy.721, s32[16384]{0:T(1024)} %copy-done.10), kind=kCustom, calls=%fused_computation.14 | custom fusion | bytes 2162688 | tf_op jit(solution)/shard_map/gather | solution.py:147
  1177.9 63.1 %gather_fusion.13 = f32[16384,16]{1,0:T(8,128)} fusion(f32[16,16896]{0,1:T(8,128)} %copy.721, s32[16384]{0:T(1024)} %copy-done.12), kind=kCustom, calls=%fused_computation.13 | custom fusion | bytes 2162688 | tf_op jit(solution)/shard_map/gather | solution.py:147
  1241.0 57.9 %gather_fusion.12 = f32[16384,16]{1,0:T(8,128)} fusion(f32[16,16896]{0,1:T(8,128)} %copy.721, s32[16384]{0:T(1024)S(1)} %broadcast_clamp_fusion.5), kind=kCustom, calls=%fused_computation.12 | custom fusion | bytes 2162688 | tf_op jit(solution)/shard_map/gather | solution.py:147
  1298.9 6.0 copy.732
  1304.9 6.0 copy.730
  1316.8 6.0 copy.726
  1328.8 6.0 copy.722
  1355.4 6.1 copy.733
  1361.5 57.9 %gather_fusion.23 = f32[16384,16]{1,0:T(8,128)} fusion(f32[16,16896]{0,1:T(8,128)} %copy.733, s32[16384]{0:T(1024)S(1)} %copy-done.5), kind=kCustom, calls=%fused_computation.23 | custom fusion | bytes 2162688 | tf_op jit(solution)/shard_map/gather | solution.py:147
  1419.4 57.9 %gather_fusion.22 = f32[16384,16]{1,0:T(8,128)} fusion(f32[16,16896]{0,1:T(8,128)} %copy.733, s32[16384]{0:T(1024)S(1)} %copy-done.7), kind=kCustom, calls=%fused_computation.22 | custom fusion | bytes 2162688 | tf_op jit(solution)/shard_map/gather | solution.py:147
  1477.3 57.8 %gather_fusion.21 = f32[16384,16]{1,0:T(8,128)} fusion(f32[16,16896]{0,1:T(8,128)} %copy.733, s32[16384]{0:T(1024)S(1)} %copy-done.9), kind=kCustom, calls=%fused_computation.21 | custom fusion | bytes 2162688 | tf_op jit(solution)/shard_map/gather | solution.py:147
  1535.2 57.9 %gather_fusion.20 = f32[16384,16]{1,0:T(8,128)} fusion(f32[16,16896]{0,1:T(8,128)} %copy.733, s32[16384]{0:T(1024)S(1)} %copy-done.11), kind=kCustom, calls=%fused_computation.20 | custom fusion | bytes 2162688 | tf_op jit(solution)/shard_map/gather | solution.py:147
  1593.1 57.8 %gather_fusion.19 = f32[16384,16]{1,0:T(8,128)} fusion(f32[16,16896]{0,1:T(8,128)} %copy.733, s32[16384]{0:T(1024)S(1)} %copy-done.13), kind=kCustom, calls=%fused_computation.19 | custom fusion | bytes 2162688 | tf_op jit(solution)/shard_map/gather | solution.py:147
  1650.9 57.9 %gather_fusion.18 = f32[16384,16]{1,0:T(8,128)} fusion(f32[16,16896]{0,1:T(8,128)} %copy.733, s32[16384]{0:T(1024)S(1)} %broadcast_clamp_fusion.5), kind=kCustom, calls=%fused_computation.18 | custom fusion | bytes 2162688 | tf_op jit(solution)/shard_map/gather | solution.py:147
  1708.8 6.0 copy.744
  1714.8 6.0 copy.742
  1732.7 6.0 copy.736
  1738.7 6.0 copy.734
  (329 shorter events, 146.3 us)
Async XLA Ops:
  0.6 20.2 %copy-start = (f32[1,8,16384]{2,1,0:T(8,128)S(1)}, f32[1,8,16384]{2,1,0:T(8,128)}, u32[]{:S(2)}) copy-start(f32[1,8,16384]{2,1,0:T(8,128)} %param.11) | copy-start | bytes 1572868
  4.7 28.5 %all-to-all-start = ((f32[16,1,16]{2,1,0:T(1,128)}), f32[16,1,16]{2,1,0:T(1,128)S(1)}, u32[]{:S(2)}, u32[]{:S(2)}) async-start(f32[16,1,16]{2,1,0:T(1,128)} %convolution_bitcast_fusion), calls=%async_computation | async-start | bytes 16384 | tf_op jit(solution)/shard_map/all_to_all | solution.py:120
  13.4 28.4 %collective-permute-start = (f32[16,256]{1,0:T(8,128)}, f32[16,256]{1,0:T(8,128)}, u32[]{:S(2)}, u32[]{:S(2)}) collective-permute-start(f32[16,256]{1,0:T(8,128)} %get-tuple-element.167), channel_id=1, source_target_pairs={{0,1},{1,2},{2,3},{3,4},{4,5},{5,6},{6,7},{7,8},{8,9},{9,10},{10,1... | collective-permute-start | bytes 49160 | tf_op jit(solution)/shard_map/ppermute | solution.py:26
  13.8 28.0 %collective-permute-start.1 = (f32[16,256]{1,0:T(8,128)}, f32[16,256]{1,0:T(8,128)}, u32[]{:S(2)}, u32[]{:S(2)}) collective-permute-start(f32[16,256]{1,0:T(8,128)} %get-tuple-element.168), channel_id=1, source_target_pairs={{1,0},{2,1},{3,2},{4,3},{5,4},{6,5},{7,6},{8,7},{9,8},{10,9},{11,1... | collective-permute-start | bytes 49160 | tf_op jit(solution)/shard_map/ppermute | solution.py:29
  20.2 21.7 %copy-start.3 = (f32[1,16,16384]{2,1,0:T(8,128)S(1)}, f32[1,16,16384]{2,1,0:T(8,128)}, u32[]{:S(2)}) copy-start(f32[1,16,16384]{2,1,0:T(8,128)} %param.10) | copy-start | bytes 3145732
  20.6 10.9 copy-start.125
  20.7 19.0 %copy-start.123 = (s32[1,16384]{1,0:T(1,128)S(1)}, s32[1,16384]{1,0:T(1,128)}, u32[]{:S(2)}) copy-start(s32[1,16384]{1,0:T(1,128)} %param.16) | copy-start | bytes 196612
  20.7 29.1 %copy-start.4 = (s32[16384]{0:T(1024)}, s32[16384]{0:T(1024)S(1)}, u32[]{:S(2)}) copy-start(s32[16384]{0:T(1024)S(1)} %broadcast_clamp_fusion) | copy-start | bytes 196612
  20.7 92.9 %copy-start.6 = (s32[16384]{0:T(1024)}, s32[16384]{0:T(1024)S(1)}, u32[]{:S(2)}) copy-start(s32[16384]{0:T(1024)S(1)} %broadcast_clamp_fusion.1) | copy-start | bytes 196612
  20.8 156.8 %copy-start.8 = (s32[16384]{0:T(1024)}, s32[16384]{0:T(1024)S(1)}, u32[]{:S(2)}) copy-start(s32[16384]{0:T(1024)S(1)} %broadcast_clamp_fusion.2) | copy-start | bytes 196612
  20.8 220.6 %copy-start.10 = (s32[16384]{0:T(1024)}, s32[16384]{0:T(1024)S(1)}, u32[]{:S(2)}) copy-start(s32[16384]{0:T(1024)S(1)} %broadcast_clamp_fusion.3) | copy-start | bytes 196612
  33.2 399.9 %all-to-all-start.1 = ((f32[16,16,1024]{2,1,0:T(8,128)}), f32[16,16,1024]{2,1,0:T(8,128)}, u32[]{:S(2)}, u32[]{:S(2)}) async-start(f32[16,16,1024]{2,1,0:T(8,128)} %fusion.54), calls=%async_computation.1 | async-start | bytes 2097152 | tf_op jit(solution)/shard_map/all_to_all | solution.py:119
  38.0 3.7 collective-permute-start.2
  39.7 265.6 %copy-start.12 = (s32[16384]{0:T(1024)}, s32[16384]{0:T(1024)S(1)}, u32[]{:S(2)}) copy-start(s32[16384]{0:T(1024)S(1)} %broadcast_clamp_fusion.4) | copy-start | bytes 196612
  433.0 28.1 %copy-start.2 = (f32[1,15,16384]{2,0,1:T(1,128)S(1)}, f32[1,15,16384]{2,0,1:T(1,128)}, u32[]{:S(2)}) copy-start(f32[1,15,16384]{2,0,1:T(1,128)} %param.19) | copy-start | bytes 2949124
  433.0 24.5 %collective-permute-start.3 = (f32[16,16,1024]{2,1,0:T(8,128)}, f32[16,16,1024]{2,1,0:T(8,128)S(1)}, u32[]{:S(2)}, u32[]{:S(2)}) collective-permute-start(f32[16,16,1024]{2,1,0:T(8,128)} %all-to-all-done.1), channel_id=1, source_target_pairs={{0,16},{16,0},{1,17},{17,1},{2,18},{18,2},{3,19},{19,3},{4,20},{20... | collective-permute-start | bytes 3145736 | tf_op jit(solution)/shard_map/ppermute | solution.py:17
  477.7 5.9 collective-permute-start.4
  477.8 6.0 collective-permute-start.5
  900.3 6.1 copy-start.19
  900.4 6.1 copy-start.23
  900.4 6.1 copy-start.27
  900.4 6.1 copy-start.31
  900.4 6.1 copy-start.35
  900.4 6.1 copy-start.39
  900.4 6.1 copy-start.43
  900.4 6.1 copy-start.47
  900.4 6.1 copy-start.51
  900.4 6.1 copy-start.55
  900.4 6.1 copy-start.59
  900.5 6.1 copy-start.63
  900.5 6.1 copy-start.67
  900.5 6.1 copy-start.71
  900.5 6.1 copy-start.113
  900.5 6.1 copy-start.116
  900.5 6.1 copy-start.119
  912.2 5.9 collective-permute-start.6
  912.2 6.1 collective-permute-start.7
  1334.9 6.1 copy-start.20
  1334.9 6.1 copy-start.24
  1347.3 6.1 collective-permute-start.8
  1347.3 6.3 collective-permute-start.9
  1352.9 8.7 copy-start.5
  1355.4 64.0 %copy-start.7 = (s32[16384]{0:T(1024)S(1)}, s32[16384]{0:T(1024)}, u32[]{:S(2)}) copy-start(s32[16384]{0:T(1024)} %copy-done.6) | copy-start | bytes 196612
  1361.5 115.8 %copy-start.9 = (s32[16384]{0:T(1024)S(1)}, s32[16384]{0:T(1024)}, u32[]{:S(2)}) copy-start(s32[16384]{0:T(1024)} %copy-done.8) | copy-start | bytes 196612
  1419.4 115.7 %copy-start.11 = (s32[16384]{0:T(1024)S(1)}, s32[16384]{0:T(1024)}, u32[]{:S(2)}) copy-start(s32[16384]{0:T(1024)} %copy-done.10) | copy-start | bytes 196612
  1477.3 115.7 %copy-start.13 = (s32[16384]{0:T(1024)S(1)}, s32[16384]{0:T(1024)}, u32[]{:S(2)}) copy-start(s32[16384]{0:T(1024)} %copy-done.12) | copy-start | bytes 196612
  1738.7 10.0 copy-start.17
  1738.7 16.8 copy-start.1
  (90 other events, 411.5 us)
where the time goes:
time: 1780 us; the launch traced here: 1760 us
  local copies, waits for them, and re-layouts  1630 us (92%)
  other arithmetic  49.9 us (3%)
  starting transfers between devices  33.8 us (2%)
  waiting for transfers between devices  24.3 us (1%)
    gather x48, local copies, waits for them, and re-layouts, local(): widened[:, neighbours[which]] - column_state  1580 us
  transfers between devices with their start and end apart: 12, of which 8 were waited for; matrix products, arithmetic and copies ran while one was open for 24% of the time, Pallas kernels for 0%

commit v1 on v0

v1 whole, which is shorter than its diff:
```python
import functools

import jax
import jax.numpy as jnp
from jax import lax
from jax.experimental import pallas as pl
from jax.experimental.pallas import tpu as pltpu
from jax.sharding import PartitionSpec as P

NB = 6
RIM = 256
STEPS = 4
LANES = 128
REACH = RIM // LANES
HALO = STEPS * REACH
PAD = 8
MIB = 2**20
CHUNK = 3 * 8

force_scale = 0.5

F32 = jnp.float32
BF16 = jnp.bfloat16


def split(value):
    high = value.astype(BF16)
    return high, (value - high.astype(F32)).astype(BF16)


def remap_kernel(
    owners, capacity, routes, target, source, me, fields, weights, *refs
):
    edges, (out, low, high, counts) = refs[:10], refs[10:]
    step = pl.program_id(0)
    per_step = weights.shape[0]
    width = fields.shape[0]
    lane = lax.broadcasted_iota(jnp.int32, (1, LANES), 1)
    label_row = capacity * width

    @pl.when(step == 0)
    def _():
        out[...] = jnp.zeros_like(out)
        for owner in range(owners):
            counts[owner] = 0
        for side, pack in ((0, low), (1, high)):
            state, coef, offset, vert, wet = edges[side::2]
            levels = state.shape[0]
            for row in range(HALO):
                for level in range(0, levels, 8):
                    tile = state[level : level + 8, row * LANES : (row + 1) * LANES]
                    pack[pl.ds(level * HALO + row, 8, stride=HALO), :] = tile
            at = levels * HALO
            for part in (coef, offset, vert):
                for index in range(part.shape[0]):
                    pack[at : at + HALO, :] = part[index].astype(F32)
                    at += HALO
            pack[at : at + HALO, :] = wet[...].astype(F32)

    for local_block in range(per_step):
        block = step * per_step + local_block
        owner = routes[block]
        rank = counts[owner]
        counts[owner] = rank + 1
        start = pl.multiple_of(source[block] * LANES, LANES)
        picked_high, picked_low = split(fields[:, pl.ds(start, LANES)])
        picked = jnp.concatenate([picked_high, picked_low], axis=0)
        high_part, low_part = split(weights[local_block])
        by_high = jnp.dot(picked, high_part, preferred_element_type=F32)
        by_low = jnp.dot(picked, low_part, preferred_element_type=F32)
        value = (by_low[:width] + by_low[width:] + by_high[width:]) + by_high[:width]
        row = pl.multiple_of(rank * width, width)
        out[owner, pl.ds(row, width), :] = value
        slot = lax.rem(me[0] * capacity + rank, LANES)
        old = out[owner, label_row : label_row + 1, :]
        out[owner, label_row : label_row + 1, :] = jnp.where(
            lane == slot, (target[block] + 1).astype(F32), old
        )


def remap(routes, target, source, me, fields, weights, state, parts, owners, capacity):
    block_count = weights.shape[0]
    width, cells = fields.shape
    levels = state.shape[0]
    rows = cells // LANES
    per_step = 16
    edge = HALO * LANES
    ends = (rows // HALO - 1, 0)
    specs = [pl.BlockSpec((levels, edge), lambda i, *_, e=e: (0, e)) for e in ends]
    edges = [state, state]
    pack_rows = levels * HALO
    for part in parts:
        if part.ndim == 3:
            count = part.shape[0]
            specs += [
                pl.BlockSpec((count, HALO, LANES), lambda i, *_, e=e: (0, e, 0)) for e in ends
            ]
        else:
            count = 1
            specs += [pl.BlockSpec((HALO, LANES), lambda i, *_, e=e: (e, 0)) for e in ends]
        pack_rows += count * HALO
        edges += [part, part]
    slots = (owners, capacity * width + 8, LANES)
    return pl.pallas_call(
        functools.partial(remap_kernel, owners, capacity),
        grid_spec=pltpu.PrefetchScalarGridSpec(
            num_scalar_prefetch=4,
            grid=(block_count // per_step,),
            in_specs=[
                pl.BlockSpec((width, cells), lambda i, *_: (0, 0)),
                pl.BlockSpec((per_step, LANES, LANES), lambda i, *_: (i, 0, 0)),
                *specs,
            ],
            out_specs=[
                pl.BlockSpec(slots, lambda i, *_: (0, 0, 0)),
                pl.BlockSpec((pack_rows, LANES), lambda i, *_: (0, 0)),
                pl.BlockSpec((pack_rows, LANES), lambda i, *_: (0, 0)),
            ],
            scratch_shapes=[pltpu.SMEM((owners,), jnp.int32)],
        ),
        out_shape=[
            jax.ShapeDtypeStruct(slots, F32),
            jax.ShapeDtypeStruct((pack_rows, LANES), F32),
            jax.ShapeDtypeStruct((pack_rows, LANES), F32),
        ],
        compiler_params=pltpu.CompilerParams(vmem_limit_bytes=60 * MIB),
        name="remap",
    )(routes, target, source, me, fields, weights, *edges)


def assemble_kernel(owners, capacity, width, slots, out, low, high, hot, values):
    rows = out.shape[1]
    count = owners * capacity
    per_row = LANES // capacity
    size = capacity * width
    pitch = size + 8
    block = lax.broadcasted_iota(jnp.int32, (rows, LANES), 0) + 1
    for sender in range(owners):
        values[sender * size : (sender + 1) * size, :] = slots[
            sender * pitch : sender * pitch + size, :
        ]
    for half in range(count // LANES):
        label = None
        for sender in range(half * per_row, (half + 1) * per_row):
            row = slots[sender * pitch + size : sender * pitch + size + 1, :]
            label = row if label is None else label + row
        label = jnp.broadcast_to(label.astype(jnp.int32), (rows, LANES))
        hot[:, half * LANES : (half + 1) * LANES] = (label == block).astype(F32).astype(BF16)
    picks = hot[...]
    for field in range(width):
        value_high, value_low = split(values[pl.ds(field, count, stride=width), :])
        both = jnp.concatenate([value_high, value_low], axis=1)
        total = jnp.dot(picks, both, preferred_element_type=F32)
        total = total[:, :LANES] + total[:, LANES:]
        out[field] = total
        low[field] = total[:HALO]
        high[field] = total[rows - HALO :]


def assemble(slots, owners, capacity, width, rows):
    return pl.pallas_call(
        functools.partial(assemble_kernel, owners, capacity, width),
        out_shape=[
            jax.ShapeDtypeStruct((width, rows, LANES), F32),
            jax.ShapeDtypeStruct((width, HALO, LANES), F32),
            jax.ShapeDtypeStruct((width, HALO, LANES), F32),
        ],
        scratch_shapes=[
            pltpu.VMEM((rows, owners * capacity), BF16),
            pltpu.VMEM((owners * capacity * width, LANES), F32),
        ],
        compiler_params=pltpu.CompilerParams(vmem_limit_bytes=12 * MIB),
        name="assemble",
    )(slots)


def lane_pick(value, index):
    return jnp.take_along_axis(value, index, axis=1, mode="promise_in_bounds")


def to_lanes(levels, total, column, wide):
    pitch = column.shape[0] // levels

    @pl.loop(0, total, unroll=8)
    def _(row):
        here = pl.ds(pl.multiple_of((row + PAD) * LANES, LANES), LANES)
        tiles = [
            column[pl.ds(level * pitch + PAD + row, 8, stride=pitch), :]
            for level in range(0, levels, 8)
        ]
        high, low = split(jnp.concatenate(tiles, axis=0))
        wide[0:levels, here] = high
        wide[levels : 2 * levels, here] = low


def spread(levels, total, column, wide, matrix, lanes, codes, coefs, mix):
    pitch = column.shape[0] // levels
    span = (2 * REACH + 1) * LANES

    @pl.loop(0, total // CHUNK)
    def _(chunk):
        base = pl.multiple_of(chunk * CHUNK, 8)
        for tile in range(CHUNK - 8):
            row = base + tile
            at = pl.multiple_of((row + PAD - REACH) * LANES, LANES)
            got = jnp.dot(
                wide[:, pl.ds(at, span)],
                matrix[chunk * (CHUNK - 8) + tile],
                preferred_element_type=F32,
            )
            got = got[:, :LANES] + got[:, LANES:]
            got = got[:levels] + got[levels:]
            for level in range(0, levels, 8):
                mix[pl.ds(level * total + row, 8, stride=total), :] = got[level : level + 8]
        row = base + CHUNK - 8
        here = pl.ds(row, 8)
        right = [None] * levels
        for which in range(NB):
            index = lanes[which, here, :]
            code = codes[which, here, :]
            factor = coefs[which, here, :]
            for level in range(levels):
                found = None
                for reach in range(2 * REACH + 1):
                    at = level * pitch + PAD - REACH + reach + row
                    picked = lane_pick(column[pl.ds(at, 8), :], index)
                    found = picked if found is None else jnp.where(code == reach, picked, found)
                found = factor * found
                right[level] = found if which == 0 else right[level] + found
        for level in range(levels):
            mix[pl.ds(level * total + row, 8), :] = right[level]


def prepare_kernel(
    state, coef, offset, vert, wet, low, high,
    column, mix, matrix, inv, from_up, from_down, lanes, codes, coefs, keep, wets,
    wide, places, merged, verts,
):
    levels = state.shape[0]
    rows = state.shape[1] // LANES
    total = rows + 2 * HALO
    pitch = column.shape[0] // levels
    inner = levels - 1

    for pack, first in ((low, 0), (high, total - HALO)):
        for level in range(levels):
            at = level * pitch + PAD + first
            column[at : at + HALO, :] = pack[level * HALO : (level + 1) * HALO, :]
        here = slice(first, first + HALO)
        at = levels * HALO
        for out, count in ((coefs, NB), (places, NB), (verts, inner)):
            for index in range(count):
                out[index, here, :] = pack[at : at + HALO, :].astype(out.dtype)
                at += HALO
        wets[here, :] = pack[at : at + HALO, :] * force_scale
    main = slice(HALO, HALO + rows)
    coefs[:, main, :] = coef[...]
    places[:, main, :] = offset[...]
    verts[:, main, :] = vert[...]
    wets[main, :] = wet[...].astype(F32) * force_scale

    @pl.loop(0, rows, unroll=8)
    def _(row):
        here = pl.ds(pl.multiple_of(row * LANES, LANES), LANES)
        for level in range(0, levels, 8):
            at = level * pitch + PAD + HALO + row
            column[pl.ds(at, 8, stride=pitch), :] = state[level : level + 8, here]

    to_lanes(levels, total, column, wide)
    lane = lax.broadcasted_iota(jnp.int32, (8, LANES), 1)

    @pl.loop(0, total // 8)
    def _(group):
        here = pl.ds(pl.multiple_of(group * 8, 8), 8)
        spots = [places[which, here, :] + lane + RIM for which in range(NB)]
        factors = [coefs[which, here, :] for which in range(NB)]
        left = 1.0
        for which in range(NB):
            places[which, here, :] = spots[which]
            lanes[which, here, :] = jnp.bitwise_and(spots[which], LANES - 1)
            codes[which, here, :] = lax.shift_right_logical(spots[which], 7)
            left = left - factors[which]
            joint = factors[which]
            for other in range(NB):
                if other != which:
                    joint = joint + jnp.where(spots[other] == spots[which], factors[other], 0.0)
            merged[which, here, :] = joint
        keep[here, :] = left
        upper = jnp.zeros((8, LANES), F32)
        carried = jnp.zeros((8, LANES), F32)
        for level in range(levels):
            lower = verts[level, here, :] if level < inner else jnp.zeros((8, LANES), F32)
            pivot = (1.0 + upper + lower) - upper * carried
            inverse = 1.0 / pivot
            carried = lower * inverse
            inv[level, here, :] = inverse
            from_up[level, here, :] = upper * inverse
            from_down[level, here, :] = carried
            upper = lower

    span = (2 * REACH + 1) * LANES
    small = jnp.int16

    @pl.loop(0, total // CHUNK)
    def _(chunk):
        @pl.loop(0, CHUNK - 8)
        def _(tile):
            row = chunk * CHUNK + tile
            at = chunk * (CHUNK - 8) + tile
            spots, highs, lows = [], [], []
            for which in range(NB):
                spot = places[which, pl.ds(row, 1), :]
                spots.append(jnp.broadcast_to(spot, (16, LANES)).astype(small))
                joint_high, joint_low = split(
                    jnp.broadcast_to(merged[which, pl.ds(row, 1), :], (16, LANES))
                )
                highs.append(joint_high)
                lows.append(joint_low)
            count = lax.broadcasted_iota(jnp.int32, (16, LANES), 0)
            for first in range(0, span, 16):
                key = (count + first).astype(small)
                by_high = jnp.zeros((16, LANES), BF16)
                by_low = jnp.zeros((16, LANES), BF16)
                for which in range(NB):
                    hit = spots[which] == key
                    by_high = jnp.where(hit, highs[which], by_high)
                    by_low = jnp.where(hit, lows[which], by_low)
                matrix[at, first : first + 16, 0:LANES] = by_high
                matrix[at, first : first + 16, LANES : 2 * LANES] = by_low

    spread(levels, total, column, wide, matrix, lanes, codes, coefs, mix)


def prepare(state, coef, offset, vert, wet, low, high):
    levels, cells = state.shape
    rows = cells // LANES
    total = rows + 2 * HALO
    pitch = total + 2 * PAD
    span = (2 * REACH + 1) * LANES
    tiles = total // CHUNK * (CHUNK - 8)
    level_shape = pltpu.VMEM((levels, total, LANES), F32)
    index_shape = pltpu.VMEM((NB, total, LANES), jnp.int32)
    return pl.pallas_call(
        prepare_kernel,
        out_shape=[
            pltpu.VMEM((levels * pitch, LANES), F32),
            pltpu.VMEM((levels * total, LANES), F32),
            pltpu.VMEM((tiles, span, 2 * LANES), BF16),
            level_shape,
            level_shape,
            level_shape,
            index_shape,
            index_shape,
            pltpu.VMEM((NB, total, LANES), F32),
            pltpu.VMEM((total, LANES), F32),
            pltpu.VMEM((total, LANES), F32),
        ],
        in_specs=[pl.BlockSpec(memory_space=pltpu.VMEM)] * 7,
        out_specs=[pl.BlockSpec(memory_space=pltpu.VMEM)] * 11,
        scratch_shapes=[
            pltpu.VMEM((2 * levels, pitch * LANES), BF16),
            pltpu.VMEM((NB, total, LANES), jnp.int32),
            pltpu.VMEM((NB, total, LANES), F32),
            pltpu.VMEM((levels - 1, total, LANES), F32),
        ],
        compiler_params=pltpu.CompilerParams(vmem_limit_bytes=14 * MIB),
        name="prepare",
    )(state, coef, offset, vert, wet, low, high)


def interval_kernel(
    width, column, mix, matrix, inv, from_up, from_down, lanes, codes, coefs, keep, wets,
    imported, low, high,
    state_out, imported_out, first, second, mixed, wide, force, flat,
):
    levels, total = inv.shape[0], inv.shape[1]
    rows = total - 2 * HALO
    pitch = column.shape[0] // levels

    force[:, 0:HALO, :] = low[...]
    force[:, HALO : HALO + rows, :] = imported[...]
    force[:, HALO + rows : total, :] = high[...]
    for field in range(width):
        flat[pl.ds(field * rows, rows), :] = imported[field]

    @pl.loop(0, rows, unroll=8)
    def _(row):
        here = pl.ds(pl.multiple_of(row * LANES, LANES), LANES)
        imported_out[:, here] = flat[pl.ds(row, width, stride=rows), :]

    def solve(source, spread_sum, out):
        @pl.loop(0, total // 8)
        def _(group):
            row = pl.multiple_of(group * 8, 8)
            here = pl.ds(row, 8)
            left = keep[here, :]
            wet = wets[here, :]
            partial = []
            for level in range(levels):
                value = left * source[pl.ds(level * pitch + PAD + row, 8), :]
                value = value + spread_sum[pl.ds(level * total + row, 8), :]
                if level < width:
                    value = value + force[level, here, :] * wet
                value = value * inv[level, here, :]
                if level:
                    value = value + from_up[level, here, :] * partial[-1]
                partial.append(value)
            following = partial[-1]
            out[pl.ds((levels - 1) * pitch + PAD + row, 8), :] = following
            for level in range(levels - 2, -1, -1):
                following = partial[level] + from_down[level, here, :] * following
                out[pl.ds(level * pitch + PAD + row, 8), :] = following

    buffers = (first, second)
    solve(column, mix, first)
    for step in range(1, STEPS):
        source, out = buffers[(step - 1) % 2], buffers[step % 2]
        to_lanes(levels, total, source, wide)
        spread(levels, total, source, wide, matrix, lanes, codes, coefs, mixed)
        solve(source, mixed, out)

    last = buffers[(STEPS - 1) % 2]

    @pl.loop(0, rows, unroll=8)
    def _(row):
        here = pl.ds(pl.multiple_of(row * LANES, LANES), LANES)
        for level in range(0, levels, 8):
            at = level * pitch + PAD + HALO + row
            state_out[level : level + 8, here] = last[pl.ds(at, 8, stride=pitch), :]


def interval(column, mix, matrix, inv, *rest):
    levels, total = inv.shape[0], inv.shape[1]
    pitch = column.shape[0] // levels
    width, rows = rest[-3].shape[0], rest[-3].shape[1]
    operands = (column, mix, matrix, inv, *rest)
    return pl.pallas_call(
        functools.partial(interval_kernel, width),
        out_shape=[
            jax.ShapeDtypeStruct((levels, rows * LANES), F32),
            jax.ShapeDtypeStruct((width, rows * LANES), F32),
        ],
        in_specs=[pl.BlockSpec(memory_space=pltpu.VMEM)] * len(operands),
        out_specs=[pl.BlockSpec(memory_space=pltpu.VMEM)] * 2,
        scratch_shapes=[
            pltpu.VMEM(column.shape, F32),
            pltpu.VMEM(column.shape, F32),
            pltpu.VMEM(mix.shape, F32),
            pltpu.VMEM((2 * levels, pitch * LANES), BF16),
            pltpu.VMEM((width, total, LANES), F32),
            pltpu.VMEM((width * rows, LANES), F32),
        ],
        compiler_params=pltpu.CompilerParams(vmem_limit_bytes=14 * MIB),
        name="interval",
    )(*operands)


def local(
    state,
    export_fields,
    remap_weights,
    routes,
    target_block,
    source_block,
    wet_mask,
    edge_coeff,
    edge_offset,
    vert_coeff,
):
    owners = lax.axis_size("dom")
    comps = lax.axis_size("comp")
    cells = state.shape[2]
    block_count = remap_weights.shape[1]
    capacity = max(2, 2 * block_count // owners)
    width = export_fields.shape[1]
    rows = cells // LANES
    me = lax.axis_index("dom").astype(jnp.int32)[None]
    coef = edge_coeff[0].reshape(-1, rows, LANES)
    offset = edge_offset[0].reshape(-1, rows, LANES)
    vert = vert_coeff[0].reshape(-1, rows, LANES)
    wet = wet_mask.reshape(rows, LANES)

    values, low, high = remap(
        routes[0, :, 0],
        target_block[0],
        source_block[0],
        me,
        export_fields[0],
        remap_weights[0],
        state[0],
        (coef, offset, vert, wet),
        owners,
        capacity,
    )
    values = lax.all_to_all(values, "dom", split_axis=0, concat_axis=0, tiled=True)

    forward = [(i, (i + 1) % owners) for i in range(owners)]
    backward = [(target, source) for source, target in forward]
    low = lax.ppermute(low, "dom", forward)
    high = lax.ppermute(high, "dom", backward)
    prepared = prepare(state[0], coef, offset, vert, wet, low, high)

    pitch = capacity * width + 8
    summed, first_rows, last_rows = assemble(
        values.reshape(owners * pitch, LANES), owners, capacity, width, rows
    )

    def across(value, shift):
        pairs = [
            (comp * owners + dom, (comp + 1) % comps * owners + (dom + shift) % owners)
            for comp in range(comps)
            for dom in range(owners)
        ]
        return lax.ppermute(value, ("comp", "dom"), pairs)

    imported = across(summed, 0)
    from_low = across(last_rows, 1)
    from_high = across(first_rows, -1)
    new_state, imported = interval(*prepared, imported, from_low, from_high)
    return (new_state[None], imported[None])


def solution(mesh):
    placed = (
        P("comp", None, "dom"),
        P("comp", None, "dom"),
        P("comp", "dom", None, None),
        P("comp", "dom", None),
        P("comp", "dom"),
        P("comp", "dom"),
        P("comp", "dom"),
        P("comp", None, "dom"),
        P("comp", None, "dom"),
        P("comp", None, "dom"),
    )
    return jax.shard_map(
        local,
        mesh=mesh,
        in_specs=placed,
        out_specs=(P("comp", None, "dom"), P("comp", None, "dom")),
        check_vma=False,
    )
```

time: 1780 us -> 136 us (0.08); the launches traced: 1760 us -> 135 us
  local copies, waits for them, and re-layouts: 1630 us -> 20.3 us
  Pallas kernels: 0 us -> 66.7 us
  other arithmetic: 49.9 us -> 0 us
  blocking collectives: 0 us -> 36.1 us
  waiting for transfers between devices: 24.3 us -> 0.01 us
  starting transfers between devices: 33.8 us -> 11.3 us
    gather x48 -> x0, local copies, waits for them, and re-layouts: 1580 us -> none  [local(): widened[:, neighbours[which]] - column_state]
    pallas_call x0 -> x4, Pallas kernels: none -> 66.7 us  [the longest x1 30.5 us: interval(): pl.pallas_call(functools.partial(interval_kernel, width), out_shape=[jax....]
    all_to_all x0 -> x1, blocking collectives: none -> 36.1 us  [local(): lax.all_to_all(values, 'dom', split_axis=0, concat_axis=0, tiled=True)]
    concatenate x4 -> x0, local copies, waits for them, and re-layouts: 24.5 us -> none  [extended(): block = jnp.concatenate([low, block, high], axis=dim)]
    ppermute x10 -> x5, waiting for transfers between devices: 24.3 us -> 0.01 us  [the longest x3 0.01 us: across(): return lax.ppermute(value, ('comp', 'dom'), pairs)]
    unnamed x252 -> x16, local copies, waits for them, and re-layouts: 2.06 us -> 20.3 us
  transfers between devices with their start and end apart: 12 -> 5, of which waited for: 8 -> 0; matrix products, arithmetic and copies ran while one was open for 24% -> 0% of each run, Pallas kernels for 0% -> 20%
where the time goes in v1:
time: 136 us; the launch traced here: 135 us
  Pallas kernels  66.7 us (49%)
  blocking collectives  36.1 us (27%)
  local copies, waits for them, and re-layouts  20.3 us (15%)
  starting transfers between devices  11.3 us (8%)
    all_to_all x1, blocking collectives, local(): lax.all_to_all(values, 'dom', split_axis=0, concat_axis=0, tiled=True)  36.1 us
    pallas_call x1, Pallas kernels, interval(): pl.pallas_call(functools.partial(interval_kernel, width), out_shape=[jax....  30.5 us
    pallas_call x1, Pallas kernels, prepare(): pl.pallas_call(prepare_kernel, out_shape=[pltpu.VMEM((levels * pitch, LAN...  26.4 us
    unnamed x16, local copies, waits for them, and re-layouts  20.3 us
    pallas_call x1, Pallas kernels, remap(): pl.pallas_call(functools.partial(remap_kernel, owners, capacity), grid_sp...  9.37 us
    ppermute x3, starting transfers between devices, across(): return lax.ppermute(value, ('comp', 'dom'), pairs)  6.9 us
    ppermute x1, starting transfers between devices, local(): high = lax.ppermute(high, 'dom', backward)  4.44 us
  transfers between devices with their start and end apart: 5, of which 0 were waited for; matrix products, arithmetic and copies ran while one was open for 0% of the time, Pallas kernels for 20%

profile of v1, /device:TPU:0, one launch (start us, length us, event | category | flops | bytes accessed | tf_op | source)
XLA Modules:
  0.0 135.2 jit_solution(5815049701394626632)
XLA Ops:
  0.6 9.4 %remap.1 = (f32[16,136,128]{2,1,0:T(8,128)}, f32[352,128]{1,0:T(8,128)}, f32[352,128]{1,0:T(8,128)}) custom-call(s32[128]{0:T(128)} %bitcast.32, s32[128]{0:T(128)} %bitcast.33, s32[128]{0:T(128)} %bitcast.34, s32[1]{0:T(128)} %bitcast.8.me, f32[8,16384]{1,0:T(8,128)} %bitcast.31, f32[128,128,128]{2,1,0:T(8,128)} %bitcast.30, f32[16,16384]{1,0:T(8,128)} %bitcast.27, ...), custom_call_target="tpu_custom_call" | custom-call | tf_op jit(solution)/shard_map/remap/pallas_call | solution.py:104
  10.0 0.0 copy-start.7
  10.0 0.0 copy-start.6
  10.0 0.0 copy-start.2
  10.0 0.0 copy-start.3
  10.0 0.0 copy-start.4
  10.1 0.0 copy-start.5
  10.1 36.1 %all_to_all.5 = f32[16,136,128]{2,1,0:T(8,128)S(1)} all-to-all(f32[16,136,128]{2,1,0:T(8,128)} %get-tuple-element.34), channel_id=1, replica_groups=mesh['comp'=2,'dom'=16] {'dom'}, dimensions={0} | all-to-all | bytes 2228224 | tf_op jit(solution)/shard_map/all_to_all | solution.py:495
  46.1 0.4 assemble.1
  46.6 1.6 %collective-permute-start.2 = (f32[8,128,128]{2,1,0:T(8,128)S(1)}, f32[8,128,128]{2,1,0:T(8,128)S(1)}, u32[]{:S(2)}, u32[]{:S(2)}) collective-permute-start(f32[8,128,128]{2,1,0:T(8,128)S(1)} %get-tuple-element.35), channel_id=1, source_target_pairs={{0,16},{1,17},{2,18},{3,19},{4,20},{5,21},{6,22},{7,23},{8,24},{9,... | collective-permute-start | bytes 1572872 | tf_op jit(solution)/shard_map/ppermute | solution.py:514
  48.1 0.0 copy-done.7
  48.1 0.0 collective-permute-start
  48.1 0.0 copy-done.6
  48.1 4.4 %collective-permute-start.1 = (f32[352,128]{1,0:T(8,128)S(1)}, f32[352,128]{1,0:T(8,128)S(1)}, u32[]{:S(2)}, u32[]{:S(2)}) collective-permute-start(f32[352,128]{1,0:T(8,128)S(1)} %copy-done.6), channel_id=1, source_target_pairs={{1,0},{2,1},{3,2},{4,3},{5,4},{6,5},{7,6},{8,7},{9,8},{10,9},{11,1... | collective-permute-start | bytes 540680 | tf_op jit(solution)/shard_map/ppermute | solution.py:500
  52.6 0.0 collective-permute-start.3
  52.6 5.3 %collective-permute-start.4 = (f32[8,8,128]{2,1,0:T(8,128)S(1)}, f32[8,8,128]{2,1,0:T(8,128)S(1)}, u32[]{:S(2)}, u32[]{:S(2)}) collective-permute-start(f32[8,8,128]{2,1,0:T(8,128)S(1)} %get-tuple-element.37), channel_id=1, source_target_pairs={{0,31},{1,16},{2,17},{3,18},{4,19},{5,20},{6,21},{7,22},{8,23},{9,... | collective-permute-start | bytes 98312 | tf_op jit(solution)/shard_map/ppermute | solution.py:514
  57.9 0.0 collective-permute-done.low
  57.9 0.0 collective-permute-done.1.high
  57.9 0.0 copy-done.2
  57.9 0.0 copy-done.3
  57.9 0.0 copy-done.4
  58.0 0.0 copy-done.5
  58.0 26.4 %prepare.1 = (f32[2560,128]{1,0:T(8,128)S(1)}, f32[2304,128]{1,0:T(8,128)S(1)}, bf16[96,640,256]{2,1,0:T(8,128)(2,1)S(1)}, f32[16,144,128]{2,1,0:T(8,128)S(1)}, ...) custom-call(f32[16,16384]{1,0:T(8,128)} %bitcast.29, ...), custom_call_target="tpu_custom_call" | custom-call | tf_op jit(solution)/shard_map/prepare/pallas_call | solution.py:343
  84.4 0.0 copy-start
  84.4 10.4 %copy-done = bf16[96,640,256]{2,1,0:T(8,128)(2,1)} copy-done((bf16[96,640,256]{2,1,0:T(8,128)(2,1)}, bf16[96,640,256]{2,1,0:T(8,128)(2,1)S(1)}, u32[]{:S(2)}) %copy-start) | copy-done | bytes 31457304
  94.8 0.0 collective-permute-done.3.low
  94.8 0.0 collective-permute-done.4.high
  94.8 0.0 collective-permute-done.2.imported
  94.8 0.0 copy-start.1
  94.8 9.9 %copy-done.1 = bf16[96,640,256]{2,1,0:T(8,128)(2,1)S(1)} copy-done((bf16[96,640,256]{2,1,0:T(8,128)(2,1)S(1)}, bf16[96,640,256]{2,1,0:T(8,128)(2,1)}, u32[]{:S(2)}) %copy-start.1) | copy-done | bytes 31457304
  104.7 30.5 %interval.1 = (f32[16,16384]{1,0:T(8,128)}, f32[8,16384]{1,0:T(8,128)}) custom-call(f32[2560,128]{1,0:T(8,128)S(1)} %get-tuple-element.23.column, f32[2304,128]{1,0:T(8,128)S(1)} %get-tuple-element.24.mix, bf16[96,640,256]{2,1,0:T(8,128)(2,1)S(1)} %copy-done.1, f32[16,144,128]{2,1,0:T(8,128)S(1)} %get-tuple-element.26.inv, ...), custom_call_target="tpu_custom_call" | custom-call | tf_op jit(solution)/shard_map/interval/pallas_call | solution.py:437
Async XLA Ops:
  10.0 38.1 %copy-start.7 = (f32[352,128]{1,0:T(8,128)S(1)}, f32[352,128]{1,0:T(8,128)}, u32[]{:S(2)}) copy-start(f32[352,128]{1,0:T(8,128)} %get-tuple-element.21) | copy-start | bytes 540676
  10.0 38.1 %copy-start.6 = (f32[352,128]{1,0:T(8,128)S(1)}, f32[352,128]{1,0:T(8,128)}, u32[]{:S(2)}) copy-start(f32[352,128]{1,0:T(8,128)} %get-tuple-element.22) | copy-start | bytes 540676
  10.0 47.9 %copy-start.2 = (f32[1,15,16384]{2,0,1:T(1,128)S(1)}, f32[1,15,16384]{2,0,1:T(1,128)}, u32[]{:S(2)}) copy-start(f32[1,15,16384]{2,0,1:T(1,128)} %param.19) | copy-start | bytes 2949124
  10.0 47.9 %copy-start.3 = (f32[1,6,16384]{2,0,1:T(1,128)S(1)}, f32[1,6,16384]{2,0,1:T(1,128)}, u32[]{:S(2)}) copy-start(f32[1,6,16384]{2,0,1:T(1,128)} %param.17) | copy-start | bytes 1179652
  10.0 47.9 %copy-start.4 = (s32[1,6,16384]{2,0,1:T(1,128)S(1)}, s32[1,6,16384]{2,0,1:T(1,128)}, u32[]{:S(2)}) copy-start(s32[1,6,16384]{2,0,1:T(1,128)} %param.18) | copy-start | bytes 1179652
  10.1 47.9 %copy-start.5 = (s32[1,16384]{1,0:T(1,128)S(1)}, s32[1,16384]{1,0:T(1,128)}, u32[]{:S(2)}) copy-start(s32[1,16384]{1,0:T(1,128)} %param.16) | copy-start | bytes 196612
  46.6 48.2 %collective-permute-start.2 = (f32[8,128,128]{2,1,0:T(8,128)S(1)}, f32[8,128,128]{2,1,0:T(8,128)S(1)}, u32[]{:S(2)}, u32[]{:S(2)}) collective-permute-start(f32[8,128,128]{2,1,0:T(8,128)S(1)} %get-tuple-element.35), channel_id=1, source_target_pairs={{0,16},{1,17},{2,18},{3,19},{4,20},{5,21},{6,22},{7,23},{8,24},{9,... | collective-permute-start | bytes 1572872 | tf_op jit(solution)/shard_map/ppermute | solution.py:514
  48.1 9.8 %collective-permute-start = (f32[352,128]{1,0:T(8,128)S(1)}, f32[352,128]{1,0:T(8,128)S(1)}, u32[]{:S(2)}, u32[]{:S(2)}) collective-permute-start(f32[352,128]{1,0:T(8,128)S(1)} %copy-done.7), channel_id=1, source_target_pairs={{0,1},{1,2},{2,3},{3,4},{4,5},{5,6},{6,7},{7,8},{8,9},{9,10},{10,1... | collective-permute-start | bytes 540680 | tf_op jit(solution)/shard_map/ppermute | solution.py:499
  48.1 9.8 %collective-permute-start.1 = (f32[352,128]{1,0:T(8,128)S(1)}, f32[352,128]{1,0:T(8,128)S(1)}, u32[]{:S(2)}, u32[]{:S(2)}) collective-permute-start(f32[352,128]{1,0:T(8,128)S(1)} %copy-done.6), channel_id=1, source_target_pairs={{1,0},{2,1},{3,2},{4,3},{5,4},{6,5},{7,6},{8,7},{9,8},{10,9},{11,1... | collective-permute-start | bytes 540680 | tf_op jit(solution)/shard_map/ppermute | solution.py:500
  52.6 42.2 %collective-permute-start.3 = (f32[8,8,128]{2,1,0:T(8,128)S(1)}, f32[8,8,128]{2,1,0:T(8,128)S(1)}, u32[]{:S(2)}, u32[]{:S(2)}) collective-permute-start(f32[8,8,128]{2,1,0:T(8,128)S(1)} %get-tuple-element.36), channel_id=1, source_target_pairs={{0,17},{1,18},{2,19},{3,20},{4,21},{5,22},{6,23},{7,24},{8,25},{9,... | collective-permute-start | bytes 98312 | tf_op jit(solution)/shard_map/ppermute | solution.py:514
  52.6 42.2 %collective-permute-start.4 = (f32[8,8,128]{2,1,0:T(8,128)S(1)}, f32[8,8,128]{2,1,0:T(8,128)S(1)}, u32[]{:S(2)}, u32[]{:S(2)}) collective-permute-start(f32[8,8,128]{2,1,0:T(8,128)S(1)} %get-tuple-element.37), channel_id=1, source_target_pairs={{0,31},{1,16},{2,17},{3,18},{4,19},{5,20},{6,21},{7,22},{8,23},{9,... | collective-permute-start | bytes 98312 | tf_op jit(solution)/shard_map/ppermute | solution.py:514
  84.4 10.4 %copy-start = (bf16[96,640,256]{2,1,0:T(8,128)(2,1)}, bf16[96,640,256]{2,1,0:T(8,128)(2,1)S(1)}, u32[]{:S(2)}) copy-start(bf16[96,640,256]{2,1,0:T(8,128)(2,1)S(1)} %get-tuple-element.25.matrix) | copy-start | bytes 94371840
  94.8 9.9 %copy-start.1 = (bf16[96,640,256]{2,1,0:T(8,128)(2,1)S(1)}, bf16[96,640,256]{2,1,0:T(8,128)(2,1)}, u32[]{:S(2)}) copy-start(bf16[96,640,256]{2,1,0:T(8,128)(2,1)} %copy-done) | copy-start | bytes 94371840

commit v2 on v1

--- a/solution.py
+++ b/solution.py
@@ -12,6 +12,7 @@
 STEPS = 4
 LANES = 128
 REACH = RIM // LANES
+WINDOW = 2 * REACH + 1
 HALO = STEPS * REACH
 PAD = 8
 MIB = 2**20
@@ -195,7 +196,7 @@
 
 def spread(levels, total, column, wide, matrix, lanes, codes, coefs, mix):
     pitch = column.shape[0] // levels
-    span = (2 * REACH + 1) * LANES
+    span = WINDOW * LANES
 
     @pl.loop(0, total // CHUNK)
     def _(chunk):
@@ -203,9 +204,10 @@
         for tile in range(CHUNK - 8):
             row = base + tile
             at = pl.multiple_of((row + PAD - REACH) * LANES, LANES)
+            entry = chunk * (CHUNK - 8) + tile
             got = jnp.dot(
                 wide[:, pl.ds(at, span)],
-                matrix[chunk * (CHUNK - 8) + tile],
+                jnp.concatenate([part[entry] for part in matrix], axis=0),
                 preferred_element_type=F32,
             )
             got = got[:, :LANES] + got[:, LANES:]
@@ -221,7 +223,7 @@
             factor = coefs[which, here, :]
             for level in range(levels):
                 found = None
-                for reach in range(2 * REACH + 1):
+                for reach in range(WINDOW):
                     at = level * pitch + PAD - REACH + reach + row
                     picked = lane_pick(column[pl.ds(at, 8), :], index)
                     found = picked if found is None else jnp.where(code == reach, picked, found)
@@ -233,9 +235,10 @@
 
 def prepare_kernel(
     state, coef, offset, vert, wet, low, high,
-    column, mix, matrix, inv, from_up, from_down, lanes, codes, coefs, keep, wets,
-    wide, places, merged, verts,
+    column, mix, inv, from_up, from_down, lanes, codes, coefs, keep, wets,
+    *refs,
 ):
+    matrix, (wide, places, merged, verts) = refs[:WINDOW], refs[WINDOW:]
     levels = state.shape[0]
     rows = state.shape[1] // LANES
     total = rows + 2 * HALO
@@ -298,7 +301,7 @@
             from_down[level, here, :] = carried
             upper = lower
 
-    span = (2 * REACH + 1) * LANES
+    span = WINDOW * LANES
     small = jnp.int16
 
     @pl.loop(0, total // CHUNK)
@@ -325,8 +328,9 @@
                     hit = spots[which] == key
                     by_high = jnp.where(hit, highs[which], by_high)
                     by_low = jnp.where(hit, lows[which], by_low)
-                matrix[at, first : first + 16, 0:LANES] = by_high
-                matrix[at, first : first + 16, LANES : 2 * LANES] = by_low
+                part, inside = matrix[first // LANES], first % LANES
+                part[at, inside : inside + 16, 0:LANES] = by_high
+                part[at, inside : inside + 16, LANES : 2 * LANES] = by_low
 
     spread(levels, total, column, wide, matrix, lanes, codes, coefs, mix)
 
@@ -336,7 +340,6 @@
     rows = cells // LANES
     total = rows + 2 * HALO
     pitch = total + 2 * PAD
-    span = (2 * REACH + 1) * LANES
     tiles = total // CHUNK * (CHUNK - 8)
     level_shape = pltpu.VMEM((levels, total, LANES), F32)
     index_shape = pltpu.VMEM((NB, total, LANES), jnp.int32)
@@ -345,7 +348,6 @@
         out_shape=[
             pltpu.VMEM((levels * pitch, LANES), F32),
             pltpu.VMEM((levels * total, LANES), F32),
-            pltpu.VMEM((tiles, span, 2 * LANES), BF16),
             level_shape,
             level_shape,
             level_shape,
@@ -354,25 +356,31 @@
             pltpu.VMEM((NB, total, LANES), F32),
             pltpu.VMEM((total, LANES), F32),
             pltpu.VMEM((total, LANES), F32),
+            *[pltpu.VMEM((tiles, LANES, 2 * LANES), BF16)] * WINDOW,
         ],
         in_specs=[pl.BlockSpec(memory_space=pltpu.VMEM)] * 7,
-        out_specs=[pl.BlockSpec(memory_space=pltpu.VMEM)] * 11,
+        out_specs=[pl.BlockSpec(memory_space=pltpu.VMEM)] * (10 + WINDOW),
         scratch_shapes=[
             pltpu.VMEM((2 * levels, pitch * LANES), BF16),
             pltpu.VMEM((NB, total, LANES), jnp.int32),
             pltpu.VMEM((NB, total, LANES), F32),
             pltpu.VMEM((levels - 1, total, LANES), F32),
         ],
-        compiler_params=pltpu.CompilerParams(vmem_limit_bytes=14 * MIB),
+        compiler_params=pltpu.CompilerParams(vmem_limit_bytes=8 * MIB),
+        cost_estimate=pl.CostEstimate(
+            flops=2 * tiles * 8 * levels * WINDOW * LANES * LANES,
+            bytes_accessed=80 * MIB,
+            transcendentals=0,
+        ),
         name="prepare",
     )(state, coef, offset, vert, wet, low, high)
 
 
 def interval_kernel(
-    width, column, mix, matrix, inv, from_up, from_down, lanes, codes, coefs, keep, wets,
-    imported, low, high,
-    state_out, imported_out, first, second, mixed, wide, force, flat,
+    width, column, mix, inv, from_up, from_down, lanes, codes, coefs, keep, wets, *refs
 ):
+    matrix, refs = refs[:WINDOW], refs[WINDOW:]
+    imported, low, high, state_out, imported_out, first, second, mixed, wide, force, flat = refs
     levels, total = inv.shape[0], inv.shape[1]
     rows = total - 2 * HALO
     pitch = column.shape[0] // levels
@@ -429,11 +437,11 @@
             state_out[level : level + 8, here] = last[pl.ds(at, 8, stride=pitch), :]
 
 
-def interval(column, mix, matrix, inv, *rest):
+def interval(column, mix, inv, *rest):
     levels, total = inv.shape[0], inv.shape[1]
     pitch = column.shape[0] // levels
     width, rows = rest[-3].shape[0], rest[-3].shape[1]
-    operands = (column, mix, matrix, inv, *rest)
+    operands = (column, mix, inv, *rest)
     return pl.pallas_call(
         functools.partial(interval_kernel, width),
         out_shape=[
@@ -450,7 +458,7 @@
             pltpu.VMEM((width, total, LANES), F32),
             pltpu.VMEM((width * rows, LANES), F32),
         ],
-        compiler_params=pltpu.CompilerParams(vmem_limit_bytes=14 * MIB),
+        compiler_params=pltpu.CompilerParams(vmem_limit_bytes=10 * MIB),
         name="interval",
     )(*operands)
 
@@ -499,6 +507,7 @@
     low = lax.ppermute(low, "dom", forward)
     high = lax.ppermute(high, "dom", backward)
     prepared = prepare(state[0], coef, offset, vert, wet, low, high)
+    values, prepared = lax.optimization_barrier((values, prepared))
 
     pitch = capacity * width + 8
     summed, first_rows, last_rows = assemble(

time: 136 us -> 159 us (1.17)
  blocking collectives: 36.1 us -> 0 us
  local copies, waits for them, and re-layouts: 20.3 us -> 47 us
  waiting for transfers between devices: 0.01 us -> 24.5 us
  starting transfers between devices: 11.3 us -> 18.9 us
    all_to_all x1 -> x0, blocking collectives: 36.1 us -> none  [local(): lax.all_to_all(values, 'dom', split_axis=0, concat_axis=0, tiled=True)]
    unnamed x16 -> x70, local copies, waits for them, and re-layouts: 20.3 us -> 47 us
    ppermute x1, waiting for transfers between devices: 0.01 us -> 21.5 us  [local(): low = lax.ppermute(low, 'dom', forward)]
    all_to_all x0 -> x1, starting transfers between devices: none -> 7.53 us  [local(): lax.all_to_all(values, 'dom', split_axis=0, concat_axis=0, tiled=True)]
    ppermute x3, waiting for transfers between devices: 0.01 us -> 3.05 us  [across(): return lax.ppermute(value, ('comp', 'dom'), pairs)]
  transfers between devices with their start and end apart: 5 -> 6, of which waited for: 0 -> 3; matrix products, arithmetic and copies ran while one was open for 0% -> 0% of each run, Pallas kernels for 20% -> 16%
where the time goes in v2:
time: 159 us; the launch traced here: 157 us
  Pallas kernels  65.7 us (41%)
  local copies, waits for them, and re-layouts  47 us (30%)
  waiting for transfers between devices  24.5 us (15%)
  starting transfers between devices  18.9 us (12%)
    unnamed x70, local copies, waits for them, and re-layouts  47 us
    pallas_call x1, Pallas kernels, interval(): pl.pallas_call(functools.partial(interval_kernel, width), out_shape=[jax....  30.5 us
    pallas_call x1, Pallas kernels, prepare(): pl.pallas_call(prepare_kernel, out_shape=[pltpu.VMEM((levels * pitch, LAN...  25.3 us
    ppermute x1, waiting for transfers between devices, local(): low = lax.ppermute(low, 'dom', forward)  21.5 us
    pallas_call x1, Pallas kernels, remap(): pl.pallas_call(functools.partial(remap_kernel, owners, capacity), grid_sp...  9.5 us
    all_to_all x1, starting transfers between devices, local(): lax.all_to_all(values, 'dom', split_axis=0, concat_axis=0, tiled=True)  7.53 us
    ppermute x3, starting transfers between devices, across(): return lax.ppermute(value, ('comp', 'dom'), pairs)  6.9 us
    ppermute x1, starting transfers between devices, local(): high = lax.ppermute(high, 'dom', backward)  4.08 us
  transfers between devices with their start and end apart: 6, of which 3 were waited for; matrix products, arithmetic and copies ran while one was open for 0% of the time, Pallas kernels for 16%

profile of v2, /device:TPU:0, one launch (start us, length us, event | category | flops | bytes accessed | tf_op | source)
XLA Modules:
  0.0 156.9 jit_solution(11454236111327772595)
XLA Ops:
  0.6 9.5 %remap.1 = (f32[16,136,128]{2,1,0:T(8,128)}, f32[352,128]{1,0:T(8,128)}, f32[352,128]{1,0:T(8,128)}) custom-call(s32[128]{0:T(128)} %bitcast.32, s32[128]{0:T(128)} %bitcast.33, s32[128]{0:T(128)} %bitcast.34, s32[1]{0:T(128)} %bitcast.3.me, f32[8,16384]{1,0:T(8,128)} %bitcast.31, f32[128,128,128]{2,1,0:T(8,128)} %bitcast.30, f32[16,16384]{1,0:T(8,128)} %bitcast.15, ...), custom_call_target="tpu_custom_call" | custom-call | tf_op jit(solution)/shard_map/remap/pallas_call | solution.py:105
  10.1 0.0 copy-start.11
  10.2 7.5 %all-to-all-start = ((f32[16,136,128]{2,1,0:T(8,128)}), f32[16,136,128]{2,1,0:T(8,128)S(1)}, u32[]{:S(2)}, u32[]{:S(2)}) async-start(f32[16,136,128]{2,1,0:T(8,128)} %get-tuple-element.41), calls=%async_computation | async-start | bytes 2228224 | tf_op jit(solution)/shard_map/all_to_all | solution.py:503
  17.7 0.4 collective-permute-start
  18.1 4.1 %collective-permute-start.1 = (f32[352,128]{1,0:T(8,128)}, f32[352,128]{1,0:T(8,128)S(1)}, u32[]{:S(2)}, u32[]{:S(2)}) collective-permute-start(f32[352,128]{1,0:T(8,128)} %get-tuple-element.43), channel_id=1, source_target_pairs={{1,0},{2,1},{3,2},{4,3},{5,4},{6,5},{7,6},{8,7},{9,8},{10,9},{11,1... | collective-permute-start | bytes 540680 | tf_op jit(solution)/shard_map/ppermute | solution.py:508
  22.2 21.5 %collective-permute-done.low = f32[352,128]{1,0:T(8,128)S(1)} collective-permute-done((f32[352,128]{1,0:T(8,128)}, f32[352,128]{1,0:T(8,128)S(1)}, u32[]{:S(2)}, u32[]{:S(2)}) %collective-permute-start) | collective-permute-done | bytes 180256 | tf_op jit(solution)/shard_map/ppermute | solution.py:507
  43.7 0.0 collective-permute-done.1.high
  43.7 0.0 copy-start.13
  43.7 1.0 copy-done.13
  44.7 0.8 copy-done.30
  45.5 25.3 %prepare.1 = (f32[2560,128]{1,0:T(8,128)S(1)}, f32[2304,128]{1,0:T(8,128)S(1)}, f32[16,144,128]{2,1,0:T(8,128)S(1)}, f32[16,144,128]{2,1,0:T(8,128)S(1)}, f32[16...) custom-call(f32[16,16384]{1,0:T(8,128)S(1)} %bitcast.17, ...), custom_call_target="tpu_custom_call" | custom-call | flops 2013265920 | bytes 83886080 | tf_op jit(solution)/shard_map/prepare/pallas_call | solution.py:346
  70.8 2.7 %copy-done = bf16[96,128,256]{2,1,0:T(8,128)(2,1)} copy-done((bf16[96,128,256]{2,1,0:T(8,128)(2,1)}, bf16[96,128,256]{2,1,0:T(8,128)(2,1)S(1)}, u32[]{:S(2)}) %copy-start) | copy-done | bytes 6291480
  73.5 2.7 %copy-done.2 = bf16[96,128,256]{2,1,0:T(8,128)(2,1)} copy-done((bf16[96,128,256]{2,1,0:T(8,128)(2,1)}, bf16[96,128,256]{2,1,0:T(8,128)(2,1)S(1)}, u32[]{:S(2)}) %copy-start.2) | copy-done | bytes 6291480
  76.1 2.6 %copy-done.4 = bf16[96,128,256]{2,1,0:T(8,128)(2,1)} copy-done((bf16[96,128,256]{2,1,0:T(8,128)(2,1)}, bf16[96,128,256]{2,1,0:T(8,128)(2,1)S(1)}, u32[]{:S(2)}) %copy-start.4) | copy-done | bytes 6291480
  78.7 2.6 %copy-done.6 = bf16[96,128,256]{2,1,0:T(8,128)(2,1)} copy-done((bf16[96,128,256]{2,1,0:T(8,128)(2,1)}, bf16[96,128,256]{2,1,0:T(8,128)(2,1)S(1)}, u32[]{:S(2)}) %copy-start.6) | copy-done | bytes 6291480
  81.4 2.7 %copy-done.8 = bf16[96,128,256]{2,1,0:T(8,128)(2,1)} copy-done((bf16[96,128,256]{2,1,0:T(8,128)(2,1)}, bf16[96,128,256]{2,1,0:T(8,128)(2,1)S(1)}, u32[]{:S(2)}) %copy-start.8) | copy-done | bytes 6291480
  84.1 1.1 copy-done.14
  85.2 1.0 copy-done.16
  86.2 1.0 copy-done.18
  87.2 1.0 copy-done.20
  88.3 1.1 copy-done.22
  89.3 0.8 copy-done.24
  90.1 0.8 copy-done.26
  90.8 0.8 copy-done.28
  91.6 0.6 copy-done.31
  92.2 0.6 copy-done.33
  92.9 0.0 all-to-all-done
  92.9 0.4 assemble.1
  93.3 1.6 collective-permute-start.2
  94.9 0.0 collective-permute-start.3
  94.9 5.3 %collective-permute-start.4 = (f32[8,8,128]{2,1,0:T(8,128)S(1)}, f32[8,8,128]{2,1,0:T(8,128)S(1)}, u32[]{:S(2)}, u32[]{:S(2)}) collective-permute-start(f32[8,8,128]{2,1,0:T(8,128)S(1)} %get-tuple-element.77), channel_id=1, source_target_pairs={{0,31},{1,16},{2,17},{3,18},{4,19},{5,20},{6,21},{7,22},{8,23},{9,... | collective-permute-start | bytes 98312 | tf_op jit(solution)/shard_map/ppermute | solution.py:523
  100.2 2.4 %collective-permute-done.3.refs_6_ = f32[8,8,128]{2,1,0:T(8,128)S(1)} collective-permute-done((f32[8,8,128]{2,1,0:T(8,128)S(1)}, f32[8,8,128]{2,1,0:T(8,128)S(1)}, u32[]{:S(2)}, u32[]{:S(2)}) %collective-permute-start.3) | collective-permute-done | bytes 32800 | tf_op jit(solution)/shard_map/ppermute | solution.py:523
  102.6 0.0 collective-permute-done.4.refs_7_
  102.6 0.7 collective-permute-done.2.refs_5_
  103.3 2.8 %copy-done.1 = bf16[96,128,256]{2,1,0:T(8,128)(2,1)S(1)} copy-done((bf16[96,128,256]{2,1,0:T(8,128)(2,1)S(1)}, bf16[96,128,256]{2,1,0:T(8,128)(2,1)}, u32[]{:S(2)}) %copy-start.1) | copy-done | bytes 6291480
  106.1 2.8 %copy-done.3 = bf16[96,128,256]{2,1,0:T(8,128)(2,1)S(1)} copy-done((bf16[96,128,256]{2,1,0:T(8,128)(2,1)S(1)}, bf16[96,128,256]{2,1,0:T(8,128)(2,1)}, u32[]{:S(2)}) %copy-start.3) | copy-done | bytes 6291480
  108.9 2.8 %copy-done.5 = bf16[96,128,256]{2,1,0:T(8,128)(2,1)S(1)} copy-done((bf16[96,128,256]{2,1,0:T(8,128)(2,1)S(1)}, bf16[96,128,256]{2,1,0:T(8,128)(2,1)}, u32[]{:S(2)}) %copy-start.5) | copy-done | bytes 6291480
  111.6 2.8 %copy-done.7 = bf16[96,128,256]{2,1,0:T(8,128)(2,1)S(1)} copy-done((bf16[96,128,256]{2,1,0:T(8,128)(2,1)S(1)}, bf16[96,128,256]{2,1,0:T(8,128)(2,1)}, u32[]{:S(2)}) %copy-start.7) | copy-done | bytes 6291480
  114.4 2.8 %copy-done.9 = bf16[96,128,256]{2,1,0:T(8,128)(2,1)S(1)} copy-done((bf16[96,128,256]{2,1,0:T(8,128)(2,1)S(1)}, bf16[96,128,256]{2,1,0:T(8,128)(2,1)}, u32[]{:S(2)}) %copy-start.9) | copy-done | bytes 6291480
  117.2 1.3 copy-done.15
  118.5 1.3 copy-done.17
  119.8 1.3 copy-done.19
  121.1 1.3 copy-done.21
  122.3 1.3 copy-done.23
  123.6 1.0 copy-done.29
  124.6 0.9 copy-done.32
  125.5 0.9 copy-done.34
  126.4 30.5 %interval.1 = (f32[16,16384]{1,0:T(8,128)}, f32[8,16384]{1,0:T(8,128)}) custom-call(f32[2560,128]{1,0:T(8,128)S(1)} %copy-done.15, f32[2304,128]{1,0:T(8,128)S(1)} %copy-done.17, f32[16,144,128]{2,1,0:T(8,128)S(1)} %copy-done.19, f32[16,144,128]{2,1,0:T(8,128)S(1)} %copy-done.21, f32[16,144,128]{2,1,0:T(8,128)S(1)} %copy-done.23, ...), custom_call_target="tpu_custom_call" | custom-call | tf_op jit(solution)/shard_map/interval/pallas_call | solution.py:445
  (38 shorter events, 0.1 us)
Async XLA Ops:
  0.6 43.0 %copy-start.12 = (f32[1,6,16384]{2,0,1:T(1,128)S(1)}, f32[1,6,16384]{2,0,1:T(1,128)}, u32[]{:S(2)}) copy-start(f32[1,6,16384]{2,0,1:T(1,128)} %param.17) | copy-start | bytes 1179652
  10.1 33.5 %copy-start.10 = (f32[1,16,16384]{2,1,0:T(8,128)S(1)}, f32[1,16,16384]{2,1,0:T(8,128)}, u32[]{:S(2)}) copy-start(f32[1,16,16384]{2,1,0:T(8,128)} %param.10) | copy-start | bytes 3145732
  10.1 33.5 %copy-start.11 = (f32[1,15,16384]{2,0,1:T(1,128)S(1)}, f32[1,15,16384]{2,0,1:T(1,128)}, u32[]{:S(2)}) copy-start(f32[1,15,16384]{2,0,1:T(1,128)} %param.19) | copy-start | bytes 2949124
  10.2 82.7 %all-to-all-start = ((f32[16,136,128]{2,1,0:T(8,128)}), f32[16,136,128]{2,1,0:T(8,128)S(1)}, u32[]{:S(2)}, u32[]{:S(2)}) async-start(f32[16,136,128]{2,1,0:T(8,128)} %get-tuple-element.41), calls=%async_computation | async-start | bytes 2228224 | tf_op jit(solution)/shard_map/all_to_all | solution.py:503
  17.7 26.0 %collective-permute-start = (f32[352,128]{1,0:T(8,128)}, f32[352,128]{1,0:T(8,128)S(1)}, u32[]{:S(2)}, u32[]{:S(2)}) collective-permute-start(f32[352,128]{1,0:T(8,128)} %get-tuple-element.42), channel_id=1, source_target_pairs={{0,1},{1,2},{2,3},{3,4},{4,5},{5,6},{6,7},{7,8},{8,9},{9,10},{10,1... | collective-permute-start | bytes 540680 | tf_op jit(solution)/shard_map/ppermute | solution.py:507
  18.1 25.5 %collective-permute-start.1 = (f32[352,128]{1,0:T(8,128)}, f32[352,128]{1,0:T(8,128)S(1)}, u32[]{:S(2)}, u32[]{:S(2)}) collective-permute-start(f32[352,128]{1,0:T(8,128)} %get-tuple-element.43), channel_id=1, source_target_pairs={{1,0},{2,1},{3,2},{4,3},{5,4},{6,5},{7,6},{8,7},{9,8},{10,9},{11,1... | collective-permute-start | bytes 540680 | tf_op jit(solution)/shard_map/ppermute | solution.py:508
  43.7 1.0 copy-start.13
  44.7 0.8 copy-start.30
  70.8 2.7 %copy-start = (bf16[96,128,256]{2,1,0:T(8,128)(2,1)}, bf16[96,128,256]{2,1,0:T(8,128)(2,1)S(1)}, u32[]{:S(2)}) copy-start(bf16[96,128,256]{2,1,0:T(8,128)(2,1)S(1)} %get-tuple-element.69.refs_0_) | copy-start | bytes 18874372
  73.5 2.7 %copy-start.2 = (bf16[96,128,256]{2,1,0:T(8,128)(2,1)}, bf16[96,128,256]{2,1,0:T(8,128)(2,1)S(1)}, u32[]{:S(2)}) copy-start(bf16[96,128,256]{2,1,0:T(8,128)(2,1)S(1)} %get-tuple-element.70.refs_1_) | copy-start | bytes 18874372
  76.1 2.6 %copy-start.4 = (bf16[96,128,256]{2,1,0:T(8,128)(2,1)}, bf16[96,128,256]{2,1,0:T(8,128)(2,1)S(1)}, u32[]{:S(2)}) copy-start(bf16[96,128,256]{2,1,0:T(8,128)(2,1)S(1)} %get-tuple-element.71.refs_2_) | copy-start | bytes 18874372
  78.7 2.6 %copy-start.6 = (bf16[96,128,256]{2,1,0:T(8,128)(2,1)}, bf16[96,128,256]{2,1,0:T(8,128)(2,1)S(1)}, u32[]{:S(2)}) copy-start(bf16[96,128,256]{2,1,0:T(8,128)(2,1)S(1)} %get-tuple-element.72.refs_3_) | copy-start | bytes 18874372
  81.4 2.7 %copy-start.8 = (bf16[96,128,256]{2,1,0:T(8,128)(2,1)}, bf16[96,128,256]{2,1,0:T(8,128)(2,1)S(1)}, u32[]{:S(2)}) copy-start(bf16[96,128,256]{2,1,0:T(8,128)(2,1)S(1)} %get-tuple-element.73.refs_4_) | copy-start | bytes 18874372
  84.1 1.1 copy-start.14
  85.2 1.0 copy-start.16
  86.2 1.1 copy-start.18
  87.2 1.0 copy-start.20
  88.3 1.1 copy-start.22
  89.3 0.8 copy-start.24
  90.1 0.8 copy-start.26
  90.8 0.8 copy-start.28
  91.6 0.6 copy-start.31
  92.2 0.6 copy-start.33
  92.9 10.4 %copy-start.25 = (s32[6,144,128]{2,1,0:T(8,128)S(1)}, s32[6,144,128]{2,1,0:T(8,128)}, u32[]{:S(2)}) copy-start(s32[6,144,128]{2,1,0:T(8,128)} %copy-done.24) | copy-start | bytes 1327108
  92.9 10.4 %copy-start.27 = (s32[6,144,128]{2,1,0:T(8,128)S(1)}, s32[6,144,128]{2,1,0:T(8,128)}, u32[]{:S(2)}) copy-start(s32[6,144,128]{2,1,0:T(8,128)} %copy-done.26) | copy-start | bytes 1327108
  93.3 9.9 %collective-permute-start.2 = (f32[8,128,128]{2,1,0:T(8,128)S(1)}, f32[8,128,128]{2,1,0:T(8,128)S(1)}, u32[]{:S(2)}, u32[]{:S(2)}) collective-permute-start(f32[8,128,128]{2,1,0:T(8,128)S(1)} %get-tuple-element.75), channel_id=1, source_target_pairs={{0,16},{1,17},{2,18},{3,19},{4,20},{5,21},{6,22},{7,23},{8,24},{9,... | collective-permute-start | bytes 1572872 | tf_op jit(solution)/shard_map/ppermute | solution.py:523
  94.9 7.7 %collective-permute-start.3 = (f32[8,8,128]{2,1,0:T(8,128)S(1)}, f32[8,8,128]{2,1,0:T(8,128)S(1)}, u32[]{:S(2)}, u32[]{:S(2)}) collective-permute-start(f32[8,8,128]{2,1,0:T(8,128)S(1)} %get-tuple-element.76), channel_id=1, source_target_pairs={{0,17},{1,18},{2,19},{3,20},{4,21},{5,22},{6,23},{7,24},{8,25},{9,... | collective-permute-start | bytes 98312 | tf_op jit(solution)/shard_map/ppermute | solution.py:523
  94.9 7.7 %collective-permute-start.4 = (f32[8,8,128]{2,1,0:T(8,128)S(1)}, f32[8,8,128]{2,1,0:T(8,128)S(1)}, u32[]{:S(2)}, u32[]{:S(2)}) collective-permute-start(f32[8,8,128]{2,1,0:T(8,128)S(1)} %get-tuple-element.77), channel_id=1, source_target_pairs={{0,31},{1,16},{2,17},{3,18},{4,19},{5,20},{6,21},{7,22},{8,23},{9,... | collective-permute-start | bytes 98312 | tf_op jit(solution)/shard_map/ppermute | solution.py:523
  103.3 2.8 %copy-start.1 = (bf16[96,128,256]{2,1,0:T(8,128)(2,1)S(1)}, bf16[96,128,256]{2,1,0:T(8,128)(2,1)}, u32[]{:S(2)}) copy-start(bf16[96,128,256]{2,1,0:T(8,128)(2,1)} %copy-done) | copy-start | bytes 18874372
  106.1 2.8 %copy-start.3 = (bf16[96,128,256]{2,1,0:T(8,128)(2,1)S(1)}, bf16[96,128,256]{2,1,0:T(8,128)(2,1)}, u32[]{:S(2)}) copy-start(bf16[96,128,256]{2,1,0:T(8,128)(2,1)} %copy-done.2) | copy-start | bytes 18874372
  108.9 2.8 %copy-start.5 = (bf16[96,128,256]{2,1,0:T(8,128)(2,1)S(1)}, bf16[96,128,256]{2,1,0:T(8,128)(2,1)}, u32[]{:S(2)}) copy-start(bf16[96,128,256]{2,1,0:T(8,128)(2,1)} %copy-done.4) | copy-start | bytes 18874372
  111.6 2.8 %copy-start.7 = (bf16[96,128,256]{2,1,0:T(8,128)(2,1)S(1)}, bf16[96,128,256]{2,1,0:T(8,128)(2,1)}, u32[]{:S(2)}) copy-start(bf16[96,128,256]{2,1,0:T(8,128)(2,1)} %copy-done.6) | copy-start | bytes 18874372
  114.4 2.8 %copy-start.9 = (bf16[96,128,256]{2,1,0:T(8,128)(2,1)S(1)}, bf16[96,128,256]{2,1,0:T(8,128)(2,1)}, u32[]{:S(2)}) copy-start(bf16[96,128,256]{2,1,0:T(8,128)(2,1)} %copy-done.8) | copy-start | bytes 18874372
  117.2 1.3 copy-start.15
  118.5 1.3 copy-start.17
  119.8 1.3 copy-start.19
  121.1 1.3 copy-start.21
  122.3 1.3 copy-start.23
  123.6 1.0 copy-start.29
  124.6 0.9 copy-start.32
  125.5 0.9 copy-start.34

commit v3 on v2

--- a/solution.py
+++ b/solution.py
@@ -16,7 +16,8 @@
 HALO = STEPS * REACH
 PAD = 8
 MIB = 2**20
-CHUNK = 3 * 8
+GROUP = 8
+CHUNK = 2 * GROUP
 
 force_scale = 0.5
 
@@ -179,71 +180,209 @@
     return jnp.take_along_axis(value, index, axis=1, mode="promise_in_bounds")
 
 
-def to_lanes(levels, total, column, wide):
+def group_rows(chunk, chunks):
+    base = chunk * CHUNK
+    late = (chunk > chunks // 2).astype(jnp.int32) * GROUP
+    return pl.multiple_of(base + GROUP - late, GROUP), pl.multiple_of(base + late, GROUP)
+
+
+def to_lanes(levels, column, wide, row):
     pitch = column.shape[0] // levels
-
-    @pl.loop(0, total, unroll=8)
-    def _(row):
-        here = pl.ds(pl.multiple_of((row + PAD) * LANES, LANES), LANES)
-        tiles = [
-            column[pl.ds(level * pitch + PAD + row, 8, stride=pitch), :]
-            for level in range(0, levels, 8)
-        ]
-        high, low = split(jnp.concatenate(tiles, axis=0))
-        wide[0:levels, here] = high
-        wide[levels : 2 * levels, here] = low
-
-
-def spread(levels, total, column, wide, matrix, lanes, codes, coefs, mix):
+    here = pl.ds(pl.multiple_of((row + PAD) * LANES, LANES), LANES)
+    tiles = [
+        column[pl.ds(level * pitch + PAD + row, 8, stride=pitch), :]
+        for level in range(0, levels, 8)
+    ]
+    high, low = split(jnp.concatenate(tiles, axis=0))
+    wide[0:levels, here] = high
+    wide[levels : 2 * levels, here] = low
+
+
+def spread_tile(levels, total, wide, matrix, entry, row, mix):
+    at = pl.multiple_of((row + PAD - REACH) * LANES, LANES)
+    got = jnp.dot(
+        wide[:, pl.ds(at, WINDOW * LANES)],
+        jnp.concatenate([part[entry] for part in matrix], axis=0),
+        preferred_element_type=F32,
+    )
+    got = got[:, :LANES] + got[:, LANES:]
+    got = got[:levels] + got[levels:]
+    for level in range(0, levels, 8):
+        mix[pl.ds(level * total + row, 8, stride=total), :] = got[level : level + 8]
+
+
+def spread_group(levels, total, column, row, terms, mix):
     pitch = column.shape[0] // levels
+    right = [None] * levels
+    for which in range(NB):
+        index, code, factor = terms(which)
+        for level in range(levels):
+            found = None
+            for reach in range(WINDOW):
+                at = level * pitch + PAD - REACH + reach + row
+                picked = lane_pick(column[pl.ds(at, GROUP), :], index)
+                found = picked if found is None else jnp.where(code == reach, picked, found)
+            found = factor * found
+            right[level] = found if which == 0 else right[level] + found
+    for level in range(levels):
+        mix[pl.ds(level * total + row, GROUP), :] = right[level]
+
+
+def spots_of(offset):
+    return offset + lax.broadcasted_iota(jnp.int32, offset.shape, offset.ndim - 1) + RIM
+
+
+def lane_of(spot):
+    return jnp.bitwise_and(spot, LANES - 1)
+
+
+def code_of(spot):
+    return lax.shift_right_logical(spot, LANES.bit_length() - 1)
+
+
+def state_rows(state, column, row):
+    levels = state.shape[0]
+    pitch = column.shape[0] // levels
+    here = pl.ds(pl.multiple_of(row * LANES, LANES), LANES)
+    for level in range(0, levels, 8):
+        at = level * pitch + PAD + HALO + row
+        column[pl.ds(at, 8, stride=pitch), :] = state[level : level + 8, here]
+
+
+def build_kernel(state, coef, offset, matrix, mix, column, wide, spots, highs, lows):
+    chunk = pl.program_id(0)
+    chunks = pl.num_programs(0)
+    levels = state.shape[0]
+    rows = state.shape[1] // LANES
+    total = rows + 2 * HALO
+
+    @pl.when(chunk == 0)
+    def _():
+        @pl.loop(0, rows, unroll=8)
+        def _(row):
+            state_rows(state, column, row)
+
+        @pl.loop(0, rows, unroll=8)
+        def _(row):
+            to_lanes(levels, column, wide, row + HALO)
+
+    by_matrix, by_gather = group_rows(chunk, chunks)
+    here = pl.ds(pl.multiple_of(by_matrix - HALO, GROUP), GROUP)
+    spot = [spots_of(offset[which, here, :]) for which in range(NB)]
+    factor = [coef[which, here, :] for which in range(NB)]
+    for which in range(NB):
+        spots[which] = spot[which]
+        joint = factor[which]
+        for other in range(NB):
+            if other != which:
+                joint = joint + jnp.where(spot[other] == spot[which], factor[other], 0.0)
+        high = joint.astype(BF16).astype(F32)
+        highs[which] = high
+        lows[which] = joint - high
+
+    small = jnp.int16
+
+    @pl.loop(0, GROUP, unroll=8)
+    def _(tile):
+        def wide_row(ref, kind):
+            return [
+                jnp.broadcast_to(ref[which, pl.ds(tile, 1), :], (16, LANES)).astype(kind)
+                for which in range(NB)
+            ]
+
+        spot_rows, high_rows, low_rows = (
+            wide_row(spots, small),
+            wide_row(highs, BF16),
+            wide_row(lows, BF16),
+        )
+        count = lax.broadcasted_iota(jnp.int32, (16, LANES), 0).astype(small)
+        for first in range(0, WINDOW * LANES, 16):
+            key = count + small(first)
+            by_high = jnp.zeros((16, LANES), BF16)
+            by_low = jnp.zeros((16, LANES), BF16)
+            for which in range(NB):
+                hit = spot_rows[which] == key
+                by_high = jnp.where(hit, high_rows[which], by_high)
+                by_low = jnp.where(hit, low_rows[which], by_low)
+            matrix[tile, first : first + 16, 0:LANES] = by_high
+            matrix[tile, first : first + 16, LANES : 2 * LANES] = by_low
+
+    for tile in range(GROUP):
+        parts = [matrix.at[:, pl.ds(reach * LANES, LANES), :] for reach in range(WINDOW)]
+        spread_tile(levels, total, wide, parts, tile, by_matrix + tile, mix)
+
+    @pl.when((chunk > 0) & (chunk < chunks - 1))
+    def _():
+        near = pl.ds(pl.multiple_of(by_gather - HALO, GROUP), GROUP)
+
+        def terms(which):
+            spot = spots_of(offset[which, near, :])
+            return lane_of(spot), code_of(spot), coef[which, near, :]
+
+        spread_group(levels, total, column, by_gather, terms, mix)
+
+
+def build(state, coef, offset):
+    levels, cells = state.shape
+    rows = cells // LANES
+    total = rows + 2 * HALO
+    pitch = total + 2 * PAD
+    chunks = total // CHUNK
     span = WINDOW * LANES
-
-    @pl.loop(0, total // CHUNK)
-    def _(chunk):
-        base = pl.multiple_of(chunk * CHUNK, 8)
-        for tile in range(CHUNK - 8):
-            row = base + tile
-            at = pl.multiple_of((row + PAD - REACH) * LANES, LANES)
-            entry = chunk * (CHUNK - 8) + tile
-            got = jnp.dot(
-                wide[:, pl.ds(at, span)],
-                jnp.concatenate([part[entry] for part in matrix], axis=0),
-                preferred_element_type=F32,
-            )
-            got = got[:, :LANES] + got[:, LANES:]
-            got = got[:levels] + got[levels:]
-            for level in range(0, levels, 8):
-                mix[pl.ds(level * total + row, 8, stride=total), :] = got[level : level + 8]
-        row = base + CHUNK - 8
-        here = pl.ds(row, 8)
-        right = [None] * levels
-        for which in range(NB):
-            index = lanes[which, here, :]
-            code = codes[which, here, :]
-            factor = coefs[which, here, :]
-            for level in range(levels):
-                found = None
-                for reach in range(WINDOW):
-                    at = level * pitch + PAD - REACH + reach + row
-                    picked = lane_pick(column[pl.ds(at, 8), :], index)
-                    found = picked if found is None else jnp.where(code == reach, picked, found)
-                found = factor * found
-                right[level] = found if which == 0 else right[level] + found
-        for level in range(levels):
-            mix[pl.ds(level * total + row, 8), :] = right[level]
+    return pl.pallas_call(
+        build_kernel,
+        grid=(chunks,),
+        in_specs=[
+            pl.BlockSpec(state.shape, lambda i: (0, 0)),
+            pl.BlockSpec(coef.shape, lambda i: (0, 0, 0)),
+            pl.BlockSpec(offset.shape, lambda i: (0, 0, 0)),
+        ],
+        out_specs=[
+            pl.BlockSpec((GROUP, span, 2 * LANES), lambda i: (i, 0, 0)),
+            pl.BlockSpec((levels * total, LANES), lambda i: (0, 0)),
+        ],
+        out_shape=[
+            jax.ShapeDtypeStruct((chunks * GROUP, span, 2 * LANES), BF16),
+            jax.ShapeDtypeStruct((levels * total, LANES), F32),
+        ],
+        scratch_shapes=[
+            pltpu.VMEM((levels * pitch, LANES), F32),
+            pltpu.VMEM((2 * levels, pitch * LANES), BF16),
+            pltpu.VMEM((NB, GROUP, LANES), jnp.int32),
+            pltpu.VMEM((NB, GROUP, LANES), F32),
+            pltpu.VMEM((NB, GROUP, LANES), F32),
+        ],
+        compiler_params=pltpu.CompilerParams(vmem_limit_bytes=56 * MIB),
+        cost_estimate=pl.CostEstimate(
+            flops=2 * chunks * GROUP * 2 * levels * span * 2 * LANES,
+            bytes_accessed=80 * MIB,
+            transcendentals=0,
+        ),
+        name="build",
+    )(state, coef, offset)
 
 
 def prepare_kernel(
-    state, coef, offset, vert, wet, low, high,
-    column, mix, inv, from_up, from_down, lanes, codes, coefs, keep, wets,
-    *refs,
+    state, coef, offset, vert, wet, low, high, matrix_far, mix_far,
+    column, mix, inv, from_up, from_down, lanes, codes, coefs, keep, wets, *refs
 ):
-    matrix, (wide, places, merged, verts) = refs[:WINDOW], refs[WINDOW:]
+    matrix, (verts, copied, mixed) = refs[:WINDOW], refs[WINDOW:]
     levels = state.shape[0]
     rows = state.shape[1] // LANES
     total = rows + 2 * HALO
     pitch = column.shape[0] // levels
     inner = levels - 1
+
+    mix_copy = pltpu.make_async_copy(mix_far, mix, mixed)
+    mix_copy.start()
+    matrix_copies = [
+        pltpu.make_async_copy(
+            matrix_far.at[:, pl.ds(reach * LANES, LANES), :], matrix[reach], copied.at[reach]
+        )
+        for reach in range(WINDOW)
+    ]
+    for copy in matrix_copies:
+        copy.start()
 
     for pack, first in ((low, 0), (high, total - HALO)):
         for level in range(levels):
@@ -251,48 +390,35 @@
             column[at : at + HALO, :] = pack[level * HALO : (level + 1) * HALO, :]
         here = slice(first, first + HALO)
         at = levels * HALO
-        for out, count in ((coefs, NB), (places, NB), (verts, inner)):
+        for out, count in ((coefs, NB), (lanes, NB), (verts, inner)):
             for index in range(count):
                 out[index, here, :] = pack[at : at + HALO, :].astype(out.dtype)
                 at += HALO
         wets[here, :] = pack[at : at + HALO, :] * force_scale
     main = slice(HALO, HALO + rows)
     coefs[:, main, :] = coef[...]
-    places[:, main, :] = offset[...]
+    lanes[:, main, :] = offset[...]
     verts[:, main, :] = vert[...]
     wets[main, :] = wet[...].astype(F32) * force_scale
 
     @pl.loop(0, rows, unroll=8)
     def _(row):
-        here = pl.ds(pl.multiple_of(row * LANES, LANES), LANES)
-        for level in range(0, levels, 8):
-            at = level * pitch + PAD + HALO + row
-            column[pl.ds(at, 8, stride=pitch), :] = state[level : level + 8, here]
-
-    to_lanes(levels, total, column, wide)
-    lane = lax.broadcasted_iota(jnp.int32, (8, LANES), 1)
-
-    @pl.loop(0, total // 8)
+        state_rows(state, column, row)
+
+    @pl.loop(0, total // GROUP)
     def _(group):
-        here = pl.ds(pl.multiple_of(group * 8, 8), 8)
-        spots = [places[which, here, :] + lane + RIM for which in range(NB)]
-        factors = [coefs[which, here, :] for which in range(NB)]
+        here = pl.ds(pl.multiple_of(group * GROUP, GROUP), GROUP)
         left = 1.0
         for which in range(NB):
-            places[which, here, :] = spots[which]
-            lanes[which, here, :] = jnp.bitwise_and(spots[which], LANES - 1)
-            codes[which, here, :] = lax.shift_right_logical(spots[which], 7)
-            left = left - factors[which]
-            joint = factors[which]
-            for other in range(NB):
-                if other != which:
-                    joint = joint + jnp.where(spots[other] == spots[which], factors[other], 0.0)
-            merged[which, here, :] = joint
+            spot = spots_of(lanes[which, here, :])
+            lanes[which, here, :] = lane_of(spot)
+            codes[which, here, :] = code_of(spot)
+            left = left - coefs[which, here, :]
         keep[here, :] = left
-        upper = jnp.zeros((8, LANES), F32)
-        carried = jnp.zeros((8, LANES), F32)
+        upper = jnp.zeros((GROUP, LANES), F32)
+        carried = jnp.zeros((GROUP, LANES), F32)
         for level in range(levels):
-            lower = verts[level, here, :] if level < inner else jnp.zeros((8, LANES), F32)
+            lower = verts[level, here, :] if level < inner else jnp.zeros((GROUP, LANES), F32)
             pivot = (1.0 + upper + lower) - upper * carried
             inverse = 1.0 / pivot
             carried = lower * inverse
@@ -301,53 +427,37 @@
             from_down[level, here, :] = carried
             upper = lower
 
-    span = WINDOW * LANES
-    small = jnp.int16
-
-    @pl.loop(0, total // CHUNK)
-    def _(chunk):
-        @pl.loop(0, CHUNK - 8)
-        def _(tile):
-            row = chunk * CHUNK + tile
-            at = chunk * (CHUNK - 8) + tile
-            spots, highs, lows = [], [], []
-            for which in range(NB):
-                spot = places[which, pl.ds(row, 1), :]
-                spots.append(jnp.broadcast_to(spot, (16, LANES)).astype(small))
-                joint_high, joint_low = split(
-                    jnp.broadcast_to(merged[which, pl.ds(row, 1), :], (16, LANES))
-                )
-                highs.append(joint_high)
-                lows.append(joint_low)
-            count = lax.broadcasted_iota(jnp.int32, (16, LANES), 0)
-            for first in range(0, span, 16):
-                key = (count + first).astype(small)
-                by_high = jnp.zeros((16, LANES), BF16)
-                by_low = jnp.zeros((16, LANES), BF16)
-                for which in range(NB):
-                    hit = spots[which] == key
-                    by_high = jnp.where(hit, highs[which], by_high)
-                    by_low = jnp.where(hit, lows[which], by_low)
-                part, inside = matrix[first // LANES], first % LANES
-                part[at, inside : inside + 16, 0:LANES] = by_high
-                part[at, inside : inside + 16, LANES : 2 * LANES] = by_low
-
-    spread(levels, total, column, wide, matrix, lanes, codes, coefs, mix)
-
-
-def prepare(state, coef, offset, vert, wet, low, high):
+    mix_copy.wait()
+
+    @pl.loop(0, 4)
+    def _(which_group):
+        far = (which_group >= 2).astype(jnp.int32)
+        row = pl.multiple_of(which_group * GROUP + far * (total - 4 * GROUP), GROUP)
+        here = pl.ds(row, GROUP)
+
+        def terms(which):
+            return lanes[which, here, :], codes[which, here, :], coefs[which, here, :]
+
+        spread_group(levels, total, column, row, terms, mix)
+
+    for copy in matrix_copies:
+        copy.wait()
+
+
+def prepare(state, coef, offset, vert, wet, low, high, matrix, mix):
     levels, cells = state.shape
     rows = cells // LANES
     total = rows + 2 * HALO
     pitch = total + 2 * PAD
-    tiles = total // CHUNK * (CHUNK - 8)
     level_shape = pltpu.VMEM((levels, total, LANES), F32)
     index_shape = pltpu.VMEM((NB, total, LANES), jnp.int32)
+    near = pl.BlockSpec(memory_space=pltpu.VMEM)
+    far = pl.BlockSpec(memory_space=pltpu.HBM)
     return pl.pallas_call(
         prepare_kernel,
         out_shape=[
             pltpu.VMEM((levels * pitch, LANES), F32),
-            pltpu.VMEM((levels * total, LANES), F32),
+            pltpu.VMEM(mix.shape, F32),
             level_shape,
             level_shape,
             level_shape,
@@ -356,34 +466,33 @@
             pltpu.VMEM((NB, total, LANES), F32),
             pltpu.VMEM((total, LANES), F32),
             pltpu.VMEM((total, LANES), F32),
-            *[pltpu.VMEM((tiles, LANES, 2 * LANES), BF16)] * WINDOW,
-        ],
-        in_specs=[pl.BlockSpec(memory_space=pltpu.VMEM)] * 7,
-        out_specs=[pl.BlockSpec(memory_space=pltpu.VMEM)] * (10 + WINDOW),
+            *[pltpu.VMEM((matrix.shape[0], LANES, 2 * LANES), BF16)] * WINDOW,
+        ],
+        in_specs=[near] * 7 + [far] * 2,
+        out_specs=[near] * (10 + WINDOW),
         scratch_shapes=[
-            pltpu.VMEM((2 * levels, pitch * LANES), BF16),
-            pltpu.VMEM((NB, total, LANES), jnp.int32),
-            pltpu.VMEM((NB, total, LANES), F32),
             pltpu.VMEM((levels - 1, total, LANES), F32),
-        ],
-        compiler_params=pltpu.CompilerParams(vmem_limit_bytes=8 * MIB),
+            pltpu.SemaphoreType.DMA((WINDOW,)),
+            pltpu.SemaphoreType.DMA,
+        ],
+        compiler_params=pltpu.CompilerParams(vmem_limit_bytes=12 * MIB),
         cost_estimate=pl.CostEstimate(
-            flops=2 * tiles * 8 * levels * WINDOW * LANES * LANES,
-            bytes_accessed=80 * MIB,
-            transcendentals=0,
+            flops=0, bytes_accessed=40 * MIB, transcendentals=0
         ),
         name="prepare",
-    )(state, coef, offset, vert, wet, low, high)
+    )(state, coef, offset, vert, wet, low, high, matrix, mix)
 
 
 def interval_kernel(
     width, column, mix, inv, from_up, from_down, lanes, codes, coefs, keep, wets, *refs
 ):
     matrix, refs = refs[:WINDOW], refs[WINDOW:]
-    imported, low, high, state_out, imported_out, first, second, mixed, wide, force, flat = refs
+    imported, low, high, state_out, imported_out, *refs = refs
+    cells, mixed, wide, force, flat = refs
     levels, total = inv.shape[0], inv.shape[1]
     rows = total - 2 * HALO
     pitch = column.shape[0] // levels
+    chunks = total // CHUNK
 
     force[:, 0:HALO, :] = low[...]
     force[:, HALO : HALO + rows, :] = imported[...]
@@ -396,17 +505,16 @@
         here = pl.ds(pl.multiple_of(row * LANES, LANES), LANES)
         imported_out[:, here] = flat[pl.ds(row, width, stride=rows), :]
 
-    def solve(source, spread_sum, out):
-        @pl.loop(0, total // 8)
-        def _(group):
-            row = pl.multiple_of(group * 8, 8)
-            here = pl.ds(row, 8)
+    def solve(chunk, source, spread_sum, out, wide):
+        for group in range(CHUNK // GROUP):
+            row = pl.multiple_of(chunk * CHUNK + group * GROUP, GROUP)
+            here = pl.ds(row, GROUP)
             left = keep[here, :]
             wet = wets[here, :]
             partial = []
             for level in range(levels):
-                value = left * source[pl.ds(level * pitch + PAD + row, 8), :]
-                value = value + spread_sum[pl.ds(level * total + row, 8), :]
+                value = left * source[pl.ds(level * pitch + PAD + row, GROUP), :]
+                value = value + spread_sum[pl.ds(level * total + row, GROUP), :]
                 if level < width:
                     value = value + force[level, here, :] * wet
                 value = value * inv[level, here, :]
@@ -414,27 +522,43 @@
                     value = value + from_up[level, here, :] * partial[-1]
                 partial.append(value)
             following = partial[-1]
-            out[pl.ds((levels - 1) * pitch + PAD + row, 8), :] = following
+            out[pl.ds((levels - 1) * pitch + PAD + row, GROUP), :] = following
             for level in range(levels - 2, -1, -1):
                 following = partial[level] + from_down[level, here, :] * following
-                out[pl.ds(level * pitch + PAD + row, 8), :] = following
-
-    buffers = (first, second)
-    solve(column, mix, first)
-    for step in range(1, STEPS):
-        source, out = buffers[(step - 1) % 2], buffers[step % 2]
-        to_lanes(levels, total, source, wide)
-        spread(levels, total, source, wide, matrix, lanes, codes, coefs, mixed)
-        solve(source, mixed, out)
-
-    last = buffers[(STEPS - 1) % 2]
+                out[pl.ds(level * pitch + PAD + row, GROUP), :] = following
+        for row in range(CHUNK):
+            to_lanes(levels, out, wide, chunk * CHUNK + row)
+
+    def spread(chunk, source, wide):
+        by_matrix, by_gather = group_rows(chunk, chunks)
+        for tile in range(GROUP):
+            spread_tile(
+                levels, total, wide, matrix, chunk * GROUP + tile, by_matrix + tile, mixed
+            )
+        here = pl.ds(by_gather, GROUP)
+
+        def terms(which):
+            return lanes[which, here, :], codes[which, here, :], coefs[which, here, :]
+
+        spread_group(levels, total, source, by_gather, terms, mixed)
+
+    @pl.loop(0, chunks)
+    def _(chunk):
+        solve(chunk, column, mix, cells, wide)
+
+    @pl.loop(1, STEPS)
+    def _(step):
+        for chunk in range(chunks):
+            spread(jnp.int32(chunk), cells, wide)
+        for chunk in range(chunks):
+            solve(chunk, cells, mixed, cells, wide)
 
     @pl.loop(0, rows, unroll=8)
     def _(row):
         here = pl.ds(pl.multiple_of(row * LANES, LANES), LANES)
         for level in range(0, levels, 8):
             at = level * pitch + PAD + HALO + row
-            state_out[level : level + 8, here] = last[pl.ds(at, 8, stride=pitch), :]
+            state_out[level : level + 8, here] = cells[pl.ds(at, 8, stride=pitch), :]
 
 
 def interval(column, mix, inv, *rest):
@@ -452,13 +576,12 @@
         out_specs=[pl.BlockSpec(memory_space=pltpu.VMEM)] * 2,
         scratch_shapes=[
             pltpu.VMEM(column.shape, F32),
-            pltpu.VMEM(column.shape, F32),
             pltpu.VMEM(mix.shape, F32),
             pltpu.VMEM((2 * levels, pitch * LANES), BF16),
             pltpu.VMEM((width, total, LANES), F32),
             pltpu.VMEM((width * rows, LANES), F32),
         ],
-        compiler_params=pltpu.CompilerParams(vmem_limit_bytes=10 * MIB),
+        compiler_params=pltpu.CompilerParams(vmem_limit_bytes=12 * MIB),
         name="interval",
     )(*operands)
 
@@ -506,8 +629,8 @@
     backward = [(target, source) for source, target in forward]
     low = lax.ppermute(low, "dom", forward)
     high = lax.ppermute(high, "dom", backward)
-    prepared = prepare(state[0], coef, offset, vert, wet, low, high)
-    values, prepared = lax.optimization_barrier((values, prepared))
+    matrix, mix = build(state[0], coef, offset)
+    values, matrix, mix, low, high = lax.optimization_barrier((values, matrix, mix, low, high))
 
     pitch = capacity * width + 8
     summed, first_rows, last_rows = assemble(
@@ -525,6 +648,7 @@
     imported = across(summed, 0)
     from_low = across(last_rows, 1)
     from_high = across(first_rows, -1)
+    prepared = prepare(state[0], coef, offset, vert, wet, low, high, matrix, mix)
     new_state, imported = interval(*prepared, imported, from_low, from_high)
     return (new_state[None], imported[None])
 

time: 159 us -> 89.6 us (0.56); the launches traced: 157 us -> 89.1 us
  local copies, waits for them, and re-layouts: 47 us -> 5.3 us
  waiting for transfers between devices: 24.5 us -> 0.02 us
    unnamed x70 -> x20, local copies, waits for them, and re-layouts: 47 us -> 5.3 us
    pallas_call x0 -> x1, Pallas kernels: none -> 23.3 us  [build(): pl.pallas_call(build_kernel, grid=(chunks,), in_specs=[pl.BlockSpec(state...]
    ppermute x1, waiting for transfers between devices: 21.5 us -> 0.01 us  [local(): low = lax.ppermute(low, 'dom', forward)]
    pallas_call x1, Pallas kernels: 25.3 us -> 8.09 us  [prepare(): pl.pallas_call(prepare_kernel, out_shape=[pltpu.VMEM((levels * pitch, LAN...]
    pallas_call x1, Pallas kernels: 30.5 us -> 23 us  [interval(): pl.pallas_call(functools.partial(interval_kernel, width), out_shape=[jax....]
    ppermute x3, waiting for transfers between devices: 3.05 us -> 0.01 us  [across(): return lax.ppermute(value, ('comp', 'dom'), pairs)]
  transfers between devices with their start and end apart: 6 -> 6, of which waited for: 3 -> 0; matrix products, arithmetic and copies ran while one was open for 0% -> 0% of each run, Pallas kernels for 16% -> 35%
where the time goes in v3:
time: 89.6 us; the launch traced here: 89.1 us
  Pallas kernels  64.3 us (72%)
  starting transfers between devices  18.8 us (21%)
  local copies, waits for them, and re-layouts  5.3 us (6%)
    pallas_call x1, Pallas kernels, build(): pl.pallas_call(build_kernel, grid=(chunks,), in_specs=[pl.BlockSpec(state...  23.3 us
    pallas_call x1, Pallas kernels, interval(): pl.pallas_call(functools.partial(interval_kernel, width), out_shape=[jax....  23 us
    pallas_call x1, Pallas kernels, remap(): pl.pallas_call(functools.partial(remap_kernel, owners, capacity), grid_sp...  9.44 us
    pallas_call x1, Pallas kernels, prepare(): pl.pallas_call(prepare_kernel, out_shape=[pltpu.VMEM((levels * pitch, LAN...  8.09 us
    all_to_all x1, starting transfers between devices, local(): lax.all_to_all(values, 'dom', split_axis=0, concat_axis=0, tiled=True)  7.39 us
    ppermute x3, starting transfers between devices, across(): return lax.ppermute(value, ('comp', 'dom'), pairs)  6.9 us
    unnamed x20, local copies, waits for them, and re-layouts  5.3 us
    ppermute x1, starting transfers between devices, local(): high = lax.ppermute(high, 'dom', backward)  4.08 us
  transfers between devices with their start and end apart: 6, of which 0 were waited for; matrix products, arithmetic and copies ran while one was open for 0% of the time, Pallas kernels for 35%

profile of v3, /device:TPU:0, one launch (start us, length us, event | category | flops | bytes accessed | tf_op | source)
XLA Modules:
  0.0 89.1 jit_solution(8043207549540632575)
XLA Ops:
  0.6 9.4 %remap.1 = (f32[16,136,128]{2,1,0:T(8,128)}, f32[352,128]{1,0:T(8,128)}, f32[352,128]{1,0:T(8,128)}) custom-call(s32[128]{0:T(128)} %bitcast.35, s32[128]{0:T(128)} %bitcast.36, s32[128]{0:T(128)} %bitcast.37, s32[1]{0:T(128)} %bitcast.8.me, f32[8,16384]{1,0:T(8,128)} %bitcast.34, f32[128,128,128]{2,1,0:T(8,128)} %bitcast.33, f32[16,16384]{1,0:T(8,128)} %bitcast.14, ...), custom_call_target="tpu_custom_call" | custom-call | tf_op jit(solution)/shard_map/remap/pallas_call | solution.py:106
  10.1 7.4 %all-to-all-start = ((f32[16,136,128]{2,1,0:T(8,128)}), f32[16,136,128]{2,1,0:T(8,128)S(1)}, u32[]{:S(2)}, u32[]{:S(2)}) async-start(f32[16,136,128]{2,1,0:T(8,128)} %get-tuple-element.32), calls=%async_computation | async-start | bytes 2228224 | tf_op jit(solution)/shard_map/all_to_all | solution.py:626
  17.5 0.4 collective-permute-start
  17.9 0.0 copy-start
  17.9 0.0 copy-start.1
  17.9 0.0 copy-start.2
  17.9 4.1 %collective-permute-start.1 = (f32[352,128]{1,0:T(8,128)}, f32[352,128]{1,0:T(8,128)S(1)}, u32[]{:S(2)}, u32[]{:S(2)}) collective-permute-start(f32[352,128]{1,0:T(8,128)} %get-tuple-element.36), channel_id=1, source_target_pairs={{1,0},{2,1},{3,2},{4,3},{5,4},{6,5},{7,6},{8,7},{9,8},{10,9},{11,1... | collective-permute-start | bytes 540680 | tf_op jit(solution)/shard_map/ppermute | solution.py:631
  22.0 23.3 %build.1 = (bf16[72,640,256]{2,1,0:T(8,128)(2,1)}, f32[2304,128]{1,0:T(8,128)}) custom-call(f32[16,16384]{1,0:T(8,128)} %bitcast.16, f32[6,128,128]{2,1,0:T(8,128)} %bitcast.24, s32[6,128,128]{2,1,0:T(8,128)} %bitcast.28), custom_call_target="tpu_custom_call" | custom-call | flops 754974720 | bytes 83886080 | tf_op jit(solution)/shard_map/build/pallas_call | solution.py:332
  45.2 0.0 collective-permute-done.low
  45.2 0.0 copy-start.6
  45.2 0.7 copy-done.6
  45.9 0.0 collective-permute-done.1.high
  45.9 0.0 copy-start.8
  45.9 0.7 copy-done.8
  46.6 0.0 all-to-all-done
  46.6 0.0 copy-start.3
  46.6 0.4 assemble.1
  47.0 1.6 %collective-permute-start.2 = (f32[8,128,128]{2,1,0:T(8,128)S(1)}, f32[8,128,128]{2,1,0:T(8,128)S(1)}, u32[]{:S(2)}, u32[]{:S(2)}) collective-permute-start(f32[8,128,128]{2,1,0:T(8,128)S(1)} %get-tuple-element.57), channel_id=1, source_target_pairs={{0,16},{1,17},{2,18},{3,19},{4,20},{5,21},{6,22},{7,23},{8,24},{9,... | collective-permute-start | bytes 1572872 | tf_op jit(solution)/shard_map/ppermute | solution.py:646
  48.6 0.0 collective-permute-start.3
  48.6 5.3 %collective-permute-start.4 = (f32[8,8,128]{2,1,0:T(8,128)S(1)}, f32[8,8,128]{2,1,0:T(8,128)S(1)}, u32[]{:S(2)}, u32[]{:S(2)}) collective-permute-start(f32[8,8,128]{2,1,0:T(8,128)S(1)} %get-tuple-element.59), channel_id=1, source_target_pairs={{0,31},{1,16},{2,17},{3,18},{4,19},{5,20},{6,21},{7,22},{8,23},{9,... | collective-permute-start | bytes 98312 | tf_op jit(solution)/shard_map/ppermute | solution.py:646
  53.9 0.0 copy-done
  53.9 0.0 copy-done.1
  53.9 0.0 copy-done.2
  53.9 0.0 copy-done.3
  54.0 0.0 copy-start.4
  54.0 1.3 %copy-done.4 = f32[2304,128]{1,0:T(8,128)S(1)} copy-done((f32[2304,128]{1,0:T(8,128)S(1)}, f32[2304,128]{1,0:T(8,128)}, u32[]{:S(2)}) %copy-start.4) | copy-done | bytes 1179672
  55.2 0.0 copy-start.5
  55.2 0.8 copy-done.5
  56.1 0.0 copy-start.7
  56.1 0.9 %copy-done.7 = f32[352,128]{1,0:T(8,128)S(1)} copy-done((f32[352,128]{1,0:T(8,128)S(1)}, f32[352,128]{1,0:T(8,128)}, u32[]{:S(2)}) %copy-start.7) | copy-done | bytes 180248
  57.0 0.0 copy-start.9
  57.0 0.9 %copy-done.9 = f32[352,128]{1,0:T(8,128)S(1)} copy-done((f32[352,128]{1,0:T(8,128)S(1)}, f32[352,128]{1,0:T(8,128)}, u32[]{:S(2)}) %copy-start.9) | copy-done | bytes 180248
  57.9 8.1 %prepare.1 = (f32[2560,128]{1,0:T(8,128)S(1)}, f32[2304,128]{1,0:T(8,128)S(1)}, f32[16,144,128]{2,1,0:T(8,128)S(1)}, f32[16,144,128]{2,1,0:T(8,128)S(1)}, f32[16...) custom-call(f32[16,16384]{1,0:T(8,128)S(1)} %bitcast.17, ...), custom_call_target="tpu_custom_call" | custom-call | bytes 41943040 | tf_op jit(solution)/shard_map/prepare/pallas_call | solution.py:456
  66.0 0.0 collective-permute-done.3.refs_6_
  66.0 0.0 collective-permute-done.4.refs_7_
  66.0 0.0 collective-permute-done.2.refs_5_
  66.0 23.0 %interval.1 = (f32[16,16384]{1,0:T(8,128)}, f32[8,16384]{1,0:T(8,128)}) custom-call(f32[2560,128]{1,0:T(8,128)S(1)} %get-tuple-element.41.column, f32[2304,128]{1,0:T(8,128)S(1)} %get-tuple-element.42.mix, f32[16,144,128]{2,1,0:T(8,128)S(1)} %get-tuple-element.43.inv, f32[16,144,128]{2,1,0:T(8,128)S(1)} %get-tuple-element.44.from_up, ...), custom_call_target="tpu_custom_call" | custom-call | tf_op jit(solution)/shard_map/interval/pallas_call | solution.py:569
Async XLA Ops:
  10.1 36.5 %all-to-all-start = ((f32[16,136,128]{2,1,0:T(8,128)}), f32[16,136,128]{2,1,0:T(8,128)S(1)}, u32[]{:S(2)}, u32[]{:S(2)}) async-start(f32[16,136,128]{2,1,0:T(8,128)} %get-tuple-element.32), calls=%async_computation | async-start | bytes 2228224 | tf_op jit(solution)/shard_map/all_to_all | solution.py:626
  17.5 27.8 %collective-permute-start = (f32[352,128]{1,0:T(8,128)}, f32[352,128]{1,0:T(8,128)S(1)}, u32[]{:S(2)}, u32[]{:S(2)}) collective-permute-start(f32[352,128]{1,0:T(8,128)} %get-tuple-element.35), channel_id=1, source_target_pairs={{0,1},{1,2},{2,3},{3,4},{4,5},{5,6},{6,7},{7,8},{8,9},{9,10},{10,1... | collective-permute-start | bytes 540680 | tf_op jit(solution)/shard_map/ppermute | solution.py:630
  17.9 36.1 %copy-start = (f32[1,16,16384]{2,1,0:T(8,128)S(1)}, f32[1,16,16384]{2,1,0:T(8,128)}, u32[]{:S(2)}) copy-start(f32[1,16,16384]{2,1,0:T(8,128)} %param.10) | copy-start | bytes 3145732
  17.9 36.1 %copy-start.1 = (f32[1,15,16384]{2,0,1:T(1,128)S(1)}, f32[1,15,16384]{2,0,1:T(1,128)}, u32[]{:S(2)}) copy-start(f32[1,15,16384]{2,0,1:T(1,128)} %param.19) | copy-start | bytes 2949124
  17.9 36.1 %copy-start.2 = (f32[1,6,16384]{2,0,1:T(1,128)S(1)}, f32[1,6,16384]{2,0,1:T(1,128)}, u32[]{:S(2)}) copy-start(f32[1,6,16384]{2,0,1:T(1,128)} %param.17) | copy-start | bytes 1179652
  17.9 28.0 %collective-permute-start.1 = (f32[352,128]{1,0:T(8,128)}, f32[352,128]{1,0:T(8,128)S(1)}, u32[]{:S(2)}, u32[]{:S(2)}) collective-permute-start(f32[352,128]{1,0:T(8,128)} %get-tuple-element.36), channel_id=1, source_target_pairs={{1,0},{2,1},{3,2},{4,3},{5,4},{6,5},{7,6},{8,7},{9,8},{10,9},{11,1... | collective-permute-start | bytes 540680 | tf_op jit(solution)/shard_map/ppermute | solution.py:631
  45.2 0.7 copy-start.6
  45.9 0.7 copy-start.8
  46.6 7.4 %copy-start.3 = (s32[1,6,16384]{2,0,1:T(1,128)S(1)}, s32[1,6,16384]{2,0,1:T(1,128)}, u32[]{:S(2)}) copy-start(s32[1,6,16384]{2,0,1:T(1,128)} %param.18) | copy-start | bytes 1179652
  47.0 19.0 %collective-permute-start.2 = (f32[8,128,128]{2,1,0:T(8,128)S(1)}, f32[8,128,128]{2,1,0:T(8,128)S(1)}, u32[]{:S(2)}, u32[]{:S(2)}) collective-permute-start(f32[8,128,128]{2,1,0:T(8,128)S(1)} %get-tuple-element.57), channel_id=1, source_target_pairs={{0,16},{1,17},{2,18},{3,19},{4,20},{5,21},{6,22},{7,23},{8,24},{9,... | collective-permute-start | bytes 1572872 | tf_op jit(solution)/shard_map/ppermute | solution.py:646
  48.6 17.4 %collective-permute-start.3 = (f32[8,8,128]{2,1,0:T(8,128)S(1)}, f32[8,8,128]{2,1,0:T(8,128)S(1)}, u32[]{:S(2)}, u32[]{:S(2)}) collective-permute-start(f32[8,8,128]{2,1,0:T(8,128)S(1)} %get-tuple-element.58), channel_id=1, source_target_pairs={{0,17},{1,18},{2,19},{3,20},{4,21},{5,22},{6,23},{7,24},{8,25},{9,... | collective-permute-start | bytes 98312 | tf_op jit(solution)/shard_map/ppermute | solution.py:646
  48.6 17.4 %collective-permute-start.4 = (f32[8,8,128]{2,1,0:T(8,128)S(1)}, f32[8,8,128]{2,1,0:T(8,128)S(1)}, u32[]{:S(2)}, u32[]{:S(2)}) collective-permute-start(f32[8,8,128]{2,1,0:T(8,128)S(1)} %get-tuple-element.59), channel_id=1, source_target_pairs={{0,31},{1,16},{2,17},{3,18},{4,19},{5,20},{6,21},{7,22},{8,23},{9,... | collective-permute-start | bytes 98312 | tf_op jit(solution)/shard_map/ppermute | solution.py:646
  54.0 1.3 %copy-start.4 = (f32[2304,128]{1,0:T(8,128)S(1)}, f32[2304,128]{1,0:T(8,128)}, u32[]{:S(2)}) copy-start(f32[2304,128]{1,0:T(8,128)} %get-tuple-element.40.mix_far) | copy-start | bytes 3538948
  55.2 0.8 copy-start.5
  56.1 0.9 %copy-start.7 = (f32[352,128]{1,0:T(8,128)S(1)}, f32[352,128]{1,0:T(8,128)}, u32[]{:S(2)}) copy-start(f32[352,128]{1,0:T(8,128)} %copy-done.6) | copy-start | bytes 540676
  57.0 0.9 %copy-start.9 = (f32[352,128]{1,0:T(8,128)S(1)}, f32[352,128]{1,0:T(8,128)}, u32[]{:S(2)}) copy-start(f32[352,128]{1,0:T(8,128)} %copy-done.8) | copy-start | bytes 540676

commit v4 on v3

--- a/solution.py
+++ b/solution.py
@@ -33,7 +33,7 @@
 def remap_kernel(
     owners, capacity, routes, target, source, me, fields, weights, *refs
 ):
-    edges, (out, low, high, counts) = refs[:10], refs[10:]
+    edges, (out, low, high, counts, marks) = refs[:10], refs[10:]
     step = pl.program_id(0)
     per_step = weights.shape[0]
     width = fields.shape[0]
@@ -43,6 +43,7 @@
     @pl.when(step == 0)
     def _():
         out[...] = jnp.zeros_like(out)
+        marks[...] = jnp.zeros_like(marks)
         for owner in range(owners):
             counts[owner] = 0
         for side, pack in ((0, low), (1, high)):
@@ -67,17 +68,21 @@
         start = pl.multiple_of(source[block] * LANES, LANES)
         picked_high, picked_low = split(fields[:, pl.ds(start, LANES)])
         picked = jnp.concatenate([picked_high, picked_low], axis=0)
-        high_part, low_part = split(weights[local_block])
-        by_high = jnp.dot(picked, high_part, preferred_element_type=F32)
-        by_low = jnp.dot(picked, low_part, preferred_element_type=F32)
-        value = (by_low[:width] + by_low[width:] + by_high[width:]) + by_high[:width]
+        both = jnp.concatenate(split(weights[local_block]), axis=1)
+        product = jnp.dot(picked, both, preferred_element_type=F32)
+        product = product[:, :LANES] + product[:, LANES:]
+        value = product[:width] + product[width:]
         row = pl.multiple_of(rank * width, width)
         out[owner, pl.ds(row, width), :] = value
         slot = lax.rem(me[0] * capacity + rank, LANES)
-        old = out[owner, label_row : label_row + 1, :]
-        out[owner, label_row : label_row + 1, :] = jnp.where(
-            lane == slot, (target[block] + 1).astype(F32), old
+        marks[pl.ds(owner, 1), :] = jnp.where(
+            lane == slot, (target[block] + 1).astype(F32), marks[pl.ds(owner, 1), :]
         )
+
+    @pl.when(step == pl.num_programs(0) - 1)
+    def _():
+        for owner in range(owners):
+            out[owner, label_row : label_row + 1, :] = marks[owner : owner + 1, :]
 
 
 def remap(routes, target, source, me, fields, weights, state, parts, owners, capacity):
@@ -118,7 +123,10 @@
                 pl.BlockSpec((pack_rows, LANES), lambda i, *_: (0, 0)),
                 pl.BlockSpec((pack_rows, LANES), lambda i, *_: (0, 0)),
             ],
-            scratch_shapes=[pltpu.SMEM((owners,), jnp.int32)],
+            scratch_shapes=[
+                pltpu.SMEM((owners,), jnp.int32),
+                pltpu.VMEM((owners, LANES), F32),
+            ],
         ),
         out_shape=[
             jax.ShapeDtypeStruct(slots, F32),
@@ -211,7 +219,7 @@
         mix[pl.ds(level * total + row, 8, stride=total), :] = got[level : level + 8]
 
 
-def spread_group(levels, total, column, row, terms, mix):
+def spread_group(levels, total, column, row, terms, mix, out=None, step=None):
     pitch = column.shape[0] // levels
     right = [None] * levels
     for which in range(NB):
@@ -224,8 +232,14 @@
                 found = picked if found is None else jnp.where(code == reach, picked, found)
             found = factor * found
             right[level] = found if which == 0 else right[level] + found
+    out, step = (row, total) if out is None else (out, step)
     for level in range(levels):
-        mix[pl.ds(level * total + row, GROUP), :] = right[level]
+        mix[pl.ds(level * step + out, GROUP), :] = right[level]
+
+
+def edge_row(index, total):
+    far = (index >= 2).astype(jnp.int32)
+    return pl.multiple_of(index * GROUP + far * (total - 4 * GROUP), GROUP)
 
 
 def spots_of(offset):
@@ -249,7 +263,8 @@
         column[pl.ds(at, 8, stride=pitch), :] = state[level : level + 8, here]
 
 
-def build_kernel(state, coef, offset, matrix, mix, column, wide, spots, highs, lows):
+def build_kernel(state, coef, offset, wet, mix, *refs):
+    matrix, (column, wide, spots, highs, lows) = refs[:WINDOW], refs[WINDOW:]
     chunk = pl.program_id(0)
     chunks = pl.num_programs(0)
     levels = state.shape[0]
@@ -265,6 +280,8 @@
         @pl.loop(0, rows, unroll=8)
         def _(row):
             to_lanes(levels, column, wide, row + HALO)
+
+        mix[pl.ds(levels * total + HALO, rows), :] = wet[...].astype(F32) * force_scale
 
     by_matrix, by_gather = group_rows(chunk, chunks)
     here = pl.ds(pl.multiple_of(by_matrix - HALO, GROUP), GROUP)
@@ -279,6 +296,15 @@
         high = joint.astype(BF16).astype(F32)
         highs[which] = high
         lows[which] = joint - high
+
+    inside = (chunk > 0) & (chunk < chunks - 1)
+    near = pl.ds(pl.multiple_of(jnp.where(inside, by_gather - HALO, 0), GROUP), GROUP)
+
+    def terms(which):
+        spot = spots_of(offset[which, near, :])
+        return lane_of(spot), code_of(spot), coef[which, near, :]
+
+    spread_group(levels, total, column, by_gather, terms, mix)
 
     small = jnp.int16
 
@@ -304,25 +330,15 @@
                 hit = spot_rows[which] == key
                 by_high = jnp.where(hit, high_rows[which], by_high)
                 by_low = jnp.where(hit, low_rows[which], by_low)
-            matrix[tile, first : first + 16, 0:LANES] = by_high
-            matrix[tile, first : first + 16, LANES : 2 * LANES] = by_low
+            part, at = matrix[first // LANES], first % LANES
+            part[tile, at : at + 16, 0:LANES] = by_high
+            part[tile, at : at + 16, LANES : 2 * LANES] = by_low
 
     for tile in range(GROUP):
-        parts = [matrix.at[:, pl.ds(reach * LANES, LANES), :] for reach in range(WINDOW)]
-        spread_tile(levels, total, wide, parts, tile, by_matrix + tile, mix)
-
-    @pl.when((chunk > 0) & (chunk < chunks - 1))
-    def _():
-        near = pl.ds(pl.multiple_of(by_gather - HALO, GROUP), GROUP)
-
-        def terms(which):
-            spot = spots_of(offset[which, near, :])
-            return lane_of(spot), code_of(spot), coef[which, near, :]
-
-        spread_group(levels, total, column, by_gather, terms, mix)
-
-
-def build(state, coef, offset):
+        spread_tile(levels, total, wide, matrix, tile, by_matrix + tile, mix)
+
+
+def build(state, coef, offset, wet):
     levels, cells = state.shape
     rows = cells // LANES
     total = rows + 2 * HALO
@@ -336,14 +352,15 @@
             pl.BlockSpec(state.shape, lambda i: (0, 0)),
             pl.BlockSpec(coef.shape, lambda i: (0, 0, 0)),
             pl.BlockSpec(offset.shape, lambda i: (0, 0, 0)),
+            pl.BlockSpec(wet.shape, lambda i: (0, 0)),
         ],
         out_specs=[
-            pl.BlockSpec((GROUP, span, 2 * LANES), lambda i: (i, 0, 0)),
-            pl.BlockSpec((levels * total, LANES), lambda i: (0, 0)),
+            pl.BlockSpec(((levels + 1) * total, LANES), lambda i: (0, 0)),
+            *[pl.BlockSpec((GROUP, LANES, 2 * LANES), lambda i: (i, 0, 0))] * WINDOW,
         ],
         out_shape=[
-            jax.ShapeDtypeStruct((chunks * GROUP, span, 2 * LANES), BF16),
-            jax.ShapeDtypeStruct((levels * total, LANES), F32),
+            jax.ShapeDtypeStruct(((levels + 1) * total, LANES), F32),
+            *[jax.ShapeDtypeStruct((chunks * GROUP, LANES, 2 * LANES), BF16)] * WINDOW,
         ],
         scratch_shapes=[
             pltpu.VMEM((levels * pitch, LANES), F32),
@@ -359,31 +376,45 @@
             transcendentals=0,
         ),
         name="build",
-    )(state, coef, offset)
+    )(state, coef, offset, wet)
 
 
 def prepare_kernel(
-    state, coef, offset, vert, wet, low, high, matrix_far, mix_far,
-    column, mix, inv, from_up, from_down, lanes, codes, coefs, keep, wets, *refs
+    state, coef, offset, vert, low_far, high_far, *refs
 ):
-    matrix, (verts, copied, mixed) = refs[:WINDOW], refs[WINDOW:]
+    far, (column, edge, inv, from_up, from_down, lanes, codes, coefs, keep, *refs) = (
+        refs[:WINDOW],
+        refs[WINDOW:],
+    )
+    matrix, (verts, low, high, packed, copied) = refs[:WINDOW], refs[WINDOW:]
+    pack_copies = [
+        pltpu.make_async_copy(source, target, packed.at[index])
+        for index, (source, target) in enumerate(((low_far, low), (high_far, high)))
+    ]
+    matrix_copies = [
+        pltpu.make_async_copy(far[reach], matrix[reach], copied.at[reach])
+        for reach in range(WINDOW)
+    ]
+    for copy in pack_copies + matrix_copies:
+        copy.start()
     levels = state.shape[0]
     rows = state.shape[1] // LANES
     total = rows + 2 * HALO
     pitch = column.shape[0] // levels
     inner = levels - 1
-
-    mix_copy = pltpu.make_async_copy(mix_far, mix, mixed)
-    mix_copy.start()
-    matrix_copies = [
-        pltpu.make_async_copy(
-            matrix_far.at[:, pl.ds(reach * LANES, LANES), :], matrix[reach], copied.at[reach]
-        )
-        for reach in range(WINDOW)
-    ]
-    for copy in matrix_copies:
-        copy.start()
-
+    pieces = levels * GROUP
+
+    main = slice(HALO, HALO + rows)
+    coefs[:, main, :] = coef[...]
+    lanes[:, main, :] = offset[...]
+    verts[:, main, :] = vert[...]
+
+    @pl.loop(0, rows, unroll=8)
+    def _(row):
+        state_rows(state, column, row)
+
+    for copy in pack_copies:
+        copy.wait()
     for pack, first in ((low, 0), (high, total - HALO)):
         for level in range(levels):
             at = level * pitch + PAD + first
@@ -394,16 +425,8 @@
             for index in range(count):
                 out[index, here, :] = pack[at : at + HALO, :].astype(out.dtype)
                 at += HALO
-        wets[here, :] = pack[at : at + HALO, :] * force_scale
-    main = slice(HALO, HALO + rows)
-    coefs[:, main, :] = coef[...]
-    lanes[:, main, :] = offset[...]
-    verts[:, main, :] = vert[...]
-    wets[main, :] = wet[...].astype(F32) * force_scale
-
-    @pl.loop(0, rows, unroll=8)
-    def _(row):
-        state_rows(state, column, row)
+        to = 4 * pieces + (0 if first == 0 else HALO)
+        edge[to : to + HALO, :] = pack[at : at + HALO, :] * force_scale
 
     @pl.loop(0, total // GROUP)
     def _(group):
@@ -427,24 +450,21 @@
             from_down[level, here, :] = carried
             upper = lower
 
-    mix_copy.wait()
-
     @pl.loop(0, 4)
-    def _(which_group):
-        far = (which_group >= 2).astype(jnp.int32)
-        row = pl.multiple_of(which_group * GROUP + far * (total - 4 * GROUP), GROUP)
+    def _(index):
+        row = edge_row(index, total)
         here = pl.ds(row, GROUP)
 
         def terms(which):
             return lanes[which, here, :], codes[which, here, :], coefs[which, here, :]
 
-        spread_group(levels, total, column, row, terms, mix)
+        spread_group(levels, total, column, row, terms, edge, index * pieces, GROUP)
 
     for copy in matrix_copies:
         copy.wait()
 
 
-def prepare(state, coef, offset, vert, wet, low, high, matrix, mix):
+def prepare(state, coef, offset, vert, low, high, matrix):
     levels, cells = state.shape
     rows = cells // LANES
     total = rows + 2 * HALO
@@ -453,11 +473,14 @@
     index_shape = pltpu.VMEM((NB, total, LANES), jnp.int32)
     near = pl.BlockSpec(memory_space=pltpu.VMEM)
     far = pl.BlockSpec(memory_space=pltpu.HBM)
+    low, high, *matrix = [
+        pltpu.with_memory_space_constraint(part, pltpu.HBM) for part in (low, high, *matrix)
+    ]
     return pl.pallas_call(
         prepare_kernel,
         out_shape=[
             pltpu.VMEM((levels * pitch, LANES), F32),
-            pltpu.VMEM(mix.shape, F32),
+            pltpu.VMEM((4 * levels * GROUP + 2 * HALO, LANES), F32),
             level_shape,
             level_shape,
             level_shape,
@@ -465,34 +488,44 @@
             index_shape,
             pltpu.VMEM((NB, total, LANES), F32),
             pltpu.VMEM((total, LANES), F32),
-            pltpu.VMEM((total, LANES), F32),
-            *[pltpu.VMEM((matrix.shape[0], LANES, 2 * LANES), BF16)] * WINDOW,
-        ],
-        in_specs=[near] * 7 + [far] * 2,
-        out_specs=[near] * (10 + WINDOW),
+            *[pltpu.VMEM(part.shape, part.dtype) for part in matrix],
+        ],
+        in_specs=[near] * 4 + [far] * (2 + WINDOW),
+        out_specs=[near] * (9 + WINDOW),
         scratch_shapes=[
             pltpu.VMEM((levels - 1, total, LANES), F32),
+            pltpu.VMEM(low.shape, F32),
+            pltpu.VMEM(high.shape, F32),
+            pltpu.SemaphoreType.DMA((2,)),
             pltpu.SemaphoreType.DMA((WINDOW,)),
-            pltpu.SemaphoreType.DMA,
         ],
         compiler_params=pltpu.CompilerParams(vmem_limit_bytes=12 * MIB),
-        cost_estimate=pl.CostEstimate(
-            flops=0, bytes_accessed=40 * MIB, transcendentals=0
-        ),
+        cost_estimate=pl.CostEstimate(flops=0, bytes_accessed=16 * MIB, transcendentals=0),
         name="prepare",
-    )(state, coef, offset, vert, wet, low, high, matrix, mix)
+    )(state, coef, offset, vert, low, high, *matrix)
 
 
 def interval_kernel(
-    width, column, mix, inv, from_up, from_down, lanes, codes, coefs, keep, wets, *refs
+    width, early, column, edge, inv, from_up, from_down, lanes, codes, coefs, keep, *refs
 ):
     matrix, refs = refs[:WINDOW], refs[WINDOW:]
     imported, low, high, state_out, imported_out, *refs = refs
-    cells, mixed, wide, force, flat = refs
+    cells, mixed, wide, force, flat, wets = refs
     levels, total = inv.shape[0], inv.shape[1]
     rows = total - 2 * HALO
     pitch = column.shape[0] // levels
     chunks = total // CHUNK
+
+    pieces = levels * GROUP
+    mixed[...] = early[0 : levels * total, :]
+    wets[...] = early[levels * total : (levels + 1) * total, :]
+    wets[0:HALO, :] = edge[4 * pieces : 4 * pieces + HALO, :]
+    wets[HALO + rows : total, :] = edge[4 * pieces + HALO : 4 * pieces + 2 * HALO, :]
+    for index in range(4):
+        row = index * GROUP + (total - 4 * GROUP if index >= 2 else 0)
+        for level in range(levels):
+            to, at = level * total + row, index * pieces + level * GROUP
+            mixed[to : to + GROUP, :] = edge[at : at + GROUP, :]
 
     force[:, 0:HALO, :] = low[...]
     force[:, HALO : HALO + rows, :] = imported[...]
@@ -544,7 +577,7 @@
 
     @pl.loop(0, chunks)
     def _(chunk):
-        solve(chunk, column, mix, cells, wide)
+        solve(chunk, column, mixed, cells, wide)
 
     @pl.loop(1, STEPS)
     def _(step):
@@ -561,11 +594,11 @@
             state_out[level : level + 8, here] = cells[pl.ds(at, 8, stride=pitch), :]
 
 
-def interval(column, mix, inv, *rest):
+def interval(early, column, edge, inv, *rest):
     levels, total = inv.shape[0], inv.shape[1]
     pitch = column.shape[0] // levels
     width, rows = rest[-3].shape[0], rest[-3].shape[1]
-    operands = (column, mix, inv, *rest)
+    operands = (early, column, edge, inv, *rest)
     return pl.pallas_call(
         functools.partial(interval_kernel, width),
         out_shape=[
@@ -576,10 +609,11 @@
         out_specs=[pl.BlockSpec(memory_space=pltpu.VMEM)] * 2,
         scratch_shapes=[
             pltpu.VMEM(column.shape, F32),
-            pltpu.VMEM(mix.shape, F32),
+            pltpu.VMEM((levels * total, LANES), F32),
             pltpu.VMEM((2 * levels, pitch * LANES), BF16),
             pltpu.VMEM((width, total, LANES), F32),
             pltpu.VMEM((width * rows, LANES), F32),
+            pltpu.VMEM((total, LANES), F32),
         ],
         compiler_params=pltpu.CompilerParams(vmem_limit_bytes=12 * MIB),
         name="interval",
@@ -629,8 +663,10 @@
     backward = [(target, source) for source, target in forward]
     low = lax.ppermute(low, "dom", forward)
     high = lax.ppermute(high, "dom", backward)
-    matrix, mix = build(state[0], coef, offset)
-    values, matrix, mix, low, high = lax.optimization_barrier((values, matrix, mix, low, high))
+    built = build(state[0], coef, offset, wet)
+    values, built, low, high = lax.optimization_barrier((values, built, low, high))
+    early, *matrix = built
+    early = pltpu.with_memory_space_constraint(early, pltpu.VMEM)
 
     pitch = capacity * width + 8
     summed, first_rows, last_rows = assemble(
@@ -648,8 +684,8 @@
     imported = across(summed, 0)
     from_low = across(last_rows, 1)
     from_high = across(first_rows, -1)
-    prepared = prepare(state[0], coef, offset, vert, wet, low, high, matrix, mix)
-    new_state, imported = interval(*prepared, imported, from_low, from_high)
+    prepared = prepare(state[0], coef, offset, vert, low, high, matrix)
+    new_state, imported = interval(early, *prepared, imported, from_low, from_high)
     return (new_state[None], imported[None])
 
 

time: 89.6 us -> 88.3 us (0.985)
  local copies, waits for them, and re-layouts: 5.3 us -> 1.68 us
  waiting for transfers between devices: 0.02 us -> 1.47 us
    unnamed x20 -> x12, local copies, waits for them, and re-layouts: 5.3 us -> 1.68 us
    pallas_call x1, Pallas kernels: 8.09 us -> 11.7 us  [prepare(): pl.pallas_call(prepare_kernel, out_shape=[pltpu.VMEM((levels * pitch, LAN...]
    pallas_call x1, Pallas kernels: 23.3 us -> 20 us  [build(): pl.pallas_call(build_kernel, grid=(chunks,), in_specs=[pl.BlockSpec(state...]
    ppermute x1, waiting for transfers between devices: 0.01 us -> 1.46 us  [local(): low = lax.ppermute(low, 'dom', forward)]
    pallas_call x1, Pallas kernels: 23 us -> 24.2 us  [interval(): pl.pallas_call(functools.partial(interval_kernel, width), out_shape=[jax....]
  transfers between devices with their start and end apart: 6 -> 6, of which waited for: 0 -> 1; matrix products, arithmetic and copies ran while one was open for 0% -> 0% of each run, Pallas kernels for 35% -> 36%
where the time goes in v4:
time: 88.3 us; the launch traced here: 87.9 us
  Pallas kernels  65.1 us (74%)
  starting transfers between devices  18.9 us (21%)
  local copies, waits for them, and re-layouts  1.68 us (2%)
  waiting for transfers between devices  1.47 us (2%)
    pallas_call x1, Pallas kernels, interval(): pl.pallas_call(functools.partial(interval_kernel, width), out_shape=[jax....  24.2 us
    pallas_call x1, Pallas kernels, build(): pl.pallas_call(build_kernel, grid=(chunks,), in_specs=[pl.BlockSpec(state...  20 us
    pallas_call x1, Pallas kernels, prepare(): pl.pallas_call(prepare_kernel, out_shape=[pltpu.VMEM((levels * pitch, LAN...  11.7 us
    pallas_call x1, Pallas kernels, remap(): pl.pallas_call(functools.partial(remap_kernel, owners, capacity), grid_sp...  8.81 us
    all_to_all x1, starting transfers between devices, local(): lax.all_to_all(values, 'dom', split_axis=0, concat_axis=0, tiled=True)  7.53 us
    ppermute x3, starting transfers between devices, across(): return lax.ppermute(value, ('comp', 'dom'), pairs)  6.9 us
    ppermute x1, starting transfers between devices, local(): high = lax.ppermute(high, 'dom', backward)  4.08 us
  transfers between devices with their start and end apart: 6, of which 1 were waited for; matrix products, arithmetic and copies ran while one was open for 0% of the time, Pallas kernels for 36%

profile of v4, /device:TPU:0, one launch (start us, length us, event | category | flops | bytes accessed | tf_op | source)
XLA Modules:
  0.0 87.9 jit_solution(17010771852254882544)
XLA Ops:
  0.6 8.8 %remap.1 = (f32[16,136,128]{2,1,0:T(8,128)}, f32[352,128]{1,0:T(8,128)}, f32[352,128]{1,0:T(8,128)}) custom-call(s32[128]{0:T(128)} %bitcast.35, s32[128]{0:T(128)} %bitcast.36, s32[128]{0:T(128)} %bitcast.37, s32[1]{0:T(128)} %bitcast.3.me, f32[8,16384]{1,0:T(8,128)} %bitcast.31, f32[128,128,128]{2,1,0:T(8,128)} %bitcast.30, f32[16,16384]{1,0:T(8,128)} %bitcast.14, ...), custom_call_target="tpu_custom_call" | custom-call | tf_op jit(solution)/shard_map/remap/pallas_call | solution.py:111
  9.4 0.0 copy-start
  9.5 0.0 copy-start.1
  9.5 0.0 copy-start.2
  9.5 7.5 %all-to-all-start = ((f32[16,136,128]{2,1,0:T(8,128)}), f32[16,136,128]{2,1,0:T(8,128)S(1)}, u32[]{:S(2)}, u32[]{:S(2)}) async-start(f32[16,136,128]{2,1,0:T(8,128)} %get-tuple-element.39), calls=%async_computation | async-start | bytes 2228224 | tf_op jit(solution)/shard_map/all_to_all | solution.py:660
  17.0 0.4 collective-permute-start
  17.4 4.1 %collective-permute-start.1 = (f32[352,128]{1,0:T(8,128)}, f32[352,128]{1,0:T(8,128)}, u32[]{:S(2)}, u32[]{:S(2)}) collective-permute-start(f32[352,128]{1,0:T(8,128)} %get-tuple-element.47), channel_id=1, source_target_pairs={{1,0},{2,1},{3,2},{4,3},{5,4},{6,5},{7,6},{8,7},{9,8},{10,9},{11,1... | collective-permute-start | bytes 540680 | tf_op jit(solution)/shard_map/ppermute | solution.py:665
  21.5 20.0 %build.1 = (f32[2448,128]{1,0:T(8,128)}, bf16[72,128,256]{2,1,0:T(8,128)(2,1)}, bf16[72,128,256]{2,1,0:T(8,128)(2,1)}, bf16[72,128,256]{2,1,0:T(8,128)(2,1)}, bf...) custom-call(f32[16,16384]{1,0:T(8,128)} %bitcast.16, f32[6,128,128]{2,1,0:T(8,128)} %bitcast.24, ...), custom_call_target="tpu_custom_call" | custom-call | flops 754974720 | bytes 83886080 | tf_op jit(solution)/shard_map/build/pallas_call | solution.py:348
  41.5 1.5 %collective-permute-done.low_far = f32[352,128]{1,0:T(8,128)S(1)} collective-permute-done((f32[352,128]{1,0:T(8,128)}, f32[352,128]{1,0:T(8,128)S(1)}, u32[]{:S(2)}, u32[]{:S(2)}) %collective-permute-start) | collective-permute-done | bytes 180256 | tf_op jit(solution)/shard_map/ppermute | solution.py:664
  43.0 0.0 copy-start.5
  43.0 0.7 copy-done.5
  43.6 0.0 collective-permute-done.1.high_far
  43.6 0.0 all-to-all-done
  43.6 0.4 assemble.1
  44.1 1.6 %collective-permute-start.2 = (f32[8,128,128]{2,1,0:T(8,128)S(1)}, f32[8,128,128]{2,1,0:T(8,128)S(1)}, u32[]{:S(2)}, u32[]{:S(2)}) collective-permute-start(f32[8,128,128]{2,1,0:T(8,128)S(1)} %get-tuple-element.71), channel_id=1, source_target_pairs={{0,16},{1,17},{2,18},{3,19},{4,20},{5,21},{6,22},{7,23},{8,24},{9,... | collective-permute-start | bytes 1572872 | tf_op jit(solution)/shard_map/ppermute | solution.py:682
  45.7 0.0 collective-permute-start.3
  45.7 5.3 %collective-permute-start.4 = (f32[8,8,128]{2,1,0:T(8,128)S(1)}, f32[8,8,128]{2,1,0:T(8,128)S(1)}, u32[]{:S(2)}, u32[]{:S(2)}) collective-permute-start(f32[8,8,128]{2,1,0:T(8,128)S(1)} %get-tuple-element.73), channel_id=1, source_target_pairs={{0,31},{1,16},{2,17},{3,18},{4,19},{5,20},{6,21},{7,22},{8,23},{9,... | collective-permute-start | bytes 98312 | tf_op jit(solution)/shard_map/ppermute | solution.py:682
  51.0 0.0 copy-done
  51.0 0.0 copy-done.1
  51.0 0.0 copy-done.2
  51.0 0.0 copy-start.3
  51.0 1.0 %copy-done.3 = s32[1,6,16384]{2,0,1:T(1,128)S(1)} copy-done((s32[1,6,16384]{2,0,1:T(1,128)S(1)}, s32[1,6,16384]{2,0,1:T(1,128)}, u32[]{:S(2)}) %copy-start.3) | copy-done | bytes 393240
  52.0 0.0 copy-start.4
  52.0 11.7 %prepare.1 = (f32[2560,128]{1,0:T(8,128)S(1)}, f32[528,128]{1,0:T(8,128)S(1)}, f32[16,144,128]{2,1,0:T(8,128)S(1)}, f32[16,144,128]{2,1,0:T(8,128)S(1)}, f32[16,...) custom-call(f32[16,16384]{1,0:T(8,128)S(1)} %bitcast.17, ...), custom_call_target="tpu_custom_call" | custom-call | bytes 16777216 | tf_op jit(solution)/shard_map/prepare/pallas_call | solution.py:479
  63.7 0.0 collective-permute-done.3.refs_6_
  63.7 0.0 collective-permute-done.4.refs_7_
  63.7 0.0 collective-permute-done.2.refs_5_
  63.8 0.0 copy-done.4
  63.8 24.2 %interval.1 = (f32[16,16384]{1,0:T(8,128)}, f32[8,16384]{1,0:T(8,128)}) custom-call(f32[2448,128]{1,0:T(8,128)S(1)} %copy-done.4, f32[2560,128]{1,0:T(8,128)S(1)} %get-tuple-element.56.column, f32[528,128]{1,0:T(8,128)S(1)} %get-tuple-element.57.edge, f32[16,144,128]{2,1,0:T(8,128)S(1)} %get-tuple-element.58.inv, ...), custom_call_target="tpu_custom_call" | custom-call | tf_op jit(solution)/shard_map/interval/pallas_call | solution.py:602
Async XLA Ops:
  9.4 41.6 %copy-start = (f32[1,16,16384]{2,1,0:T(8,128)S(1)}, f32[1,16,16384]{2,1,0:T(8,128)}, u32[]{:S(2)}) copy-start(f32[1,16,16384]{2,1,0:T(8,128)} %param.10) | copy-start | bytes 3145732
  9.5 41.6 %copy-start.1 = (f32[1,15,16384]{2,0,1:T(1,128)S(1)}, f32[1,15,16384]{2,0,1:T(1,128)}, u32[]{:S(2)}) copy-start(f32[1,15,16384]{2,0,1:T(1,128)} %param.19) | copy-start | bytes 2949124
  9.5 41.5 %copy-start.2 = (f32[1,6,16384]{2,0,1:T(1,128)S(1)}, f32[1,6,16384]{2,0,1:T(1,128)}, u32[]{:S(2)}) copy-start(f32[1,6,16384]{2,0,1:T(1,128)} %param.17) | copy-start | bytes 1179652
  9.5 34.2 %all-to-all-start = ((f32[16,136,128]{2,1,0:T(8,128)}), f32[16,136,128]{2,1,0:T(8,128)S(1)}, u32[]{:S(2)}, u32[]{:S(2)}) async-start(f32[16,136,128]{2,1,0:T(8,128)} %get-tuple-element.39), calls=%async_computation | async-start | bytes 2228224 | tf_op jit(solution)/shard_map/all_to_all | solution.py:660
  17.0 26.0 %collective-permute-start = (f32[352,128]{1,0:T(8,128)}, f32[352,128]{1,0:T(8,128)S(1)}, u32[]{:S(2)}, u32[]{:S(2)}) collective-permute-start(f32[352,128]{1,0:T(8,128)} %get-tuple-element.46), channel_id=1, source_target_pairs={{0,1},{1,2},{2,3},{3,4},{4,5},{5,6},{6,7},{7,8},{8,9},{9,10},{10,1... | collective-permute-start | bytes 540680 | tf_op jit(solution)/shard_map/ppermute | solution.py:664
  17.4 26.2 %collective-permute-start.1 = (f32[352,128]{1,0:T(8,128)}, f32[352,128]{1,0:T(8,128)}, u32[]{:S(2)}, u32[]{:S(2)}) collective-permute-start(f32[352,128]{1,0:T(8,128)} %get-tuple-element.47), channel_id=1, source_target_pairs={{1,0},{2,1},{3,2},{4,3},{5,4},{6,5},{7,6},{8,7},{9,8},{10,9},{11,1... | collective-permute-start | bytes 540680 | tf_op jit(solution)/shard_map/ppermute | solution.py:665
  43.0 0.7 copy-start.5
  44.1 19.7 %collective-permute-start.2 = (f32[8,128,128]{2,1,0:T(8,128)S(1)}, f32[8,128,128]{2,1,0:T(8,128)S(1)}, u32[]{:S(2)}, u32[]{:S(2)}) collective-permute-start(f32[8,128,128]{2,1,0:T(8,128)S(1)} %get-tuple-element.71), channel_id=1, source_target_pairs={{0,16},{1,17},{2,18},{3,19},{4,20},{5,21},{6,22},{7,23},{8,24},{9,... | collective-permute-start | bytes 1572872 | tf_op jit(solution)/shard_map/ppermute | solution.py:682
  45.7 18.1 %collective-permute-start.3 = (f32[8,8,128]{2,1,0:T(8,128)S(1)}, f32[8,8,128]{2,1,0:T(8,128)S(1)}, u32[]{:S(2)}, u32[]{:S(2)}) collective-permute-start(f32[8,8,128]{2,1,0:T(8,128)S(1)} %get-tuple-element.72), channel_id=1, source_target_pairs={{0,17},{1,18},{2,19},{3,20},{4,21},{5,22},{6,23},{7,24},{8,25},{9,... | collective-permute-start | bytes 98312 | tf_op jit(solution)/shard_map/ppermute | solution.py:682
  45.7 18.1 %collective-permute-start.4 = (f32[8,8,128]{2,1,0:T(8,128)S(1)}, f32[8,8,128]{2,1,0:T(8,128)S(1)}, u32[]{:S(2)}, u32[]{:S(2)}) collective-permute-start(f32[8,8,128]{2,1,0:T(8,128)S(1)} %get-tuple-element.73), channel_id=1, source_target_pairs={{0,31},{1,16},{2,17},{3,18},{4,19},{5,20},{6,21},{7,22},{8,23},{9,... | collective-permute-start | bytes 98312 | tf_op jit(solution)/shard_map/ppermute | solution.py:682
  51.0 1.0 %copy-start.3 = (s32[1,6,16384]{2,0,1:T(1,128)S(1)}, s32[1,6,16384]{2,0,1:T(1,128)}, u32[]{:S(2)}) copy-start(s32[1,6,16384]{2,0,1:T(1,128)} %param.18) | copy-start | bytes 1179652
  52.0 11.8 %copy-start.4 = (f32[2448,128]{1,0:T(8,128)S(1)}, f32[2448,128]{1,0:T(8,128)}, u32[]{:S(2)}) copy-start(f32[2448,128]{1,0:T(8,128)} %get-tuple-element.48.early) | copy-start | bytes 3760132

commit v5 on v4

--- a/solution.py
+++ b/solution.py
@@ -13,6 +13,7 @@
 LANES = 128
 REACH = RIM // LANES
 WINDOW = 2 * REACH + 1
+EARLY = WINDOW - REACH
 HALO = STEPS * REACH
 PAD = 8
 MIB = 2**20
@@ -31,44 +32,85 @@
 
 
 def remap_kernel(
-    owners, capacity, routes, target, source, me, fields, weights, *refs
+    owners, capacity, routes, target, source, me, fields_far, weights_far, *refs
 ):
-    edges, (out, low, high, counts, marks) = refs[:10], refs[10:]
-    step = pl.program_id(0)
-    per_step = weights.shape[0]
+    far, (out, low, high, fields, weights, *refs) = refs[:5], refs[5:]
+    near, (counts, marks, filled, loaded) = refs[:10], refs[10:]
+    block_count = weights.shape[0]
+    per_step = 16
     width = fields.shape[0]
+    levels, cells = far[0].shape
+    rows = cells // LANES
+    edge = HALO * LANES
     lane = lax.broadcasted_iota(jnp.int32, (1, LANES), 1)
     label_row = capacity * width
 
-    @pl.when(step == 0)
-    def _():
-        out[...] = jnp.zeros_like(out)
-        marks[...] = jnp.zeros_like(marks)
-        for owner in range(owners):
-            counts[owner] = 0
-        for side, pack in ((0, low), (1, high)):
-            state, coef, offset, vert, wet = edges[side::2]
-            levels = state.shape[0]
-            for row in range(HALO):
-                for level in range(0, levels, 8):
-                    tile = state[level : level + 8, row * LANES : (row + 1) * LANES]
-                    pack[pl.ds(level * HALO + row, 8, stride=HALO), :] = tile
-            at = levels * HALO
-            for part in (coef, offset, vert):
-                for index in range(part.shape[0]):
-                    pack[at : at + HALO, :] = part[index].astype(F32)
-                    at += HALO
-            pack[at : at + HALO, :] = wet[...].astype(F32)
-
-    for local_block in range(per_step):
-        block = step * per_step + local_block
+    def chunk_copy(step):
+        here = pl.ds(step * per_step, per_step)
+        return pltpu.make_async_copy(weights_far.at[here], weights.at[here], loaded.at[step])
+
+    fields_copy = pltpu.make_async_copy(fields_far, fields, filled.at[10])
+    fields_copy.start()
+    for step in range(block_count // per_step):
+        chunk_copy(step).start()
+    edge_copies = []
+    for index, part in enumerate(far):
+        for side in range(2):
+            if index == 0:
+                piece = part.at[:, pl.ds((0 if side else cells - edge), edge)]
+            elif len(part.shape) == 3:
+                piece = part.at[:, pl.ds((0 if side else rows - HALO), HALO), :]
+            else:
+                piece = part.at[pl.ds((0 if side else rows - HALO), HALO), :]
+            at = 2 * index + side
+            edge_copies.append(pltpu.make_async_copy(piece, near[at], filled.at[at]))
+            edge_copies[-1].start()
+
+    out[...] = jnp.zeros_like(out)
+    marks[...] = jnp.zeros_like(marks)
+    for owner in range(owners):
+        counts[owner] = 0
+    fields_copy.wait()
+
+    @pl.loop(0, block_count // per_step)
+    def _(step):
+        chunk_copy(step).wait()
+        remap_blocks(
+            capacity, step * per_step, per_step, routes, target, source, me, fields, weights,
+            out, counts, marks, lane,
+        )
+
+    for owner in range(owners):
+        out[owner, label_row : label_row + 1, :] = marks[owner : owner + 1, :]
+    for copy in edge_copies:
+        copy.wait()
+    for side, pack in ((0, low), (1, high)):
+        state, coef, offset, vert, wet = near[side::2]
+        for row in range(HALO):
+            for level in range(0, levels, 8):
+                tile = state[level : level + 8, row * LANES : (row + 1) * LANES]
+                pack[pl.ds(level * HALO + row, 8, stride=HALO), :] = tile
+        at = levels * HALO
+        for part in (coef, offset, vert):
+            for index in range(part.shape[0]):
+                pack[at : at + HALO, :] = part[index].astype(F32)
+                at += HALO
+        pack[at : at + HALO, :] = wet[...].astype(F32)
+
+
+def remap_blocks(
+    capacity, first, count, routes, target, source, me, fields, weights, out, counts, marks, lane
+):
+    width = fields.shape[0]
+    for index in range(count):
+        block = first + index
         owner = routes[block]
         rank = counts[owner]
         counts[owner] = rank + 1
         start = pl.multiple_of(source[block] * LANES, LANES)
         picked_high, picked_low = split(fields[:, pl.ds(start, LANES)])
         picked = jnp.concatenate([picked_high, picked_low], axis=0)
-        both = jnp.concatenate(split(weights[local_block]), axis=1)
+        both = jnp.concatenate(split(weights[block]), axis=1)
         product = jnp.dot(picked, both, preferred_element_type=F32)
         product = product[:, :LANES] + product[:, LANES:]
         value = product[:width] + product[width:]
@@ -79,63 +121,42 @@
             lane == slot, (target[block] + 1).astype(F32), marks[pl.ds(owner, 1), :]
         )
 
-    @pl.when(step == pl.num_programs(0) - 1)
-    def _():
-        for owner in range(owners):
-            out[owner, label_row : label_row + 1, :] = marks[owner : owner + 1, :]
-
 
 def remap(routes, target, source, me, fields, weights, state, parts, owners, capacity):
     block_count = weights.shape[0]
-    width, cells = fields.shape
+    width = fields.shape[0]
     levels = state.shape[0]
-    rows = cells // LANES
-    per_step = 16
-    edge = HALO * LANES
-    ends = (rows // HALO - 1, 0)
-    specs = [pl.BlockSpec((levels, edge), lambda i, *_, e=e: (0, e)) for e in ends]
-    edges = [state, state]
+    scratch = [pltpu.VMEM((levels, HALO * LANES), F32)] * 2
     pack_rows = levels * HALO
     for part in parts:
-        if part.ndim == 3:
-            count = part.shape[0]
-            specs += [
-                pl.BlockSpec((count, HALO, LANES), lambda i, *_, e=e: (0, e, 0)) for e in ends
-            ]
-        else:
-            count = 1
-            specs += [pl.BlockSpec((HALO, LANES), lambda i, *_, e=e: (e, 0)) for e in ends]
+        count = part.shape[0] if part.ndim == 3 else 1
+        scratch += [pltpu.VMEM((*part.shape[:-2], HALO, LANES), part.dtype)] * 2
         pack_rows += count * HALO
-        edges += [part, part]
     slots = (owners, capacity * width + 8, LANES)
+    scalar = pl.BlockSpec(memory_space=pltpu.SMEM)
+    far = pl.BlockSpec(memory_space=pltpu.HBM)
+    near = pl.BlockSpec(memory_space=pltpu.VMEM)
     return pl.pallas_call(
         functools.partial(remap_kernel, owners, capacity),
-        grid_spec=pltpu.PrefetchScalarGridSpec(
-            num_scalar_prefetch=4,
-            grid=(block_count // per_step,),
-            in_specs=[
-                pl.BlockSpec((width, cells), lambda i, *_: (0, 0)),
-                pl.BlockSpec((per_step, LANES, LANES), lambda i, *_: (i, 0, 0)),
-                *specs,
-            ],
-            out_specs=[
-                pl.BlockSpec(slots, lambda i, *_: (0, 0, 0)),
-                pl.BlockSpec((pack_rows, LANES), lambda i, *_: (0, 0)),
-                pl.BlockSpec((pack_rows, LANES), lambda i, *_: (0, 0)),
-            ],
-            scratch_shapes=[
-                pltpu.SMEM((owners,), jnp.int32),
-                pltpu.VMEM((owners, LANES), F32),
-            ],
-        ),
+        in_specs=[scalar] * 4 + [far] * 7,
+        out_specs=[near] * 3,
         out_shape=[
             jax.ShapeDtypeStruct(slots, F32),
             jax.ShapeDtypeStruct((pack_rows, LANES), F32),
             jax.ShapeDtypeStruct((pack_rows, LANES), F32),
         ],
+        scratch_shapes=[
+            pltpu.VMEM(fields.shape, F32),
+            pltpu.VMEM(weights.shape, F32),
+            *scratch,
+            pltpu.SMEM((owners,), jnp.int32),
+            pltpu.VMEM((owners, LANES), F32),
+            pltpu.SemaphoreType.DMA((11,)),
+            pltpu.SemaphoreType.DMA((block_count // 16,)),
+        ],
         compiler_params=pltpu.CompilerParams(vmem_limit_bytes=60 * MIB),
         name="remap",
-    )(routes, target, source, me, fields, weights, *edges)
+    )(routes, target, source, me, fields, weights, state, *parts)
 
 
 def assemble_kernel(owners, capacity, width, slots, out, low, high, hot, values):
@@ -383,19 +404,19 @@
     state, coef, offset, vert, low_far, high_far, *refs
 ):
     far, (column, edge, inv, from_up, from_down, lanes, codes, coefs, keep, *refs) = (
-        refs[:WINDOW],
-        refs[WINDOW:],
+        refs[:EARLY],
+        refs[EARLY:],
     )
-    matrix, (verts, low, high, packed, copied) = refs[:WINDOW], refs[WINDOW:]
+    matrix, (verts, low, high, packed, copied) = refs[:EARLY], refs[EARLY:]
     pack_copies = [
         pltpu.make_async_copy(source, target, packed.at[index])
         for index, (source, target) in enumerate(((low_far, low), (high_far, high)))
     ]
     matrix_copies = [
         pltpu.make_async_copy(far[reach], matrix[reach], copied.at[reach])
-        for reach in range(WINDOW)
+        for reach in range(EARLY)
     ]
-    for copy in pack_copies + matrix_copies:
+    for copy in pack_copies:
         copy.start()
     levels = state.shape[0]
     rows = state.shape[1] // LANES
@@ -415,6 +436,8 @@
 
     for copy in pack_copies:
         copy.wait()
+    for copy in matrix_copies:
+        copy.start()
     for pack, first in ((low, 0), (high, total - HALO)):
         for level in range(levels):
             at = level * pitch + PAD + first
@@ -490,16 +513,16 @@
             pltpu.VMEM((total, LANES), F32),
             *[pltpu.VMEM(part.shape, part.dtype) for part in matrix],
         ],
-        in_specs=[near] * 4 + [far] * (2 + WINDOW),
-        out_specs=[near] * (9 + WINDOW),
+        in_specs=[near] * 4 + [far] * (2 + EARLY),
+        out_specs=[near] * (9 + EARLY),
         scratch_shapes=[
             pltpu.VMEM((levels - 1, total, LANES), F32),
             pltpu.VMEM(low.shape, F32),
             pltpu.VMEM(high.shape, F32),
             pltpu.SemaphoreType.DMA((2,)),
-            pltpu.SemaphoreType.DMA((WINDOW,)),
-        ],
-        compiler_params=pltpu.CompilerParams(vmem_limit_bytes=12 * MIB),
+            pltpu.SemaphoreType.DMA((EARLY,)),
+        ],
+        compiler_params=pltpu.CompilerParams(vmem_limit_bytes=24 * MIB),
         cost_estimate=pl.CostEstimate(flops=0, bytes_accessed=16 * MIB, transcendentals=0),
         name="prepare",
     )(state, coef, offset, vert, low, high, *matrix)
@@ -508,25 +531,26 @@
 def interval_kernel(
     width, early, column, edge, inv, from_up, from_down, lanes, codes, coefs, keep, *refs
 ):
-    matrix, refs = refs[:WINDOW], refs[WINDOW:]
-    imported, low, high, state_out, imported_out, *refs = refs
-    cells, mixed, wide, force, flat, wets = refs
+    matrix, refs = refs[:EARLY], refs[EARLY:]
+    imported, low, high, refs = *refs[:3], refs[3:]
+    late_far, (state_out, imported_out, *refs) = refs[: WINDOW - EARLY], refs[WINDOW - EARLY :]
+    cells, mixed, wide, force, flat, wets, copied, *late = refs
+    matrix = (*matrix, *late)
+    late_copies = [
+        pltpu.make_async_copy(source, part, copied.at[index])
+        for index, (source, part) in enumerate(zip(late_far, late))
+    ]
+    for copy in late_copies:
+        copy.start()
     levels, total = inv.shape[0], inv.shape[1]
     rows = total - 2 * HALO
     pitch = column.shape[0] // levels
     chunks = total // CHUNK
 
     pieces = levels * GROUP
-    mixed[...] = early[0 : levels * total, :]
     wets[...] = early[levels * total : (levels + 1) * total, :]
     wets[0:HALO, :] = edge[4 * pieces : 4 * pieces + HALO, :]
     wets[HALO + rows : total, :] = edge[4 * pieces + HALO : 4 * pieces + 2 * HALO, :]
-    for index in range(4):
-        row = index * GROUP + (total - 4 * GROUP if index >= 2 else 0)
-        for level in range(levels):
-            to, at = level * total + row, index * pieces + level * GROUP
-            mixed[to : to + GROUP, :] = edge[at : at + GROUP, :]
-
     force[:, 0:HALO, :] = low[...]
     force[:, HALO : HALO + rows, :] = imported[...]
     force[:, HALO + rows : total, :] = high[...]
@@ -537,6 +561,9 @@
     def _(row):
         here = pl.ds(pl.multiple_of(row * LANES, LANES), LANES)
         imported_out[:, here] = flat[pl.ds(row, width, stride=rows), :]
+
+    def from_mixed(level, group, row):
+        return mixed[pl.ds(level * total + row, GROUP), :]
 
     def solve(chunk, source, spread_sum, out, wide):
         for group in range(CHUNK // GROUP):
@@ -547,7 +574,7 @@
             partial = []
             for level in range(levels):
                 value = left * source[pl.ds(level * pitch + PAD + row, GROUP), :]
-                value = value + spread_sum[pl.ds(level * total + row, GROUP), :]
+                value = value + spread_sum(level, group, row)
                 if level < width:
                     value = value + force[level, here, :] * wet
                 value = value * inv[level, here, :]
@@ -575,16 +602,28 @@
 
         spread_group(levels, total, source, by_gather, terms, mixed)
 
-    @pl.loop(0, chunks)
+    def from_early(level, group, row):
+        return early[pl.ds(level * total + row, GROUP), :]
+
+    def from_edge(last, level, group, row):
+        return edge[pl.ds((2 * last + group) * pieces + level * GROUP, GROUP), :]
+
+    solve(0, column, functools.partial(from_edge, 0), cells, wide)
+
+    @pl.loop(1, chunks - 1)
     def _(chunk):
-        solve(chunk, column, mixed, cells, wide)
+        solve(chunk, column, from_early, cells, wide)
+
+    solve(chunks - 1, column, functools.partial(from_edge, 1), cells, wide)
+    for copy in late_copies:
+        copy.wait()
 
     @pl.loop(1, STEPS)
     def _(step):
         for chunk in range(chunks):
             spread(jnp.int32(chunk), cells, wide)
         for chunk in range(chunks):
-            solve(chunk, cells, mixed, cells, wide)
+            solve(chunk, cells, from_mixed, cells, wide)
 
     @pl.loop(0, rows, unroll=8)
     def _(row):
@@ -594,18 +633,20 @@
             state_out[level : level + 8, here] = cells[pl.ds(at, 8, stride=pitch), :]
 
 
-def interval(early, column, edge, inv, *rest):
+def interval(late, early, column, edge, inv, *rest):
     levels, total = inv.shape[0], inv.shape[1]
     pitch = column.shape[0] // levels
     width, rows = rest[-3].shape[0], rest[-3].shape[1]
     operands = (early, column, edge, inv, *rest)
+    late = [pltpu.with_memory_space_constraint(part, pltpu.HBM) for part in late]
     return pl.pallas_call(
         functools.partial(interval_kernel, width),
         out_shape=[
             jax.ShapeDtypeStruct((levels, rows * LANES), F32),
             jax.ShapeDtypeStruct((width, rows * LANES), F32),
         ],
-        in_specs=[pl.BlockSpec(memory_space=pltpu.VMEM)] * len(operands),
+        in_specs=[pl.BlockSpec(memory_space=pltpu.VMEM)] * len(operands)
+        + [pl.BlockSpec(memory_space=pltpu.HBM)] * len(late),
         out_specs=[pl.BlockSpec(memory_space=pltpu.VMEM)] * 2,
         scratch_shapes=[
             pltpu.VMEM(column.shape, F32),
@@ -614,10 +655,12 @@
             pltpu.VMEM((width, total, LANES), F32),
             pltpu.VMEM((width * rows, LANES), F32),
             pltpu.VMEM((total, LANES), F32),
-        ],
-        compiler_params=pltpu.CompilerParams(vmem_limit_bytes=12 * MIB),
+            pltpu.SemaphoreType.DMA((len(late),)),
+            *[pltpu.VMEM(part.shape, part.dtype) for part in late],
+        ],
+        compiler_params=pltpu.CompilerParams(vmem_limit_bytes=24 * MIB),
         name="interval",
-    )(*operands)
+    )(*operands, *late)
 
 
 def local(
@@ -684,8 +727,10 @@
     imported = across(summed, 0)
     from_low = across(last_rows, 1)
     from_high = across(first_rows, -1)
-    prepared = prepare(state[0], coef, offset, vert, low, high, matrix)
-    new_state, imported = interval(early, *prepared, imported, from_low, from_high)
+    prepared = prepare(state[0], coef, offset, vert, low, high, matrix[:EARLY])
+    new_state, imported = interval(
+        matrix[EARLY:], early, *prepared, imported, from_low, from_high
+    )
     return (new_state[None], imported[None])
 
 

time: 88.3 us -> 84.4 us (0.956)
  the two profiles are of different devices: /device:TPU:0 before, /device:TPU:9 now
where the time goes in v5:
time: 84.4 us; the launch traced here: 84.1 us
  Pallas kernels  58.6 us (69%)
  waiting for transfers between devices  11.9 us (14%)
  starting transfers between devices  11.2 us (13%)
  local copies, waits for them, and re-layouts  1.68 us (2%)
    pallas_call x1, Pallas kernels, interval(): pl.pallas_call(functools.partial(interval_kernel, width), out_shape=[jax....  26 us
    pallas_call x1, Pallas kernels, build(): pl.pallas_call(build_kernel, grid=(chunks,), in_specs=[pl.BlockSpec(state...  20 us
    all_to_all x1, starting transfers between devices, local(): lax.all_to_all(values, 'dom', split_axis=0, concat_axis=0, tiled=True)  6.76 us
    pallas_call x1, Pallas kernels, prepare(): pl.pallas_call(prepare_kernel, out_shape=[pltpu.VMEM((levels * pitch, LAN...  6.28 us
    all_to_all x1, waiting for transfers between devices, local(): lax.all_to_all(values, 'dom', split_axis=0, concat_axis=0, tiled=True)  6 us
    pallas_call x1, Pallas kernels, remap(): pl.pallas_call(functools.partial(remap_kernel, owners, capacity), in_spec...  5.92 us
    ppermute x3, waiting for transfers between devices, across(): return lax.ppermute(value, ('comp', 'dom'), pairs)  5.88 us
    ppermute x3, starting transfers between devices, across(): return lax.ppermute(value, ('comp', 'dom'), pairs)  3.02 us
  transfers between devices with their start and end apart: 6, of which 3 were waited for; matrix products, arithmetic and copies ran while one was open for 0% of the time, Pallas kernels for 31%

profile of v5, /device:TPU:9, one launch (start us, length us, event | category | flops | bytes accessed | tf_op | source)
XLA Modules:
  0.0 84.1 jit_solution(6659204546482645834)
XLA Ops:
  0.6 5.9 %remap.1 = (f32[16,136,128]{2,1,0:T(8,128)}, f32[352,128]{1,0:T(8,128)}, f32[352,128]{1,0:T(8,128)}) custom-call(s32[128]{0:T(128)} %bitcast.30, s32[128]{0:T(128)} %bitcast.31, s32[128]{0:T(128)} %bitcast.32, s32[1]{0:T(128)} %bitcast.3.me, f32[8,16384]{1,0:T(8,128)} %bitcast.27, f32[128,128,128]{2,1,0:T(8,128)} %bitcast.26, f32[16,16384]{1,0:T(8,128)} %bitcast.15, ...), custom_call_target="tpu_custom_call" | custom-call | tf_op jit(solution)/shard_map/remap/pallas_call | solution.py:139
  6.6 0.0 copy-start
  6.6 0.0 copy-start.1
  6.6 0.0 copy-start.2
  6.6 6.8 %all-to-all-start = ((f32[16,136,128]{2,1,0:T(8,128)}), f32[16,136,128]{2,1,0:T(8,128)S(1)}, u32[]{:S(2)}, u32[]{:S(2)}) async-start(f32[16,136,128]{2,1,0:T(8,128)} %get-tuple-element.37), calls=%async_computation | async-start | bytes 2228224 | tf_op jit(solution)/shard_map/all_to_all | solution.py:703
  13.4 1.4 %collective-permute-start = (f32[352,128]{1,0:T(8,128)}, f32[352,128]{1,0:T(8,128)S(1)}, u32[]{:S(2)}, u32[]{:S(2)}) collective-permute-start(f32[352,128]{1,0:T(8,128)} %get-tuple-element.44), channel_id=1, source_target_pairs={{0,1},{1,2},{2,3},{3,4},{4,5},{5,6},{6,7},{7,8},{8,9},{9,10},{10,1... | collective-permute-start | bytes 540680 | tf_op jit(solution)/shard_map/ppermute | solution.py:707
  14.8 0.0 collective-permute-start.1
  14.8 20.0 %build.1 = (f32[2448,128]{1,0:T(8,128)}, bf16[72,128,256]{2,1,0:T(8,128)(2,1)}, bf16[72,128,256]{2,1,0:T(8,128)(2,1)}, bf16[72,128,256]{2,1,0:T(8,128)(2,1)}, bf...) custom-call(f32[16,16384]{1,0:T(8,128)} %bitcast.16, f32[6,128,128]{2,1,0:T(8,128)} %bitcast.21, ...), custom_call_target="tpu_custom_call" | custom-call | flops 754974720 | bytes 83886080 | tf_op jit(solution)/shard_map/build/pallas_call | solution.py:369
  34.8 0.0 collective-permute-done.low_far
  34.8 0.0 copy-start.5
  34.9 0.7 copy-done.5
  35.5 0.0 collective-permute-done.1.high_far
  35.5 6.0 %all-to-all-done = f32[16,136,128]{2,1,0:T(8,128)S(1)} async-done(((f32[16,136,128]{2,1,0:T(8,128)}), f32[16,136,128]{2,1,0:T(8,128)S(1)}, u32[]{:S(2)}, u32[]{:S(2)}) %all-to-all-start) | async-done | bytes 1114144 | tf_op jit(solution)/shard_map/all_to_all | solution.py:703
  41.5 0.4 assemble.1
  42.0 1.3 %collective-permute-start.2 = (f32[8,128,128]{2,1,0:T(8,128)S(1)}, f32[8,128,128]{2,1,0:T(8,128)S(1)}, u32[]{:S(2)}, u32[]{:S(2)}) collective-permute-start(f32[8,128,128]{2,1,0:T(8,128)S(1)} %get-tuple-element.65), channel_id=1, source_target_pairs={{0,16},{1,17},{2,18},{3,19},{4,20},{5,21},{6,22},{7,23},{8,24},{9,... | collective-permute-start | bytes 1572872 | tf_op jit(solution)/shard_map/ppermute | solution.py:725
  43.2 1.7 %collective-permute-start.3 = (f32[8,8,128]{2,1,0:T(8,128)S(1)}, f32[8,8,128]{2,1,0:T(8,128)S(1)}, u32[]{:S(2)}, u32[]{:S(2)}) collective-permute-start(f32[8,8,128]{2,1,0:T(8,128)S(1)} %get-tuple-element.66), channel_id=1, source_target_pairs={{0,17},{1,18},{2,19},{3,20},{4,21},{5,22},{6,23},{7,24},{8,25},{9,... | collective-permute-start | bytes 98312 | tf_op jit(solution)/shard_map/ppermute | solution.py:725
  44.9 0.1 collective-permute-start.4
  45.0 0.0 copy-done
  45.0 0.0 copy-done.1
  45.0 0.0 copy-done.2
  45.0 0.0 copy-start.3
  45.0 1.0 %copy-done.3 = s32[1,6,16384]{2,0,1:T(1,128)S(1)} copy-done((s32[1,6,16384]{2,0,1:T(1,128)S(1)}, s32[1,6,16384]{2,0,1:T(1,128)}, u32[]{:S(2)}) %copy-start.3) | copy-done | bytes 393240
  46.0 0.0 copy-start.4
  46.0 6.3 %prepare.1 = (f32[2560,128]{1,0:T(8,128)S(1)}, f32[528,128]{1,0:T(8,128)S(1)}, f32[16,144,128]{2,1,0:T(8,128)S(1)}, f32[16,144,128]{2,1,0:T(8,128)S(1)}, f32[16,...) custom-call(f32[16,16384]{1,0:T(8,128)S(1)} %bitcast.17, ...), custom_call_target="tpu_custom_call" | custom-call | bytes 16777216 | tf_op jit(solution)/shard_map/prepare/pallas_call | solution.py:502
  52.3 4.9 %collective-permute-done.3.refs_4_ = f32[8,8,128]{2,1,0:T(8,128)S(1)} collective-permute-done((f32[8,8,128]{2,1,0:T(8,128)S(1)}, f32[8,8,128]{2,1,0:T(8,128)S(1)}, u32[]{:S(2)}, u32[]{:S(2)}) %collective-permute-start.3) | collective-permute-done | bytes 32800 | tf_op jit(solution)/shard_map/ppermute | solution.py:725
  57.2 0.9 %collective-permute-done.4.refs_5_ = f32[8,8,128]{2,1,0:T(8,128)S(1)} collective-permute-done((f32[8,8,128]{2,1,0:T(8,128)S(1)}, f32[8,8,128]{2,1,0:T(8,128)S(1)}, u32[]{:S(2)}, u32[]{:S(2)}) %collective-permute-start.4) | collective-permute-done | bytes 32800 | tf_op jit(solution)/shard_map/ppermute | solution.py:725
  58.2 0.0 collective-permute-done.2.refs_3_
  58.2 0.0 copy-done.4
  58.2 26.0 %interval.1 = (f32[16,16384]{1,0:T(8,128)}, f32[8,16384]{1,0:T(8,128)}) custom-call(f32[2448,128]{1,0:T(8,128)S(1)} %copy-done.4, f32[2560,128]{1,0:T(8,128)S(1)} %get-tuple-element.52.column, f32[528,128]{1,0:T(8,128)S(1)} %get-tuple-element.53.edge, f32[16,144,128]{2,1,0:T(8,128)S(1)} %get-tuple-element.54.inv, ...), custom_call_target="tpu_custom_call" | custom-call | tf_op jit(solution)/shard_map/interval/pallas_call | solution.py:642
Async XLA Ops:
  6.6 38.4 %copy-start = (f32[1,16,16384]{2,1,0:T(8,128)S(1)}, f32[1,16,16384]{2,1,0:T(8,128)}, u32[]{:S(2)}) copy-start(f32[1,16,16384]{2,1,0:T(8,128)} %param.10) | copy-start | bytes 3145732
  6.6 38.4 %copy-start.1 = (f32[1,15,16384]{2,0,1:T(1,128)S(1)}, f32[1,15,16384]{2,0,1:T(1,128)}, u32[]{:S(2)}) copy-start(f32[1,15,16384]{2,0,1:T(1,128)} %param.19) | copy-start | bytes 2949124
  6.6 38.4 %copy-start.2 = (f32[1,6,16384]{2,0,1:T(1,128)S(1)}, f32[1,6,16384]{2,0,1:T(1,128)}, u32[]{:S(2)}) copy-start(f32[1,6,16384]{2,0,1:T(1,128)} %param.17) | copy-start | bytes 1179652
  6.6 34.9 %all-to-all-start = ((f32[16,136,128]{2,1,0:T(8,128)}), f32[16,136,128]{2,1,0:T(8,128)S(1)}, u32[]{:S(2)}, u32[]{:S(2)}) async-start(f32[16,136,128]{2,1,0:T(8,128)} %get-tuple-element.37), calls=%async_computation | async-start | bytes 2228224 | tf_op jit(solution)/shard_map/all_to_all | solution.py:703
  13.4 21.5 %collective-permute-start = (f32[352,128]{1,0:T(8,128)}, f32[352,128]{1,0:T(8,128)S(1)}, u32[]{:S(2)}, u32[]{:S(2)}) collective-permute-start(f32[352,128]{1,0:T(8,128)} %get-tuple-element.44), channel_id=1, source_target_pairs={{0,1},{1,2},{2,3},{3,4},{4,5},{5,6},{6,7},{7,8},{8,9},{9,10},{10,1... | collective-permute-start | bytes 540680 | tf_op jit(solution)/shard_map/ppermute | solution.py:707
  14.8 20.7 %collective-permute-start.1 = (f32[352,128]{1,0:T(8,128)}, f32[352,128]{1,0:T(8,128)}, u32[]{:S(2)}, u32[]{:S(2)}) collective-permute-start(f32[352,128]{1,0:T(8,128)} %get-tuple-element.45), channel_id=1, source_target_pairs={{1,0},{2,1},{3,2},{4,3},{5,4},{6,5},{7,6},{8,7},{9,8},{10,9},{11,1... | collective-permute-start | bytes 540680 | tf_op jit(solution)/shard_map/ppermute | solution.py:708
  34.8 0.7 copy-start.5
  42.0 16.2 %collective-permute-start.2 = (f32[8,128,128]{2,1,0:T(8,128)S(1)}, f32[8,128,128]{2,1,0:T(8,128)S(1)}, u32[]{:S(2)}, u32[]{:S(2)}) collective-permute-start(f32[8,128,128]{2,1,0:T(8,128)S(1)} %get-tuple-element.65), channel_id=1, source_target_pairs={{0,16},{1,17},{2,18},{3,19},{4,20},{5,21},{6,22},{7,23},{8,24},{9,... | collective-permute-start | bytes 1572872 | tf_op jit(solution)/shard_map/ppermute | solution.py:725
  43.2 14.0 %collective-permute-start.3 = (f32[8,8,128]{2,1,0:T(8,128)S(1)}, f32[8,8,128]{2,1,0:T(8,128)S(1)}, u32[]{:S(2)}, u32[]{:S(2)}) collective-permute-start(f32[8,8,128]{2,1,0:T(8,128)S(1)} %get-tuple-element.66), channel_id=1, source_target_pairs={{0,17},{1,18},{2,19},{3,20},{4,21},{5,22},{6,23},{7,24},{8,25},{9,... | collective-permute-start | bytes 98312 | tf_op jit(solution)/shard_map/ppermute | solution.py:725
  44.9 13.3 %collective-permute-start.4 = (f32[8,8,128]{2,1,0:T(8,128)S(1)}, f32[8,8,128]{2,1,0:T(8,128)S(1)}, u32[]{:S(2)}, u32[]{:S(2)}) collective-permute-start(f32[8,8,128]{2,1,0:T(8,128)S(1)} %get-tuple-element.67), channel_id=1, source_target_pairs={{0,31},{1,16},{2,17},{3,18},{4,19},{5,20},{6,21},{7,22},{8,23},{9,... | collective-permute-start | bytes 98312 | tf_op jit(solution)/shard_map/ppermute | solution.py:725
  45.0 1.0 %copy-start.3 = (s32[1,6,16384]{2,0,1:T(1,128)S(1)}, s32[1,6,16384]{2,0,1:T(1,128)}, u32[]{:S(2)}) copy-start(s32[1,6,16384]{2,0,1:T(1,128)} %param.18) | copy-start | bytes 1179652
  46.0 12.2 %copy-start.4 = (f32[2448,128]{1,0:T(8,128)S(1)}, f32[2448,128]{1,0:T(8,128)}, u32[]{:S(2)}) copy-start(f32[2448,128]{1,0:T(8,128)} %get-tuple-element.46.early) | copy-start | bytes 3760132

commit v6 on v5

--- a/solution.py
+++ b/solution.py
@@ -13,7 +13,7 @@
 LANES = 128
 REACH = RIM // LANES
 WINDOW = 2 * REACH + 1
-EARLY = WINDOW - REACH
+EARLY = WINDOW - 1
 HALO = STEPS * REACH
 PAD = 8
 MIB = 2**20
@@ -565,8 +565,8 @@
     def from_mixed(level, group, row):
         return mixed[pl.ds(level * total + row, GROUP), :]
 
-    def solve(chunk, source, spread_sum, out, wide):
-        for group in range(CHUNK // GROUP):
+    def solve(chunk, source, spread_sum, out, wide, groups=(0, 1)):
+        for group in groups:
             row = pl.multiple_of(chunk * CHUNK + group * GROUP, GROUP)
             here = pl.ds(row, GROUP)
             left = keep[here, :]
@@ -586,15 +586,17 @@
             for level in range(levels - 2, -1, -1):
                 following = partial[level] + from_down[level, here, :] * following
                 out[pl.ds(level * pitch + PAD + row, GROUP), :] = following
-        for row in range(CHUNK):
+        for row in range(CHUNK if wide is not None else 0):
             to_lanes(levels, out, wide, chunk * CHUNK + row)
 
-    def spread(chunk, source, wide):
+    def spread(chunk, source, wide, gathers=True):
         by_matrix, by_gather = group_rows(chunk, chunks)
         for tile in range(GROUP):
             spread_tile(
                 levels, total, wide, matrix, chunk * GROUP + tile, by_matrix + tile, mixed
             )
+        if not gathers:
+            return
         here = pl.ds(by_gather, GROUP)
 
         def terms(which):
@@ -618,12 +620,18 @@
     for copy in late_copies:
         copy.wait()
 
-    @pl.loop(1, STEPS)
+    @pl.loop(1, STEPS - 1)
     def _(step):
         for chunk in range(chunks):
             spread(jnp.int32(chunk), cells, wide)
         for chunk in range(chunks):
             solve(chunk, cells, from_mixed, cells, wide)
+
+    for chunk in range(chunks):
+        spread(jnp.int32(chunk), cells, wide, 0 < chunk < chunks - 1)
+    for chunk in range(chunks):
+        groups = (1,) if chunk == 0 else (0,) if chunk == chunks - 1 else (0, 1)
+        solve(chunk, cells, from_mixed, cells, None, groups)
 
     @pl.loop(0, rows, unroll=8)
     def _(row):

time: 84.4 us -> 81.2 us (0.962)
  the two profiles are of different devices: /device:TPU:9 before, /device:TPU:11 now
where the time goes in v6:
time: 81.2 us; the launch traced here: 80.9 us
  Pallas kernels  56.6 us (70%)
  starting transfers between devices  11.1 us (14%)
  waiting for transfers between devices  10.6 us (13%)
  local copies, waits for them, and re-layouts  1.68 us (2%)
  between operations  0.89 us (1%)
    pallas_call x1, Pallas kernels, interval(): pl.pallas_call(functools.partial(interval_kernel, width), out_shape=[jax....  22.5 us
    pallas_call x1, Pallas kernels, build(): pl.pallas_call(build_kernel, grid=(chunks,), in_specs=[pl.BlockSpec(state...  20 us
    pallas_call x1, Pallas kernels, prepare(): pl.pallas_call(prepare_kernel, out_shape=[pltpu.VMEM((levels * pitch, LAN...  7.62 us
    all_to_all x1, starting transfers between devices, local(): lax.all_to_all(values, 'dom', split_axis=0, concat_axis=0, tiled=True)  6.76 us
    all_to_all x1, waiting for transfers between devices, local(): lax.all_to_all(values, 'dom', split_axis=0, concat_axis=0, tiled=True)  6 us
    pallas_call x1, Pallas kernels, remap(): pl.pallas_call(functools.partial(remap_kernel, owners, capacity), in_spec...  5.92 us
    ppermute x3, waiting for transfers between devices, across(): return lax.ppermute(value, ('comp', 'dom'), pairs)  4.6 us
    ppermute x3, starting transfers between devices, across(): return lax.ppermute(value, ('comp', 'dom'), pairs)  2.95 us
  transfers between devices with their start and end apart: 6, of which 3 were waited for; matrix products, arithmetic and copies ran while one was open for 0% of the time, Pallas kernels for 34%

profile of v6, /device:TPU:11, one launch (start us, length us, event | category | flops | bytes accessed | tf_op | source)
XLA Modules:
  0.0 80.9 jit_solution(13498313006325634818)
XLA Ops:
  0.6 5.9 %remap.1 = (f32[16,136,128]{2,1,0:T(8,128)}, f32[352,128]{1,0:T(8,128)}, f32[352,128]{1,0:T(8,128)}) custom-call(s32[128]{0:T(128)} %bitcast.30, s32[128]{0:T(128)} %bitcast.31, s32[128]{0:T(128)} %bitcast.32, s32[1]{0:T(128)} %bitcast.3.me, f32[8,16384]{1,0:T(8,128)} %bitcast.27, f32[128,128,128]{2,1,0:T(8,128)} %bitcast.26, f32[16,16384]{1,0:T(8,128)} %bitcast.15, ...), custom_call_target="tpu_custom_call" | custom-call | tf_op jit(solution)/shard_map/remap/pallas_call | solution.py:139
  6.6 0.0 copy-start
  6.6 0.0 copy-start.1
  6.6 0.0 copy-start.2
  6.6 6.8 %all-to-all-start = ((f32[16,136,128]{2,1,0:T(8,128)}), f32[16,136,128]{2,1,0:T(8,128)S(1)}, u32[]{:S(2)}, u32[]{:S(2)}) async-start(f32[16,136,128]{2,1,0:T(8,128)} %get-tuple-element.38), calls=%async_computation | async-start | bytes 2228224 | tf_op jit(solution)/shard_map/all_to_all | solution.py:711
  13.4 1.4 %collective-permute-start = (f32[352,128]{1,0:T(8,128)}, f32[352,128]{1,0:T(8,128)S(1)}, u32[]{:S(2)}, u32[]{:S(2)}) collective-permute-start(f32[352,128]{1,0:T(8,128)} %get-tuple-element.45), channel_id=1, source_target_pairs={{0,1},{1,2},{2,3},{3,4},{4,5},{5,6},{6,7},{7,8},{8,9},{9,10},{10,1... | collective-permute-start | bytes 540680 | tf_op jit(solution)/shard_map/ppermute | solution.py:715
  14.8 0.0 collective-permute-start.1
  14.8 20.0 %build.1 = (f32[2448,128]{1,0:T(8,128)}, bf16[72,128,256]{2,1,0:T(8,128)(2,1)}, bf16[72,128,256]{2,1,0:T(8,128)(2,1)}, bf16[72,128,256]{2,1,0:T(8,128)(2,1)}, bf...) custom-call(f32[16,16384]{1,0:T(8,128)} %bitcast.16, f32[6,128,128]{2,1,0:T(8,128)} %bitcast.21, ...), custom_call_target="tpu_custom_call" | custom-call | flops 754974720 | bytes 83886080 | tf_op jit(solution)/shard_map/build/pallas_call | solution.py:369
  34.8 0.0 collective-permute-done.low_far
  34.8 0.0 copy-start.5
  34.9 0.7 copy-done.5
  35.5 0.0 collective-permute-done.1.high_far
  35.5 6.0 %all-to-all-done = f32[16,136,128]{2,1,0:T(8,128)S(1)} async-done(((f32[16,136,128]{2,1,0:T(8,128)}), f32[16,136,128]{2,1,0:T(8,128)S(1)}, u32[]{:S(2)}, u32[]{:S(2)}) %all-to-all-start) | async-done | bytes 1114144 | tf_op jit(solution)/shard_map/all_to_all | solution.py:711
  41.5 0.4 assemble.1
  42.0 0.3 collective-permute-start.2
  42.3 2.6 %collective-permute-start.3 = (f32[8,8,128]{2,1,0:T(8,128)S(1)}, f32[8,8,128]{2,1,0:T(8,128)S(1)}, u32[]{:S(2)}, u32[]{:S(2)}) collective-permute-start(f32[8,8,128]{2,1,0:T(8,128)S(1)} %get-tuple-element.69), channel_id=1, source_target_pairs={{0,17},{1,18},{2,19},{3,20},{4,21},{5,22},{6,23},{7,24},{8,25},{9,... | collective-permute-start | bytes 98312 | tf_op jit(solution)/shard_map/ppermute | solution.py:733
  44.9 0.0 collective-permute-start.4
  44.9 0.0 copy-done
  44.9 0.0 copy-done.1
  44.9 0.0 copy-done.2
  44.9 0.0 copy-start.3
  45.0 1.0 %copy-done.3 = s32[1,6,16384]{2,0,1:T(1,128)S(1)} copy-done((s32[1,6,16384]{2,0,1:T(1,128)S(1)}, s32[1,6,16384]{2,0,1:T(1,128)}, u32[]{:S(2)}) %copy-start.3) | copy-done | bytes 393240
  45.9 0.0 copy-start.4
  45.9 7.6 %prepare.1 = (f32[2560,128]{1,0:T(8,128)S(1)}, f32[528,128]{1,0:T(8,128)S(1)}, f32[16,144,128]{2,1,0:T(8,128)S(1)}, f32[16,144,128]{2,1,0:T(8,128)S(1)}, f32[16,...) custom-call(f32[16,16384]{1,0:T(8,128)S(1)} %bitcast.17, ...), custom_call_target="tpu_custom_call" | custom-call | bytes 16777216 | tf_op jit(solution)/shard_map/prepare/pallas_call | solution.py:502
  53.6 3.7 %collective-permute-done.3.refs_5_ = f32[8,8,128]{2,1,0:T(8,128)S(1)} collective-permute-done((f32[8,8,128]{2,1,0:T(8,128)S(1)}, f32[8,8,128]{2,1,0:T(8,128)S(1)}, u32[]{:S(2)}, u32[]{:S(2)}) %collective-permute-start.3) | collective-permute-done | bytes 32800 | tf_op jit(solution)/shard_map/ppermute | solution.py:733
  57.2 0.9 %collective-permute-done.4.refs_6_ = f32[8,8,128]{2,1,0:T(8,128)S(1)} collective-permute-done((f32[8,8,128]{2,1,0:T(8,128)S(1)}, f32[8,8,128]{2,1,0:T(8,128)S(1)}, u32[]{:S(2)}, u32[]{:S(2)}) %collective-permute-start.4) | collective-permute-done | bytes 32800 | tf_op jit(solution)/shard_map/ppermute | solution.py:733
  58.2 0.0 collective-permute-done.2.refs_4_
  58.2 0.0 copy-done.4
  58.2 22.5 %interval.1 = (f32[16,16384]{1,0:T(8,128)}, f32[8,16384]{1,0:T(8,128)}) custom-call(f32[2448,128]{1,0:T(8,128)S(1)} %copy-done.4, f32[2560,128]{1,0:T(8,128)S(1)} %get-tuple-element.54.column, f32[528,128]{1,0:T(8,128)S(1)} %get-tuple-element.55.edge, f32[16,144,128]{2,1,0:T(8,128)S(1)} %get-tuple-element.56.inv, ...), custom_call_target="tpu_custom_call" | custom-call | tf_op jit(solution)/shard_map/interval/pallas_call | solution.py:650
Async XLA Ops:
  6.6 38.4 %copy-start = (f32[1,16,16384]{2,1,0:T(8,128)S(1)}, f32[1,16,16384]{2,1,0:T(8,128)}, u32[]{:S(2)}) copy-start(f32[1,16,16384]{2,1,0:T(8,128)} %param.10) | copy-start | bytes 3145732
  6.6 38.4 %copy-start.1 = (f32[1,15,16384]{2,0,1:T(1,128)S(1)}, f32[1,15,16384]{2,0,1:T(1,128)}, u32[]{:S(2)}) copy-start(f32[1,15,16384]{2,0,1:T(1,128)} %param.19) | copy-start | bytes 2949124
  6.6 38.3 %copy-start.2 = (f32[1,6,16384]{2,0,1:T(1,128)S(1)}, f32[1,6,16384]{2,0,1:T(1,128)}, u32[]{:S(2)}) copy-start(f32[1,6,16384]{2,0,1:T(1,128)} %param.17) | copy-start | bytes 1179652
  6.6 34.9 %all-to-all-start = ((f32[16,136,128]{2,1,0:T(8,128)}), f32[16,136,128]{2,1,0:T(8,128)S(1)}, u32[]{:S(2)}, u32[]{:S(2)}) async-start(f32[16,136,128]{2,1,0:T(8,128)} %get-tuple-element.38), calls=%async_computation | async-start | bytes 2228224 | tf_op jit(solution)/shard_map/all_to_all | solution.py:711
  13.4 21.5 %collective-permute-start = (f32[352,128]{1,0:T(8,128)}, f32[352,128]{1,0:T(8,128)S(1)}, u32[]{:S(2)}, u32[]{:S(2)}) collective-permute-start(f32[352,128]{1,0:T(8,128)} %get-tuple-element.45), channel_id=1, source_target_pairs={{0,1},{1,2},{2,3},{3,4},{4,5},{5,6},{6,7},{7,8},{8,9},{9,10},{10,1... | collective-permute-start | bytes 540680 | tf_op jit(solution)/shard_map/ppermute | solution.py:715
  14.8 20.7 %collective-permute-start.1 = (f32[352,128]{1,0:T(8,128)}, f32[352,128]{1,0:T(8,128)}, u32[]{:S(2)}, u32[]{:S(2)}) collective-permute-start(f32[352,128]{1,0:T(8,128)} %get-tuple-element.46), channel_id=1, source_target_pairs={{1,0},{2,1},{3,2},{4,3},{5,4},{6,5},{7,6},{8,7},{9,8},{10,9},{11,1... | collective-permute-start | bytes 540680 | tf_op jit(solution)/shard_map/ppermute | solution.py:716
  34.8 0.7 copy-start.5
  42.0 16.2 %collective-permute-start.2 = (f32[8,128,128]{2,1,0:T(8,128)S(1)}, f32[8,128,128]{2,1,0:T(8,128)S(1)}, u32[]{:S(2)}, u32[]{:S(2)}) collective-permute-start(f32[8,128,128]{2,1,0:T(8,128)S(1)} %get-tuple-element.68), channel_id=1, source_target_pairs={{0,16},{1,17},{2,18},{3,19},{4,20},{5,21},{6,22},{7,23},{8,24},{9,... | collective-permute-start | bytes 1572872 | tf_op jit(solution)/shard_map/ppermute | solution.py:733
  42.3 14.9 %collective-permute-start.3 = (f32[8,8,128]{2,1,0:T(8,128)S(1)}, f32[8,8,128]{2,1,0:T(8,128)S(1)}, u32[]{:S(2)}, u32[]{:S(2)}) collective-permute-start(f32[8,8,128]{2,1,0:T(8,128)S(1)} %get-tuple-element.69), channel_id=1, source_target_pairs={{0,17},{1,18},{2,19},{3,20},{4,21},{5,22},{6,23},{7,24},{8,25},{9,... | collective-permute-start | bytes 98312 | tf_op jit(solution)/shard_map/ppermute | solution.py:733
  44.9 13.3 %collective-permute-start.4 = (f32[8,8,128]{2,1,0:T(8,128)S(1)}, f32[8,8,128]{2,1,0:T(8,128)S(1)}, u32[]{:S(2)}, u32[]{:S(2)}) collective-permute-start(f32[8,8,128]{2,1,0:T(8,128)S(1)} %get-tuple-element.70), channel_id=1, source_target_pairs={{0,31},{1,16},{2,17},{3,18},{4,19},{5,20},{6,21},{7,22},{8,23},{9,... | collective-permute-start | bytes 98312 | tf_op jit(solution)/shard_map/ppermute | solution.py:733
  44.9 1.0 %copy-start.3 = (s32[1,6,16384]{2,0,1:T(1,128)S(1)}, s32[1,6,16384]{2,0,1:T(1,128)}, u32[]{:S(2)}) copy-start(s32[1,6,16384]{2,0,1:T(1,128)} %param.18) | copy-start | bytes 1179652
  45.9 12.2 %copy-start.4 = (f32[2448,128]{1,0:T(8,128)S(1)}, f32[2448,128]{1,0:T(8,128)}, u32[]{:S(2)}) copy-start(f32[2448,128]{1,0:T(8,128)} %get-tuple-element.47.early) | copy-start | bytes 3760132

commit v7 on v6

--- a/solution.py
+++ b/solution.py
@@ -401,7 +401,7 @@
 
 
 def prepare_kernel(
-    state, coef, offset, vert, low_far, high_far, *refs
+    state, coef, vert, offset_far, low_far, high_far, *refs
 ):
     far, (column, edge, inv, from_up, from_down, lanes, codes, coefs, keep, *refs) = (
         refs[:EARLY],
@@ -410,7 +410,13 @@
     matrix, (verts, low, high, packed, copied) = refs[:EARLY], refs[EARLY:]
     pack_copies = [
         pltpu.make_async_copy(source, target, packed.at[index])
-        for index, (source, target) in enumerate(((low_far, low), (high_far, high)))
+        for index, (source, target) in enumerate(
+            (
+                (low_far, low),
+                (high_far, high),
+                (offset_far, lanes.at[:, pl.ds(HALO, state.shape[1] // LANES), :]),
+            )
+        )
     ]
     matrix_copies = [
         pltpu.make_async_copy(far[reach], matrix[reach], copied.at[reach])
@@ -427,7 +433,6 @@
 
     main = slice(HALO, HALO + rows)
     coefs[:, main, :] = coef[...]
-    lanes[:, main, :] = offset[...]
     verts[:, main, :] = vert[...]
 
     @pl.loop(0, rows, unroll=8)
@@ -496,8 +501,9 @@
     index_shape = pltpu.VMEM((NB, total, LANES), jnp.int32)
     near = pl.BlockSpec(memory_space=pltpu.VMEM)
     far = pl.BlockSpec(memory_space=pltpu.HBM)
-    low, high, *matrix = [
-        pltpu.with_memory_space_constraint(part, pltpu.HBM) for part in (low, high, *matrix)
+    offset, low, high, *matrix = [
+        pltpu.with_memory_space_constraint(part, pltpu.HBM)
+        for part in (offset, low, high, *matrix)
     ]
     return pl.pallas_call(
         prepare_kernel,
@@ -513,19 +519,19 @@
             pltpu.VMEM((total, LANES), F32),
             *[pltpu.VMEM(part.shape, part.dtype) for part in matrix],
         ],
-        in_specs=[near] * 4 + [far] * (2 + EARLY),
+        in_specs=[near] * 3 + [far] * (3 + EARLY),
         out_specs=[near] * (9 + EARLY),
         scratch_shapes=[
             pltpu.VMEM((levels - 1, total, LANES), F32),
             pltpu.VMEM(low.shape, F32),
             pltpu.VMEM(high.shape, F32),
-            pltpu.SemaphoreType.DMA((2,)),
+            pltpu.SemaphoreType.DMA((3,)),
             pltpu.SemaphoreType.DMA((EARLY,)),
         ],
         compiler_params=pltpu.CompilerParams(vmem_limit_bytes=24 * MIB),
         cost_estimate=pl.CostEstimate(flops=0, bytes_accessed=16 * MIB, transcendentals=0),
         name="prepare",
-    )(state, coef, offset, vert, low, high, *matrix)
+    )(state, coef, vert, offset, low, high, *matrix)
 
 
 def interval_kernel(

time: 81.2 us -> 83.1 us (1.023)
  Pallas kernels: 56.6 us -> 58.6 us
  local copies, waits for them, and re-layouts: 1.68 us -> 0.69 us
  waiting for transfers between devices: 10.6 us -> 11.5 us
    pallas_call x1, Pallas kernels: 22.5 us -> 24.5 us  [interval(): pl.pallas_call(functools.partial(interval_kernel, width), out_shape=[jax....]
    unnamed x12 -> x10, local copies, waits for them, and re-layouts: 1.68 us -> 0.69 us
where the time goes in v7:
time: 83.1 us; the launch traced here: 82.8 us
  Pallas kernels  58.6 us (71%)
  waiting for transfers between devices  11.5 us (14%)
  starting transfers between devices  11.1 us (13%)
  between operations  0.89 us (1%)
    pallas_call x1, Pallas kernels, interval(): pl.pallas_call(functools.partial(interval_kernel, width), out_shape=[jax....  24.5 us
    pallas_call x1, Pallas kernels, build(): pl.pallas_call(build_kernel, grid=(chunks,), in_specs=[pl.BlockSpec(state...  20 us
    pallas_call x1, Pallas kernels, prepare(): pl.pallas_call(prepare_kernel, out_shape=[pltpu.VMEM((levels * pitch, LAN...  7.79 us
    all_to_all x1, starting transfers between devices, local(): lax.all_to_all(values, 'dom', split_axis=0, concat_axis=0, tiled=True)  6.75 us
    all_to_all x1, waiting for transfers between devices, local(): lax.all_to_all(values, 'dom', split_axis=0, concat_axis=0, tiled=True)  6.03 us
    pallas_call x1, Pallas kernels, remap(): pl.pallas_call(functools.partial(remap_kernel, owners, capacity), in_spec...  5.92 us
    ppermute x3, waiting for transfers between devices, across(): return lax.ppermute(value, ('comp', 'dom'), pairs)  5.42 us
    ppermute x3, starting transfers between devices, across(): return lax.ppermute(value, ('comp', 'dom'), pairs)  2.95 us
  transfers between devices with their start and end apart: 6, of which 3 were waited for; matrix products, arithmetic and copies ran while one was open for 0% of the time, Pallas kernels for 34%

profile of v7, /device:TPU:11, one launch (start us, length us, event | category | flops | bytes accessed | tf_op | source)
XLA Modules:
  0.0 82.8 jit_solution(17602643832352193214)
XLA Ops:
  0.6 5.9 %remap.1 = (f32[16,136,128]{2,1,0:T(8,128)}, f32[352,128]{1,0:T(8,128)}, f32[352,128]{1,0:T(8,128)}) custom-call(s32[128]{0:T(128)} %bitcast.30, s32[128]{0:T(128)} %bitcast.31, s32[128]{0:T(128)} %bitcast.32, s32[1]{0:T(128)} %bitcast.3.me, f32[8,16384]{1,0:T(8,128)} %bitcast.27, f32[128,128,128]{2,1,0:T(8,128)} %bitcast.23, f32[16,16384]{1,0:T(8,128)} %bitcast.15, ...), custom_call_target="tpu_custom_call" | custom-call | tf_op jit(solution)/shard_map/remap/pallas_call | solution.py:139
  6.6 0.0 copy-start
  6.6 0.0 copy-start.1
  6.6 0.0 copy-start.2
  6.6 6.8 %all-to-all-start = ((f32[16,136,128]{2,1,0:T(8,128)}), f32[16,136,128]{2,1,0:T(8,128)S(1)}, u32[]{:S(2)}, u32[]{:S(2)}) async-start(f32[16,136,128]{2,1,0:T(8,128)} %get-tuple-element.38), calls=%async_computation | async-start | bytes 2228224 | tf_op jit(solution)/shard_map/all_to_all | solution.py:717
  13.4 1.4 %collective-permute-start = (f32[352,128]{1,0:T(8,128)}, f32[352,128]{1,0:T(8,128)S(1)}, u32[]{:S(2)}, u32[]{:S(2)}) collective-permute-start(f32[352,128]{1,0:T(8,128)} %get-tuple-element.45), channel_id=1, source_target_pairs={{0,1},{1,2},{2,3},{3,4},{4,5},{5,6},{6,7},{7,8},{8,9},{9,10},{10,1... | collective-permute-start | bytes 540680 | tf_op jit(solution)/shard_map/ppermute | solution.py:721
  14.8 0.0 collective-permute-start.1
  14.8 20.0 %build.1 = (f32[2448,128]{1,0:T(8,128)}, bf16[72,128,256]{2,1,0:T(8,128)(2,1)}, bf16[72,128,256]{2,1,0:T(8,128)(2,1)}, bf16[72,128,256]{2,1,0:T(8,128)(2,1)}, bf...) custom-call(f32[16,16384]{1,0:T(8,128)} %bitcast.16, f32[6,128,128]{2,1,0:T(8,128)} %bitcast.21, ...), custom_call_target="tpu_custom_call" | custom-call | flops 754974720 | bytes 83886080 | tf_op jit(solution)/shard_map/build/pallas_call | solution.py:369
  34.8 0.0 collective-permute-done.low_far
  34.8 0.0 copy-start.4
  34.8 0.7 copy-done.4
  35.5 0.0 collective-permute-done.1.high_far
  35.5 6.0 %all-to-all-done = f32[16,136,128]{2,1,0:T(8,128)S(1)} async-done(((f32[16,136,128]{2,1,0:T(8,128)}), f32[16,136,128]{2,1,0:T(8,128)S(1)}, u32[]{:S(2)}, u32[]{:S(2)}) %all-to-all-start) | async-done | bytes 1114144 | tf_op jit(solution)/shard_map/all_to_all | solution.py:717
  41.5 0.4 assemble.1
  42.0 0.3 collective-permute-start.2
  42.3 2.6 %collective-permute-start.3 = (f32[8,8,128]{2,1,0:T(8,128)S(1)}, f32[8,8,128]{2,1,0:T(8,128)S(1)}, u32[]{:S(2)}, u32[]{:S(2)}) collective-permute-start(f32[8,8,128]{2,1,0:T(8,128)S(1)} %get-tuple-element.69), channel_id=1, source_target_pairs={{0,17},{1,18},{2,19},{3,20},{4,21},{5,22},{6,23},{7,24},{8,25},{9,... | collective-permute-start | bytes 98312 | tf_op jit(solution)/shard_map/ppermute | solution.py:739
  44.9 0.0 copy-start.3
  44.9 0.0 collective-permute-start.4
  44.9 0.0 copy-done
  44.9 0.0 copy-done.1
  44.9 0.0 copy-done.2
  44.9 7.8 %prepare.1 = (f32[2560,128]{1,0:T(8,128)S(1)}, f32[528,128]{1,0:T(8,128)S(1)}, f32[16,144,128]{2,1,0:T(8,128)S(1)}, f32[16,144,128]{2,1,0:T(8,128)S(1)}, f32[16,...) custom-call(f32[16,16384]{1,0:T(8,128)S(1)} %bitcast.17, ...), custom_call_target="tpu_custom_call" | custom-call | bytes 16777216 | tf_op jit(solution)/shard_map/prepare/pallas_call | solution.py:508
  52.8 4.5 %collective-permute-done.3.refs_5_ = f32[8,8,128]{2,1,0:T(8,128)S(1)} collective-permute-done((f32[8,8,128]{2,1,0:T(8,128)S(1)}, f32[8,8,128]{2,1,0:T(8,128)S(1)}, u32[]{:S(2)}, u32[]{:S(2)}) %collective-permute-start.3) | collective-permute-done | bytes 32800 | tf_op jit(solution)/shard_map/ppermute | solution.py:739
  57.2 0.9 %collective-permute-done.4.refs_6_ = f32[8,8,128]{2,1,0:T(8,128)S(1)} collective-permute-done((f32[8,8,128]{2,1,0:T(8,128)S(1)}, f32[8,8,128]{2,1,0:T(8,128)S(1)}, u32[]{:S(2)}, u32[]{:S(2)}) %collective-permute-start.4) | collective-permute-done | bytes 32800 | tf_op jit(solution)/shard_map/ppermute | solution.py:739
  58.2 0.0 collective-permute-done.2.refs_4_
  58.2 0.0 copy-done.3
  58.2 24.5 %interval.1 = (f32[16,16384]{1,0:T(8,128)}, f32[8,16384]{1,0:T(8,128)}) custom-call(f32[2448,128]{1,0:T(8,128)S(1)} %copy-done.3, f32[2560,128]{1,0:T(8,128)S(1)} %get-tuple-element.54.column, f32[528,128]{1,0:T(8,128)S(1)} %get-tuple-element.55.edge, f32[16,144,128]{2,1,0:T(8,128)S(1)} %get-tuple-element.56.inv, ...), custom_call_target="tpu_custom_call" | custom-call | tf_op jit(solution)/shard_map/interval/pallas_call | solution.py:656
Async XLA Ops:
  6.6 38.4 %copy-start = (f32[1,16,16384]{2,1,0:T(8,128)S(1)}, f32[1,16,16384]{2,1,0:T(8,128)}, u32[]{:S(2)}) copy-start(f32[1,16,16384]{2,1,0:T(8,128)} %param.10) | copy-start | bytes 3145732
  6.6 38.4 %copy-start.1 = (f32[1,15,16384]{2,0,1:T(1,128)S(1)}, f32[1,15,16384]{2,0,1:T(1,128)}, u32[]{:S(2)}) copy-start(f32[1,15,16384]{2,0,1:T(1,128)} %param.19) | copy-start | bytes 2949124
  6.6 38.3 %copy-start.2 = (f32[1,6,16384]{2,0,1:T(1,128)S(1)}, f32[1,6,16384]{2,0,1:T(1,128)}, u32[]{:S(2)}) copy-start(f32[1,6,16384]{2,0,1:T(1,128)} %param.17) | copy-start | bytes 1179652
  6.6 34.9 %all-to-all-start = ((f32[16,136,128]{2,1,0:T(8,128)}), f32[16,136,128]{2,1,0:T(8,128)S(1)}, u32[]{:S(2)}, u32[]{:S(2)}) async-start(f32[16,136,128]{2,1,0:T(8,128)} %get-tuple-element.38), calls=%async_computation | async-start | bytes 2228224 | tf_op jit(solution)/shard_map/all_to_all | solution.py:717
  13.4 21.4 %collective-permute-start = (f32[352,128]{1,0:T(8,128)}, f32[352,128]{1,0:T(8,128)S(1)}, u32[]{:S(2)}, u32[]{:S(2)}) collective-permute-start(f32[352,128]{1,0:T(8,128)} %get-tuple-element.45), channel_id=1, source_target_pairs={{0,1},{1,2},{2,3},{3,4},{4,5},{5,6},{6,7},{7,8},{8,9},{9,10},{10,1... | collective-permute-start | bytes 540680 | tf_op jit(solution)/shard_map/ppermute | solution.py:721
  14.8 20.7 %collective-permute-start.1 = (f32[352,128]{1,0:T(8,128)}, f32[352,128]{1,0:T(8,128)}, u32[]{:S(2)}, u32[]{:S(2)}) collective-permute-start(f32[352,128]{1,0:T(8,128)} %get-tuple-element.46), channel_id=1, source_target_pairs={{1,0},{2,1},{3,2},{4,3},{5,4},{6,5},{7,6},{8,7},{9,8},{10,9},{11,1... | collective-permute-start | bytes 540680 | tf_op jit(solution)/shard_map/ppermute | solution.py:722
  34.8 0.7 copy-start.4
  42.0 16.2 %collective-permute-start.2 = (f32[8,128,128]{2,1,0:T(8,128)S(1)}, f32[8,128,128]{2,1,0:T(8,128)S(1)}, u32[]{:S(2)}, u32[]{:S(2)}) collective-permute-start(f32[8,128,128]{2,1,0:T(8,128)S(1)} %get-tuple-element.68), channel_id=1, source_target_pairs={{0,16},{1,17},{2,18},{3,19},{4,20},{5,21},{6,22},{7,23},{8,24},{9,... | collective-permute-start | bytes 1572872 | tf_op jit(solution)/shard_map/ppermute | solution.py:739
  42.3 14.9 %collective-permute-start.3 = (f32[8,8,128]{2,1,0:T(8,128)S(1)}, f32[8,8,128]{2,1,0:T(8,128)S(1)}, u32[]{:S(2)}, u32[]{:S(2)}) collective-permute-start(f32[8,8,128]{2,1,0:T(8,128)S(1)} %get-tuple-element.69), channel_id=1, source_target_pairs={{0,17},{1,18},{2,19},{3,20},{4,21},{5,22},{6,23},{7,24},{8,25},{9,... | collective-permute-start | bytes 98312 | tf_op jit(solution)/shard_map/ppermute | solution.py:739
  44.9 13.3 %copy-start.3 = (f32[2448,128]{1,0:T(8,128)S(1)}, f32[2448,128]{1,0:T(8,128)}, u32[]{:S(2)}) copy-start(f32[2448,128]{1,0:T(8,128)} %get-tuple-element.47.early) | copy-start | bytes 3760132
  44.9 13.3 %collective-permute-start.4 = (f32[8,8,128]{2,1,0:T(8,128)S(1)}, f32[8,8,128]{2,1,0:T(8,128)S(1)}, u32[]{:S(2)}, u32[]{:S(2)}) collective-permute-start(f32[8,8,128]{2,1,0:T(8,128)S(1)} %get-tuple-element.70), channel_id=1, source_target_pairs={{0,31},{1,16},{2,17},{3,18},{4,19},{5,20},{6,21},{7,22},{8,23},{9,... | collective-permute-start | bytes 98312 | tf_op jit(solution)/shard_map/ppermute | solution.py:739
